TPU v7x, 512 devices: a whole 4x8x8 slice. The times are simulated.
512 devices in a mesh: dp: 64 (over z, y_hi, core), replica: 8 (over x, y_lo).
Axes of the slice: x: 4, y: 8 (y_hi: 4, y_lo: 2; y = y_hi * 2 + y_lo), z: 8, core: 2. Of those that a mesh axis runs over, the one named last changes fastest.
Arguments:
- images: bfloat16 [131072, 1152], P(('dp', 'replica')), may hold values from -0.1875 to 0.1875
- texts: bfloat16 [131072, 1152], P(('dp', 'replica')), may hold values from -0.1875 to 0.1875
- head: bfloat16 [1152, 1152], P('replica'), may hold values from -0.1875 to 0.1875
- scale: float32 [1], replicated, may hold values from 10 to 30
- bias: float32 [1], replicated, may hold values from -6 to -2
- offsets: int32 [512], P(('dp', 'replica')), may hold values from 0 to 255
Outputs:
- image_grad: bfloat16 [131072, 1152], P(('dp', 'replica'))
- text_grad: bfloat16 [131072, 1152], P(('dp', 'replica'))
- head_grad: float32 [1152, 1152], P('replica')
All inputs are finite; a program needn't handle non-finite values.
Results may differ from a plain program's by a relative error of at most 0.017.
Values may be sent and summed in bfloat16 or wider, within the bound.
No kernel may reach another device: no remote copies, remote signals or barrier semaphores. Data moves between devices by JAX's collectives and lax.ppermute only.
A program may use at most 64 MiB of HBM per device.

v0:
```python
import jax
import jax.numpy as jnp
from jax import lax
from jax.sharding import PartitionSpec as P

STEPS = 4


EPS = 1e-06


def passed_along(array, axis, by):
    size = lax.axis_size(axis)
    return lax.ppermute(array, axis, [(i, (i + by) % size) for i in range(size)])


def unit_rows(values):
    inverse = lax.rsqrt(jnp.sum(values * values, axis=-1, keepdims=True) + EPS)
    return (values * inverse, inverse)


def pair_weights(img_b, other, step, offset_value, scale_value, bias_value):
    logits = (
        scale_value
        * lax.dot_general(
            img_b, other, (((1,), (1,)), ((), ())), preferred_element_type=jnp.float32
        )
        + bias_value
    )
    count = img_b.shape[0]
    target = (jnp.arange(count, dtype=jnp.int32) + offset_value) % count
    positive = jnp.logical_and(
        jnp.arange(count, dtype=jnp.int32)[None, :] == target[:, None], step == 0
    )
    sign = jnp.where(positive, jnp.float32(1.0), jnp.float32(-1.0))
    coef = -sign * jax.nn.sigmoid(-sign * logits)
    return (scale_value * coef).astype(jnp.bfloat16)


def text_part(weights, img_b):
    return lax.dot_general(
        weights, img_b, (((0,), (0,)), ((), ())), preferred_element_type=jnp.float32
    ).astype(jnp.bfloat16)


def widen(part):
    return lax.optimization_barrier(part).astype(jnp.float32)


def per_device(images, texts, head, scale, bias, offsets):
    rows = images.shape[0]
    width = images.shape[1]
    scale_value = scale[0]
    bias_value = bias[0]
    offset_value = offsets[0]
    full_head = lax.all_gather(head, "replica", axis=0, tiled=True)
    proj = jnp.dot(images, full_head, preferred_element_type=jnp.float32)
    img_unit, inv_img = unit_rows(proj)
    img_b = img_unit.astype(jnp.bfloat16)
    txt_unit, inv_txt = unit_rows(texts.astype(jnp.float32))
    txt_b = txt_unit.astype(jnp.bfloat16)
    img_dir = jnp.zeros((rows, width), jnp.float32)
    current = txt_b
    txt_dir = jnp.zeros((rows, width), jnp.float32)
    for step in range(STEPS):
        if step > 0:
            current = passed_along(current, "dp", 1)
        weights = pair_weights(img_b, current, step, offset_value, scale_value, bias_value)
        img_dir = img_dir + jnp.dot(weights, current, preferred_element_type=jnp.float32)
        part = text_part(weights, img_b)
        if step == 0:
            txt_dir = widen(part)
        else:
            txt_dir = txt_dir + passed_along(part, "dp", -step).astype(jnp.float32)
    text_grad = (
        (txt_dir - txt_unit * jnp.sum(txt_unit * txt_dir, axis=-1, keepdims=True)) * inv_txt
    ).astype(jnp.bfloat16)
    proj_grad = (
        (img_dir - img_unit * jnp.sum(img_unit * img_dir, axis=-1, keepdims=True)) * inv_img
    ).astype(jnp.bfloat16)
    image_grad = lax.dot_general(
        proj_grad, full_head, (((1,), (1,)), ((), ())), preferred_element_type=jnp.float32
    ).astype(jnp.bfloat16)
    share = lax.psum_scatter(
        lax.dot_general(
            images, proj_grad, (((0,), (0,)), ((), ())), preferred_element_type=jnp.float32
        ).astype(jnp.bfloat16),
        "replica",
        scatter_dimension=0,
        tiled=True,
    ).astype(jnp.float32)
    head_grad = lax.psum(share, "dp")
    return (image_grad, text_grad, head_grad)


def solution(mesh):
    in_specs = (
        P(("dp", "replica"), None),
        P(("dp", "replica"), None),
        P("replica", None),
        P(),
        P(),
        P(("dp", "replica")),
    )
    out_specs = (P(("dp", "replica"), None), P(("dp", "replica"), None), P("replica", None))
    return jax.shard_map(
        per_device, mesh=mesh, in_specs=in_specs, out_specs=out_specs, check_vma=False
    )
```

profile of v0, /device:TPU:1, one launch (start us, length us, event | category | flops | bytes accessed | tf_op | source)
XLA Modules:
  0.0 542.1 jit_solution(4276247690705258242)
XLA Ops:
  7.2 0.7 all-gather.2.cloned.1.call-update
  8.0 1.3 fusion.8
  9.4 5.6 %collective-permute-start = (bf16[256,1152]{1,0:T(8,128)(2,1)S(1)}, bf16[256,1152]{1,0:T(8,128)(2,1)S(1)}, u32[]{:S(2)}, u32[]{:S(2)}) collective-permute-start(bf16[256,1152]{1,0:T(8,128)(2,1)S(1)} %fusion.3), channel_id=1, source_target_pairs={{0,8},{8,16},{16,24},{24,32},{32,40},{40,48},{48,56},{56,64},{64,7... | collective-permute-start | bytes 1769480 | tf_op jit(solution)/shard_map/ppermute | solution.py:14
  15.1 8.6 %collective-permute-done = bf16[256,1152]{1,0:T(8,128)(2,1)S(1)} collective-permute-done((bf16[256,1152]{1,0:T(8,128)(2,1)S(1)}, bf16[256,1152]{1,0:T(8,128)(2,1)S(1)}, u32[]{:S(2)}, u32[]{:S(2)}) %collective-permute-start) | collective-permute-done | bytes 589856 | tf_op jit(solution)/shard_map/ppermute | solution.py:14
  23.6 5.3 collective-permute-start.1
  30.9 31.3 %collective-permute-done.1 = bf16[256,1152]{1,0:T(8,128)(2,1)S(1)} collective-permute-done((bf16[256,1152]{1,0:T(8,128)(2,1)S(1)}, bf16[256,1152]{1,0:T(8,128)(2,1)S(1)}, u32[]{:S(2)}, u32[]{:S(2)}) %collective-permute-start.1) | collective-permute-done | bytes 589856 | tf_op jit(solution)/shard_map/ppermute | solution.py:14
  62.3 5.6 %collective-permute-start.2 = (bf16[256,1152]{1,0:T(8,128)(2,1)S(1)}, bf16[256,1152]{1,0:T(8,128)(2,1)S(1)}, u32[]{:S(2)}, u32[]{:S(2)}) collective-permute-start(bf16[256,1152]{1,0:T(8,128)(2,1)S(1)} %collective-permute-done.1), channel_id=1, source_target_pairs={{0,8},{8,16},{16,24},{24,32},{32,40},{40,48},{48,56},{56,64},{64,7... | collective-permute-start | bytes 1769480 | tf_op jit(solution)/shard_map/ppermute | solution.py:14
  67.9 38.3 %all-gather.2.cloned.1.call-done = bf16[1152,1152]{1,0:T(8,128)(2,1)} async-done(((bf16[144,1152]{1,0:T(8,128)(2,1)}), bf16[1152,1152]{1,0:T(8,128)(2,1)}) %all-gather.2.cloned.1.call-update) | async-done | bytes 2654224 | tf_op jit(solution)/shard_map/all_gather | solution.py:56
  106.1 2.8 multiply_reduce_fusion.1
  109.1 0.4 fusion.35
  109.9 0.4 fusion.36
  110.4 0.4 fusion.37
  111.5 0.4 fusion.38
  111.9 0.4 multiply_reduce_fusion
  112.8 0.8 copy-done.5
  113.6 1.0 fusion
  114.6 3.2 copy.11
  117.9 1.0 copy-done.2
  119.7 0.4 convolution_convert_fusion.4
  120.1 10.6 %collective-permute-start.5 = (bf16[256,1152]{1,0:T(8,128)(2,1)S(1)}, bf16[256,1152]{1,0:T(8,128)(2,1)S(1)}, u32[]{:S(2)}, u32[]{:S(2)}) collective-permute-start(bf16[256,1152]{1,0:T(8,128)(2,1)S(1)} %convolution_convert_fusion.2), channel_id=1, source_target_pairs={{0,488},{8,496},{16,504},{24,0},{32,8},{40,16},{48,24},{56,32},{64... | collective-permute-start | bytes 1769480 | tf_op jit(solution)/shard_map/ppermute | solution.py:14
  130.7 4.1 collective-permute-start.4
  134.8 3.4 collective-permute-start.3
  138.2 0.4 convolution_convert_fusion.5
  138.6 1.9 convolution_convert_fusion.1
  140.4 2.0 collective-permute-done.5
  142.4 17.4 %collective-permute-done.4 = bf16[256,1152]{1,0:T(8,128)(2,1)S(1)} collective-permute-done((bf16[256,1152]{1,0:T(8,128)(2,1)S(1)}, bf16[256,1152]{1,0:T(8,128)(2,1)S(1)}, u32[]{:S(2)}, u32[]{:S(2)}) %collective-permute-start.4) | collective-permute-done | bytes 589856 | tf_op jit(solution)/shard_map/ppermute | solution.py:14
  159.8 0.5 fusion.4
  160.3 1.3 fusion.7
  161.6 83.4 %reduce-scatter.4.cloned.1.call-done = bf16[144,1152]{1,0:T(8,128)(2,1)} async-done(((bf16[1152,1152]{1,0:T(8,128)(2,1)}), bf16[144,1152]{1,0:T(8,128)(2,1)}) %reduce-scatter.4.cloned.1.call-update) | async-done | bytes 331792
  245.0 1.2 copy.12
  246.2 287.8 %all-reduce.1 = f32[144,1152]{0,1:T(8,128)S(1)} all-reduce(bf16[144,1152]{0,1:T(8,128)(2,1)S(1)} %copy.12), channel_id=1, replica_groups=mesh['dp'=64,'replica'=8] {'dp'}, use_global_device_ids=true, to_apply=%region_5.6 | all-reduce | flops 165888 | bytes 995328 | tf_op jit(solution)/shard_map/psum | solution.py:92
  534.0 1.2 copy.10
  (38 shorter events, 2.7 us)
Async XLA Ops:
  7.2 99.0 %copy-start = (bf16[256,1152]{1,0:T(8,128)(2,1)S(1)}, bf16[256,1152]{1,0:T(8,128)(2,1)}, u32[]{:S(2)}) copy-start(bf16[256,1152]{1,0:T(8,128)(2,1)} %param.6) | copy-start | bytes 1769476
  7.2 2.1 copy-start.3
  7.2 99.0 %all-gather.2.cloned.1.call-start = ((), (), s32[]{:S(2)}) async-start(), calls=%async_computation.1 | async-start | bytes 2985984 | tf_op jit(solution)/shard_map/all_gather | solution.py:56
  7.9 237.1 %reduce-scatter.4.cloned.1.call-start = ((), (), s32[]{:S(2)}) async-start(), calls=%async_computation.2 | async-start | bytes 2985984
  9.4 14.2 %collective-permute-start = (bf16[256,1152]{1,0:T(8,128)(2,1)S(1)}, bf16[256,1152]{1,0:T(8,128)(2,1)S(1)}, u32[]{:S(2)}, u32[]{:S(2)}) collective-permute-start(bf16[256,1152]{1,0:T(8,128)(2,1)S(1)} %fusion.3), channel_id=1, source_target_pairs={{0,8},{8,16},{16,24},{24,32},{32,40},{40,48},{48,56},{56,64},{64,7... | collective-permute-start | bytes 1769480 | tf_op jit(solution)/shard_map/ppermute | solution.py:14
  23.6 38.6 %collective-permute-start.1 = (bf16[256,1152]{1,0:T(8,128)(2,1)S(1)}, bf16[256,1152]{1,0:T(8,128)(2,1)S(1)}, u32[]{:S(2)}, u32[]{:S(2)}) collective-permute-start(bf16[256,1152]{1,0:T(8,128)(2,1)S(1)} %collective-permute-done), channel_id=1, source_target_pairs={{0,8},{8,16},{16,24},{24,32},{32,40},{40,48},{48,56},{56,64},{64,7... | collective-permute-start | bytes 1769480 | tf_op jit(solution)/shard_map/ppermute | solution.py:14
  62.3 49.2 %collective-permute-start.2 = (bf16[256,1152]{1,0:T(8,128)(2,1)S(1)}, bf16[256,1152]{1,0:T(8,128)(2,1)S(1)}, u32[]{:S(2)}, u32[]{:S(2)}) collective-permute-start(bf16[256,1152]{1,0:T(8,128)(2,1)S(1)} %collective-permute-done.1), channel_id=1, source_target_pairs={{0,8},{8,16},{16,24},{24,32},{32,40},{40,48},{48,56},{56,64},{64,7... | collective-permute-start | bytes 1769480 | tf_op jit(solution)/shard_map/ppermute | solution.py:14
  109.1 2.3 copy-start.1
  109.6 0.8 copy-start.7
  111.9 0.7 copy-start.9
  112.8 0.8 copy-start.5
  117.9 1.1 copy-start.2
  117.9 1.1 copy-start.10
  119.3 18.9 %copy-start.8 = (bf16[256,256]{1,0:T(8,128)(2,1)S(1)}, bf16[256,256]{1,0:T(8,128)(2,1)}, u32[]{:S(2)}) copy-start(bf16[256,256]{1,0:T(8,128)(2,1)} %copy-done.7) | copy-start | bytes 393220
  119.3 19.2 %copy-start.11 = (bf16[1152,1152]{1,0:T(8,128)(2,1)S(1)}, bf16[1152,1152]{1,0:T(8,128)(2,1)}, u32[]{:S(2)}) copy-start(bf16[1152,1152]{1,0:T(8,128)(2,1)} %all-gather.2.cloned.1.call-done) | copy-start | bytes 7962628
  119.7 18.9 %copy-start.6 = (bf16[256,1152]{1,0:T(8,128)(2,1)S(1)}, bf16[256,1152]{1,0:T(8,128)(2,1)}, u32[]{:S(2)}) copy-start(bf16[256,1152]{1,0:T(8,128)(2,1)} %copy-done.5) | copy-start | bytes 1769476
  120.1 22.3 %collective-permute-start.5 = (bf16[256,1152]{1,0:T(8,128)(2,1)S(1)}, bf16[256,1152]{1,0:T(8,128)(2,1)S(1)}, u32[]{:S(2)}, u32[]{:S(2)}) collective-permute-start(bf16[256,1152]{1,0:T(8,128)(2,1)S(1)} %convolution_convert_fusion.2), channel_id=1, source_target_pairs={{0,488},{8,496},{16,504},{24,0},{32,8},{40,16},{48,24},{56,32},{64... | collective-permute-start | bytes 1769480 | tf_op jit(solution)/shard_map/ppermute | solution.py:14
  130.7 29.1 %collective-permute-start.4 = (bf16[256,1152]{1,0:T(8,128)(2,1)S(1)}, bf16[256,1152]{1,0:T(8,128)(2,1)S(1)}, u32[]{:S(2)}, u32[]{:S(2)}) collective-permute-start(bf16[256,1152]{1,0:T(8,128)(2,1)S(1)} %convolution_convert_fusion.3), channel_id=1, source_target_pairs={{0,496},{8,504},{16,0},{24,8},{32,16},{40,24},{48,32},{56,40},{64,... | collective-permute-start | bytes 1769480 | tf_op jit(solution)/shard_map/ppermute | solution.py:14
  134.8 25.0 %collective-permute-start.3 = (bf16[256,1152]{1,0:T(8,128)(2,1)S(1)}, bf16[256,1152]{1,0:T(8,128)(2,1)S(1)}, u32[]{:S(2)}, u32[]{:S(2)}) collective-permute-start(bf16[256,1152]{1,0:T(8,128)(2,1)S(1)} %convolution_convert_fusion.4), channel_id=1, source_target_pairs={{0,504},{8,0},{16,8},{24,16},{32,24},{40,32},{48,40},{56,48},{64,5... | collective-permute-start | bytes 1769480 | tf_op jit(solution)/shard_map/ppermute | solution.py:14
  138.6 21.2 %copy-start.4 = (bf16[256,1152]{1,0:T(8,128)(2,1)S(1)}, bf16[256,1152]{1,0:T(8,128)(2,1)}, u32[]{:S(2)}) copy-start(bf16[256,1152]{1,0:T(8,128)(2,1)} %param.7) | copy-start | bytes 1769476
Sparse Core Ops, SparseCore 0:
  10.1 95.9 all-gather.1
  118.0 126.9 reduce-scatter.3
where the time goes:
time: 546 us; the launch traced here: 542 us
  blocking collectives  288 us (53%)
  waiting for transfers between devices  182 us (33%)
  starting transfers between devices  34.7 us (6%)
  between operations  16.3 us (3%)
  matrix products  10.2 us (2%)
  local copies, waits for them, and re-layouts  7.75 us (1%)
    psum x1, blocking collectives, per_device(): head_grad = lax.psum(share, 'dp')  288 us
    unnamed x3, waiting for transfers between devices  84.1 us
    ppermute x6, waiting for transfers between devices, passed_along(): lax.ppermute(array, axis, [(i, (i + by) % size) for i in range(size)])  59.3 us
    all_gather x1, waiting for transfers between devices, per_device(): full_head = lax.all_gather(head, 'replica', axis=0, tiled=True)  38.3 us
    ppermute x6, starting transfers between devices, passed_along(): lax.ppermute(array, axis, [(i, (i + by) % size) for i in range(size)])  34.6 us
  transfers between devices with their start and end apart: 8, of which 6 were waited for; matrix products, arithmetic and copies ran while one was open for 2% of the time, Pallas kernels for 0%

commit v1 on v0

v1 whole, which is shorter than its diff:
```python
import jax
import jax.numpy as jnp
from jax import lax
from jax.sharding import Mesh
from jax.sharding import PartitionSpec as P

EPS = 1e-06
DP = ("z", "yh", "core")
RING = ("z", "yh")
REP = ("x", "yl")
ALL = DP + REP


def dot(a, b, ca, cb):
    return lax.dot_general(a, b, (((ca,), (cb,)), ((), ())), preferred_element_type=jnp.float32)


def by_chip(shift):
    return [(p, (p + 2 * shift) % 64) for p in range(64)]


SWAP = [(0, 1), (1, 0)]
REST = [(p, p + 1) if p % 2 == 0 else (p, (p + 3) % 64) for p in range(64)]
REST_BACK = [(b, a) for a, b in REST]


def exchange(array, axes):
    return lax.all_to_all(array, axes, split_axis=0, concat_axis=0, tiled=True)


def spread(array, axes, count):
    return exchange(jnp.broadcast_to(array[None], (count,) + array.shape), axes)


def unit_rows(values):
    inverse = lax.rsqrt(jnp.sum(values * values, axis=-1, keepdims=True) + EPS)
    return values * inverse, inverse


def weights_of(img_b, other, scale, bias, target=None):
    logits = scale * dot(img_b, other, 1, 1) + bias
    if target is None:
        return (scale * jax.nn.sigmoid(logits)).astype(jnp.bfloat16)
    count = img_b.shape[0]
    positive = jnp.arange(count, dtype=jnp.int32)[None, :] == target[:, None]
    sign = jnp.where(positive, jnp.float32(1.0), jnp.float32(-1.0))
    return (scale * (-sign * jax.nn.sigmoid(-sign * logits))).astype(jnp.bfloat16)


def per_device(images, texts, head, scale, bias, offsets):
    rows, width = images.shape
    share = head.shape[0]
    half = share // 2
    scale, bias, offset = scale[0], bias[0], offsets[0]
    core = lax.axis_index("core")

    text_a = lax.ppermute(texts, DP, by_chip(1))
    text_c = lax.ppermute(texts, DP, REST)
    text_b = lax.ppermute(text_a, "core", SWAP)

    own_half = lax.dynamic_slice_in_dim(head, core * half, half, 0)
    halves = spread(own_half, REP, 8)
    other = lax.ppermute(halves, "core", SWAP)
    full_head = jnp.where(
        core == 0, jnp.stack([halves, other], 1), jnp.stack([other, halves], 1)
    ).reshape(width, width)

    proj = dot(images, full_head, 1, 0)
    img_unit, inv_img = unit_rows(proj)
    img_b = img_unit.astype(jnp.bfloat16)
    txt_unit, inv_txt = unit_rows(texts.astype(jnp.float32))
    txt_b = txt_unit.astype(jnp.bfloat16)
    target = (jnp.arange(rows, dtype=jnp.int32) + offset) % rows

    img_dir = jnp.zeros((rows, width), jnp.float32)
    parts = []
    for index, block in enumerate((texts, text_a, text_b, text_c)):
        block_b = txt_b if index == 0 else unit_rows(block.astype(jnp.float32))[0].astype(jnp.bfloat16)
        weights = weights_of(img_b, block_b, scale, bias, target if index == 0 else None)
        img_dir = img_dir + dot(weights, block_b, 1, 0)
        parts.append(dot(weights, img_b, 0, 0))

    proj_grad = (
        (img_dir - img_unit * jnp.sum(img_unit * img_dir, axis=-1, keepdims=True)) * inv_img
    ).astype(jnp.bfloat16)

    from_b = lax.ppermute(parts[2].astype(jnp.bfloat16), "core", SWAP)
    back_c = lax.ppermute(parts[3].astype(jnp.bfloat16), DP, REST_BACK)
    pair = (parts[1] + from_b.astype(jnp.float32)).astype(jnp.bfloat16)
    back_a = lax.ppermute(pair, DP, by_chip(-1))

    term = dot(images, proj_grad, 0, 0).astype(jnp.bfloat16)
    term = term.reshape(8, 2, half, width).transpose(1, 0, 2, 3)
    term = exchange(term, "core")
    term = jnp.sum(term.astype(jnp.float32), axis=0).astype(jnp.bfloat16)
    term = exchange(term, REP)
    term = jnp.sum(term.astype(jnp.float32), axis=0).astype(jnp.bfloat16)
    padded = jnp.pad(term, ((0, 96 - half), (0, 0))).reshape(32, 3, width)
    padded = exchange(padded, RING)
    mine = jnp.sum(padded.astype(jnp.float32), axis=0).astype(jnp.bfloat16)
    done = spread(mine, RING, 32).reshape(96, width)[:half]
    head_grad = spread(done, "core", 2).reshape(share, width).astype(jnp.float32)

    image_grad = dot(proj_grad, full_head, 1, 1).astype(jnp.bfloat16)
    txt_dir = parts[0] + back_a.astype(jnp.float32) + back_c.astype(jnp.float32)
    text_grad = (
        (txt_dir - txt_unit * jnp.sum(txt_unit * txt_dir, axis=-1, keepdims=True)) * inv_txt
    ).astype(jnp.bfloat16)
    return image_grad, text_grad, head_grad


def solution(mesh):
    fine = Mesh(mesh.devices.reshape(8, 4, 2, 4, 2), ALL)
    in_specs = (P(ALL, None), P(ALL, None), P(REP, None), P(), P(), P(ALL))
    out_specs = (P(ALL, None), P(ALL, None), P(REP, None))
    return jax.shard_map(
        per_device, mesh=fine, in_specs=in_specs, out_specs=out_specs, check_vma=False
    )
```

time: 546 us -> 191 us (0.35)
  the two profiles are of different devices: /device:TPU:1 before, /device:TPU:9 now
where the time goes in v1:
time: 191 us; the launch traced here: 190 us
  starting transfers between devices  90.1 us (47%)
  waiting for transfers between devices  39.3 us (21%)
  blocking collectives  26.2 us (14%)
  matrix products  16.3 us (9%)
  other arithmetic  10.4 us (5%)
  local copies, waits for them, and re-layouts  4.79 us (3%)
  between operations  2.92 us (2%)
    all_to_all x4, starting transfers between devices, exchange(): return lax.all_to_all(array, axes, split_axis=0, concat_axis=0, tiled=True)  54.6 us
    all_to_all x4, waiting for transfers between devices, exchange(): return lax.all_to_all(array, axes, split_axis=0, concat_axis=0, tiled=True)  31.7 us
    all_to_all x2, blocking collectives, exchange(): return lax.all_to_all(array, axes, split_axis=0, concat_axis=0, tiled=True)  26.2 us
    dot_general x15, matrix products, dot(): lax.dot_general(a, b, (((ca,), (cb,)), ((), ())), preferred_element_type=...  16.3 us
    ppermute x1, starting transfers between devices, per_device(): other = lax.ppermute(halves, 'core', SWAP)  11.7 us
    ppermute x1, waiting for transfers between devices, per_device(): back_a = lax.ppermute(pair, DP, by_chip(-1))  6.94 us
    ppermute x1, starting transfers between devices, per_device(): back_a = lax.ppermute(pair, DP, by_chip(-1))  6.73 us
    ppermute x1, starting transfers between devices, per_device(): text_c = lax.ppermute(texts, DP, REST)  6.16 us
  transfers between devices with their start and end apart: 11, of which 6 were waited for; matrix products, arithmetic and copies ran while one was open for 7% of the time, Pallas kernels for 0%

profile of v1, /device:TPU:9, one launch (start us, length us, event | category | flops | bytes accessed | tf_op | source)
XLA Modules:
  0.0 190.0 jit_solution(8721326532205098564)
XLA Ops:
  0.7 1.0 constant_dynamic-slice_fusion
  1.6 1.2 broadcast_in_dim.18
  2.8 5.3 %all-to-all-start = ((bf16[8,72,1152]{2,1,0:T(8,128)(2,1)}), bf16[8,72,1152]{2,1,0:T(8,128)(2,1)S(1)}, u32[]{:S(2)}, u32[]{:S(2)}) async-start(bf16[8,72,1152]{2,1,0:T(8,128)(2,1)} %broadcast_in_dim.18), calls=%async_computation | async-start | bytes 2654208 | tf_op jit(solution)/shard_map/all_to_all | solution.py:28
  8.2 4.2 %collective-permute-start.1 = (bf16[256,1152]{1,0:T(8,128)(2,1)S(1)}, bf16[256,1152]{1,0:T(8,128)(2,1)}, u32[]{:S(2)}, u32[]{:S(2)}) collective-permute-start(bf16[256,1152]{1,0:T(8,128)(2,1)S(1)} %copy-done.1), channel_id=1, source_target_pairs={{0,16},{8,24},{16,32},{24,40},{32,48},{40,56},{48,64},{56,72},{64,... | collective-permute-start | bytes 1769480 | tf_op jit(solution)/shard_map/ppermute | solution.py:57
  12.4 6.2 %collective-permute-start.3 = (bf16[256,1152]{1,0:T(8,128)(2,1)S(1)}, bf16[256,1152]{1,0:T(8,128)(2,1)S(1)}, u32[]{:S(2)}, u32[]{:S(2)}) collective-permute-start(bf16[256,1152]{1,0:T(8,128)(2,1)S(1)} %copy-done.1), channel_id=1, source_target_pairs={{0,8},{8,32},{16,24},{24,48},{32,40},{40,64},{48,56},{56,80},{64,7... | collective-permute-start | bytes 1769480 | tf_op jit(solution)/shard_map/ppermute | solution.py:58
  20.7 11.2 %all-to-all-done = bf16[8,72,1152]{2,1,0:T(8,128)(2,1)S(1)} async-done(((bf16[8,72,1152]{2,1,0:T(8,128)(2,1)}), bf16[8,72,1152]{2,1,0:T(8,128)(2,1)S(1)}, u32[]{:S(2)}, u32[]{:S(2)}) %all-to-all-start) | async-done | bytes 1327136 | tf_op jit(solution)/shard_map/all_to_all | solution.py:28
  31.9 11.7 %collective-permute-start = (bf16[8,72,1152]{2,1,0:T(8,128)(2,1)S(1)}, bf16[8,72,1152]{2,1,0:T(8,128)(2,1)S(1)}, u32[]{:S(2)}, u32[]{:S(2)}) collective-permute-start(bf16[8,72,1152]{2,1,0:T(8,128)(2,1)S(1)} %all-to-all-done), channel_id=1, source_target_pairs={{0,8},{8,0},{1,9},{9,1},{2,10},{10,2},{3,11},{11,3},{4,12},{12,4},... | collective-permute-start | bytes 3981320 | tf_op jit(solution)/shard_map/ppermute | solution.py:63
  43.6 1.9 %collective-permute-start.2 = (bf16[256,1152]{1,0:T(8,128)(2,1)}, bf16[256,1152]{1,0:T(8,128)(2,1)S(1)}, u32[]{:S(2)}, u32[]{:S(2)}) collective-permute-start(bf16[256,1152]{1,0:T(8,128)(2,1)} %collective-permute-done.1), channel_id=1, source_target_pairs={{0,8},{8,0},{1,9},{9,1},{2,10},{10,2},{3,11},{11,3},{4,12},{12,4},... | collective-permute-start | bytes 1769480 | tf_op jit(solution)/shard_map/ppermute | solution.py:59
  45.5 1.3 fusion.9
  48.7 1.0 multiply_reduce_fusion
  52.3 1.5 fusion.46
  53.9 1.6 convolution_add_fusion.1
  56.7 1.0 convolution_convert_fusion
  57.9 9.0 %all_to_all.30 = bf16[2,8,72,1152]{3,2,1,0:T(8,128)(2,1)} all-to-all(bf16[2,8,72,1152]{3,2,1,0:T(8,128)(2,1)S(1)} %bitcast.58), channel_id=1, replica_groups=mesh['z'=8,'yh'=4,'core'=2,'x'=4,'yl'=2] {'core'}, dimensions={0} | all-to-all | bytes 5308416 | tf_op jit(solution)/shard_map/all_to_all | solution.py:28
  66.9 3.7 %reduce_sum.106 = bf16[8,72,1152]{2,1,0:T(8,128)(2,1)} reduce(bf16[2,8,72,1152]{3,2,1,0:T(8,128)(2,1)} %all_to_all.30, bf16[]{:T(256)} %constant.39.clone.1), dimensions={0}, to_apply=%region_7.8 | reduce | flops 663552 | bytes 3981314 | tf_op jit(solution)/shard_map/reduce_sum | solution.py:95
  70.6 25.7 %all-to-all-start.2 = ((bf16[8,72,1152]{2,1,0:T(8,128)(2,1)}), bf16[8,72,1152]{2,1,0:T(8,128)(2,1)S(1)}, u32[]{:S(2)}, u32[]{:S(2)}) async-start(bf16[8,72,1152]{2,1,0:T(8,128)(2,1)} %reduce_sum.106), calls=%async_computation.2 | async-start | bytes 2654208 | tf_op jit(solution)/shard_map/all_to_all | solution.py:28
  96.7 2.8 %collective-permute-start.4 = (bf16[256,1152]{1,0:T(8,128)(2,1)S(1)}, bf16[256,1152]{1,0:T(8,128)(2,1)S(1)}, u32[]{:S(2)}, u32[]{:S(2)}) collective-permute-start(bf16[256,1152]{1,0:T(8,128)(2,1)S(1)} %convolution_convert_fusion.3), channel_id=1, source_target_pairs={{0,8},{8,0},{1,9},{9,1},{2,10},{10,2},{3,11},{11,3},{4,12},{12,4},... | collective-permute-start | bytes 1769480 | tf_op jit(solution)/shard_map/ppermute | solution.py:87
  99.5 1.2 convolution_convert_fusion.2
  100.7 1.9 %collective-permute-start.6 = (bf16[256,1152]{1,0:T(8,128)(2,1)}, bf16[256,1152]{1,0:T(8,128)(2,1)}, u32[]{:S(2)}, u32[]{:S(2)}) collective-permute-start(bf16[256,1152]{1,0:T(8,128)(2,1)} %convolution_convert_fusion.2), channel_id=1, source_target_pairs={{8,0},{32,8},{24,16},{48,24},{40,32},{64,40},{56,48},{80,56},{72,6... | collective-permute-start | bytes 1769480 | tf_op jit(solution)/shard_map/ppermute | solution.py:88
  102.7 1.2 add_convert_fusion
  103.8 6.7 %collective-permute-start.5 = (bf16[256,1152]{1,0:T(8,128)(2,1)}, bf16[256,1152]{1,0:T(8,128)(2,1)}, u32[]{:S(2)}, u32[]{:S(2)}) collective-permute-start(bf16[256,1152]{1,0:T(8,128)(2,1)} %add_convert_fusion), channel_id=1, source_target_pairs={{0,496},{8,504},{16,0},{24,8},{32,16},{40,24},{48,32},{56,40},{64,... | collective-permute-start | bytes 1769480 | tf_op jit(solution)/shard_map/ppermute | solution.py:90
  110.6 3.1 %all-to-all-done.2 = bf16[8,72,1152]{2,1,0:T(8,128)(2,1)S(1)} async-done(((bf16[8,72,1152]{2,1,0:T(8,128)(2,1)}), bf16[8,72,1152]{2,1,0:T(8,128)(2,1)S(1)}, u32[]{:S(2)}, u32[]{:S(2)}) %all-to-all-start.2) | async-done | bytes 1327136 | tf_op jit(solution)/shard_map/all_to_all | solution.py:28
  114.7 16.5 %all-to-all-start.3 = ((bf16[32,3,1152]{2,1,0:T(4,128)(2,1)}), bf16[32,3,1152]{2,1,0:T(4,128)(2,1)S(1)}, u32[]{:S(2)}, u32[]{:S(2)}) async-start(bf16[32,3,1152]{2,1,0:T(4,128)(2,1)} %reshape.74), calls=%async_computation.3 | async-start | bytes 589824 | tf_op jit(solution)/shard_map/all_to_all | solution.py:28
  131.3 3.6 %convolution_convert_fusion.1 = bf16[256,1152]{1,0:T(8,128)(2,1)} fusion(bf16[256,1152]{0,1:T(8,128)(2,1)S(1)} %copy-done.4, bf16[1152,1152]{1,0:T(8,128)(2,1)} %bitcast.62), kind=kOutput, calls=%fused_computation.6 | convolution fusion | flops 679772160 | bytes 3833856 | tf_op jit(solution)/shard_map/dot_general | solution.py:15
  134.9 6.9 %collective-permute-done.5 = bf16[256,1152]{1,0:T(8,128)(2,1)} collective-permute-done((bf16[256,1152]{1,0:T(8,128)(2,1)}, bf16[256,1152]{1,0:T(8,128)(2,1)}, u32[]{:S(2)}, u32[]{:S(2)}) %collective-permute-start.5) | collective-permute-done | bytes 589856 | tf_op jit(solution)/shard_map/ppermute | solution.py:90
  141.8 1.9 fusion.4
  143.7 8.2 %all-to-all-done.3 = bf16[32,3,1152]{2,1,0:T(4,128)(2,1)S(1)} async-done(((bf16[32,3,1152]{2,1,0:T(4,128)(2,1)}), bf16[32,3,1152]{2,1,0:T(4,128)(2,1)S(1)}, u32[]{:S(2)}, u32[]{:S(2)}) %all-to-all-start.3) | async-done | bytes 221216 | tf_op jit(solution)/shard_map/all_to_all | solution.py:28
  152.8 7.1 %all-to-all-start.4 = ((bf16[32,3,1152]{2,1,0:T(4,128)(2,1)}), bf16[32,3,1152]{2,1,0:T(4,128)(2,1)S(1)}, u32[]{:S(2)}, u32[]{:S(2)}) async-start(bf16[32,3,1152]{2,1,0:T(4,128)(2,1)} %broadcast_in_dim.19), calls=%async_computation.4 | async-start | bytes 589824 | tf_op jit(solution)/shard_map/all_to_all | solution.py:28
  159.9 2.4 %fusion.7 = bf16[256,1152]{1,0:T(8,128)(2,1)} fusion(bf16[256,1152]{1,0:T(8,128)(2,1)S(1)} %copy-done.1, f32[256]{0:T(256)S(1)} %get-tuple-element.7, f32[256]{0:T(256)S(1)} %add_rsqrt_fusion.3, bf16[256,1152]{1,0:T(8,128)(2,1)} %collective-permute-done.6, f32[256,1152]{1,0:T(8,128)S(1)} %get-tuple-element.8, bf16[256,1152]{1,0:T(8,128)(2,1)} %collective-permute-done.5), kind=kLoop, calls=%fused_computation.23 | loop fusion | flops 2949120 | bytes 3540992 | tf_op jit(solution)/shard_map/convert_element_type | solution.py:108
  162.4 9.2 %all-to-all-done.4 = bf16[32,3,1152]{2,1,0:T(4,128)(2,1)S(1)} async-done(((bf16[32,3,1152]{2,1,0:T(4,128)(2,1)}), bf16[32,3,1152]{2,1,0:T(4,128)(2,1)S(1)}, u32[]{:S(2)}, u32[]{:S(2)}) %all-to-all-start.4) | async-done | bytes 221216 | tf_op jit(solution)/shard_map/all_to_all | solution.py:28
  171.9 17.2 %all_to_all.31 = bf16[2,72,1152]{2,1,0:T(8,128)(2,1)S(1)} all-to-all(bf16[2,72,1152]{2,1,0:T(8,128)(2,1)S(1)} %broadcast_in_dim.21), channel_id=1, replica_groups=mesh['z'=8,'yh'=4,'core'=2,'x'=4,'yl'=2] {'core'}, dimensions={0} | all-to-all | bytes 663552 | tf_op jit(solution)/shard_map/all_to_all | solution.py:28
  189.1 0.9 bitcast_convert_fusion.1
  (48 shorter events, 8.8 us)
Async XLA Ops:
  0.6 48.1 %copy-start = (bf16[256,1152]{1,0:T(8,128)(2,1)S(1)}, bf16[256,1152]{1,0:T(8,128)(2,1)}, u32[]{:S(2)}) copy-start(bf16[256,1152]{1,0:T(8,128)(2,1)} %param.6) | copy-start | bytes 1769476
  2.8 5.3 %copy-start.1 = (bf16[256,1152]{1,0:T(8,128)(2,1)S(1)}, bf16[256,1152]{1,0:T(8,128)(2,1)}, u32[]{:S(2)}) copy-start(bf16[256,1152]{1,0:T(8,128)(2,1)} %param.7) | copy-start | bytes 1769476
  2.8 29.0 %all-to-all-start = ((bf16[8,72,1152]{2,1,0:T(8,128)(2,1)}), bf16[8,72,1152]{2,1,0:T(8,128)(2,1)S(1)}, u32[]{:S(2)}, u32[]{:S(2)}) async-start(bf16[8,72,1152]{2,1,0:T(8,128)(2,1)} %broadcast_in_dim.18), calls=%async_computation | async-start | bytes 2654208 | tf_op jit(solution)/shard_map/all_to_all | solution.py:28
  8.2 35.4 %collective-permute-start.1 = (bf16[256,1152]{1,0:T(8,128)(2,1)S(1)}, bf16[256,1152]{1,0:T(8,128)(2,1)}, u32[]{:S(2)}, u32[]{:S(2)}) collective-permute-start(bf16[256,1152]{1,0:T(8,128)(2,1)S(1)} %copy-done.1), channel_id=1, source_target_pairs={{0,16},{8,24},{16,32},{24,40},{32,48},{40,56},{48,64},{56,72},{64,... | collective-permute-start | bytes 1769480 | tf_op jit(solution)/shard_map/ppermute | solution.py:57
  12.4 34.4 %collective-permute-start.3 = (bf16[256,1152]{1,0:T(8,128)(2,1)S(1)}, bf16[256,1152]{1,0:T(8,128)(2,1)S(1)}, u32[]{:S(2)}, u32[]{:S(2)}) collective-permute-start(bf16[256,1152]{1,0:T(8,128)(2,1)S(1)} %copy-done.1), channel_id=1, source_target_pairs={{0,8},{8,32},{16,24},{24,48},{32,40},{40,64},{48,56},{56,80},{64,7... | collective-permute-start | bytes 1769480 | tf_op jit(solution)/shard_map/ppermute | solution.py:58
  31.9 16.0 %collective-permute-start = (bf16[8,72,1152]{2,1,0:T(8,128)(2,1)S(1)}, bf16[8,72,1152]{2,1,0:T(8,128)(2,1)S(1)}, u32[]{:S(2)}, u32[]{:S(2)}) collective-permute-start(bf16[8,72,1152]{2,1,0:T(8,128)(2,1)S(1)} %all-to-all-done), channel_id=1, source_target_pairs={{0,8},{8,0},{1,9},{9,1},{2,10},{10,2},{3,11},{11,3},{4,12},{12,4},... | collective-permute-start | bytes 3981320 | tf_op jit(solution)/shard_map/ppermute | solution.py:63
  43.6 4.1 %collective-permute-start.2 = (bf16[256,1152]{1,0:T(8,128)(2,1)}, bf16[256,1152]{1,0:T(8,128)(2,1)S(1)}, u32[]{:S(2)}, u32[]{:S(2)}) collective-permute-start(bf16[256,1152]{1,0:T(8,128)(2,1)} %collective-permute-done.1), channel_id=1, source_target_pairs={{0,8},{8,0},{1,9},{9,1},{2,10},{10,2},{3,11},{11,3},{4,12},{12,4},... | collective-permute-start | bytes 1769480 | tf_op jit(solution)/shard_map/ppermute | solution.py:59
  48.7 1.5 copy-start.2
  53.9 1.6 copy-start.5
  56.7 1.0 copy-start.3
  70.6 43.1 %all-to-all-start.2 = ((bf16[8,72,1152]{2,1,0:T(8,128)(2,1)}), bf16[8,72,1152]{2,1,0:T(8,128)(2,1)S(1)}, u32[]{:S(2)}, u32[]{:S(2)}) async-start(bf16[8,72,1152]{2,1,0:T(8,128)(2,1)} %reduce_sum.106), calls=%async_computation.2 | async-start | bytes 2654208 | tf_op jit(solution)/shard_map/all_to_all | solution.py:28
  96.3 6.4 %copy-start.6 = (bf16[256,256]{1,0:T(8,128)(2,1)S(1)}, bf16[256,256]{1,0:T(8,128)(2,1)}, u32[]{:S(2)}) copy-start(bf16[256,256]{1,0:T(8,128)(2,1)} %copy-done.5) | copy-start | bytes 393220
  96.7 6.0 %collective-permute-start.4 = (bf16[256,1152]{1,0:T(8,128)(2,1)S(1)}, bf16[256,1152]{1,0:T(8,128)(2,1)S(1)}, u32[]{:S(2)}, u32[]{:S(2)}) collective-permute-start(bf16[256,1152]{1,0:T(8,128)(2,1)S(1)} %convolution_convert_fusion.3), channel_id=1, source_target_pairs={{0,8},{8,0},{1,9},{9,1},{2,10},{10,2},{3,11},{11,3},{4,12},{12,4},... | collective-permute-start | bytes 1769480 | tf_op jit(solution)/shard_map/ppermute | solution.py:87
  100.7 34.2 %collective-permute-start.6 = (bf16[256,1152]{1,0:T(8,128)(2,1)}, bf16[256,1152]{1,0:T(8,128)(2,1)}, u32[]{:S(2)}, u32[]{:S(2)}) collective-permute-start(bf16[256,1152]{1,0:T(8,128)(2,1)} %convolution_convert_fusion.2), channel_id=1, source_target_pairs={{8,0},{32,8},{24,16},{48,24},{40,32},{64,40},{56,48},{80,56},{72,6... | collective-permute-start | bytes 1769480 | tf_op jit(solution)/shard_map/ppermute | solution.py:88
  103.8 38.0 %collective-permute-start.5 = (bf16[256,1152]{1,0:T(8,128)(2,1)}, bf16[256,1152]{1,0:T(8,128)(2,1)}, u32[]{:S(2)}, u32[]{:S(2)}) collective-permute-start(bf16[256,1152]{1,0:T(8,128)(2,1)} %add_convert_fusion), channel_id=1, source_target_pairs={{0,496},{8,504},{16,0},{24,8},{32,16},{40,24},{48,32},{56,40},{64,... | collective-permute-start | bytes 1769480 | tf_op jit(solution)/shard_map/ppermute | solution.py:90
  113.9 17.4 %copy-start.4 = (bf16[256,1152]{0,1:T(8,128)(2,1)S(1)}, bf16[256,1152]{0,1:T(8,128)(2,1)}, u32[]{:S(2)}) copy-start(bf16[256,1152]{0,1:T(8,128)(2,1)} %copy-done.3) | copy-start | bytes 1769476
  114.7 37.2 %all-to-all-start.3 = ((bf16[32,3,1152]{2,1,0:T(4,128)(2,1)}), bf16[32,3,1152]{2,1,0:T(4,128)(2,1)S(1)}, u32[]{:S(2)}, u32[]{:S(2)}) async-start(bf16[32,3,1152]{2,1,0:T(4,128)(2,1)} %reshape.74), calls=%async_computation.3 | async-start | bytes 589824 | tf_op jit(solution)/shard_map/all_to_all | solution.py:28
  152.8 18.8 %all-to-all-start.4 = ((bf16[32,3,1152]{2,1,0:T(4,128)(2,1)}), bf16[32,3,1152]{2,1,0:T(4,128)(2,1)S(1)}, u32[]{:S(2)}, u32[]{:S(2)}) async-start(bf16[32,3,1152]{2,1,0:T(4,128)(2,1)} %broadcast_in_dim.19), calls=%async_computation.4 | async-start | bytes 589824 | tf_op jit(solution)/shard_map/all_to_all | solution.py:28

commit v2 on v1

v2 whole, which is shorter than its diff:
```python
import jax
import jax.numpy as jnp
from jax import lax
from jax.sharding import Mesh
from jax.sharding import PartitionSpec as P

EPS = 1e-06
DP = ("z", "yh", "core")
RING = ("z", "yh")
REP = ("x", "yl")
ALL = DP + REP


def dot(a, b, ca, cb):
    return lax.dot_general(a, b, (((ca,), (cb,)), ((), ())), preferred_element_type=jnp.float32)


def by_chip(shift):
    return [(p, (p + 2 * shift) % 64) for p in range(64)]


SWAP = [(0, 1), (1, 0)]
AHEAD = [(p + 1, p) if p % 2 == 0 else ((p + 3) % 64, p) for p in range(64)]


def place(dp, x, y_lo):
    return dp * 8 + x * 2 + y_lo


def far_moves():
    first, second = [], []
    for x in range(4):
        for y_lo in range(2):
            for p in range(0, 64, 2):
                first.append((place(p, x, y_lo), place(p, x, y_lo)))
                second.append((place(p, x, y_lo), place(p + 1, x, y_lo)))
                source = (p + 61) % 64
                z, y, core = source // 8, (source // 2 % 4) * 2 + y_lo, source % 2
                back = (y + 7) % 8
                via = place((z * 4 + back // 2) * 2 + core, x, back % 2)
                first.append((place(source, x, y_lo), via))
                second.append((via, place(p, x, y_lo)))
    return sorted(first), sorted(second)


FAR_FIRST, FAR_SECOND = far_moves()


def exchange(array, axes):
    return lax.all_to_all(array, axes, split_axis=0, concat_axis=0, tiled=True)


def spread(array, axes, count):
    return exchange(jnp.broadcast_to(array[None], (count,) + array.shape), axes)


def unit_rows(values):
    inverse = lax.rsqrt(jnp.sum(values * values, axis=-1, keepdims=True) + EPS)
    return values * inverse, inverse


def negatives(logits, scale):
    return (scale * jax.nn.sigmoid(logits)).astype(jnp.bfloat16)


def off_unit(direction, unit, inverse):
    return (direction - unit * jnp.sum(unit * direction, axis=-1, keepdims=True)) * inverse


def per_device(images, texts, head, scale, bias, offsets):
    rows, width = images.shape
    share = head.shape[0]
    half = share // 2
    scale, bias, offset = scale[0], bias[0], offsets[0]
    core = lax.axis_index("core")

    far = lax.ppermute(texts, ALL, FAR_FIRST)
    text_a = lax.ppermute(texts, DP, by_chip(1))
    text_c = lax.ppermute(far, ALL, FAR_SECOND)
    text_b = lax.ppermute(text_a, "core", SWAP)

    own_half = lax.dynamic_slice_in_dim(head, core * half, half, 0)
    pair = spread(own_half, "yl", 2)
    halves = spread(pair, "x", 4)
    other = lax.ppermute(halves, "core", SWAP)
    halves, other = halves.reshape(8, half, width), other.reshape(8, half, width)
    full_head = jnp.where(
        core == 0, jnp.stack([halves, other], 1), jnp.stack([other, halves], 1)
    ).reshape(width, width)

    image_p = lax.ppermute(images, "core", SWAP)
    image_a = lax.ppermute(images, DP, by_chip(-1))
    image_c = lax.ppermute(images, DP, AHEAD)
    image_b = lax.ppermute(image_a, "core", SWAP)

    place_of = jnp.arange(width // 2, dtype=jnp.int32)
    wanted = (place_of // half) * share + core * half + place_of % half
    pick = (jnp.arange(width, dtype=jnp.int32)[:, None] == wanted[None, :]).astype(jnp.bfloat16)
    picked = jnp.concatenate([dot(images, pick, 1, 0), dot(image_p, pick, 1, 0)], 0).astype(jnp.bfloat16)

    proj = dot(images, full_head, 1, 0)
    img_unit, inv_img = unit_rows(proj)
    img_b = img_unit.astype(jnp.bfloat16)
    txt_unit, inv_txt = unit_rows(texts.astype(jnp.float32))
    txt_b = txt_unit.astype(jnp.bfloat16)
    target = (jnp.arange(rows, dtype=jnp.int32) + offset) % rows
    positive = jnp.arange(rows, dtype=jnp.int32)[None, :] == target[:, None]
    sign = jnp.where(positive, jnp.float32(1.0), jnp.float32(-1.0))
    logits = scale * dot(img_b, txt_b, 1, 1) + bias
    own_weights = (scale * (-sign * jax.nn.sigmoid(-sign * logits))).astype(jnp.bfloat16)

    img_dir = dot(own_weights, txt_b, 1, 0)
    for block in (text_a, text_b, text_c):
        block_b = unit_rows(block.astype(jnp.float32))[0].astype(jnp.bfloat16)
        weights = negatives(scale * dot(img_b, block_b, 1, 1) + bias, scale)
        img_dir = img_dir + dot(weights, block_b, 1, 0)
    proj_grad = off_unit(img_dir, img_unit, inv_img).astype(jnp.bfloat16)

    grad_p = lax.ppermute(proj_grad, "core", SWAP)
    term = dot(picked, jnp.concatenate([proj_grad, grad_p], 0), 0, 0).astype(jnp.bfloat16)
    term = exchange(term.reshape(8, half, width), REP)
    term = jnp.sum(term.astype(jnp.float32), axis=0).astype(jnp.bfloat16)
    padded = jnp.pad(term, ((0, 96 - half), (0, 0))).reshape(32, 3, width)
    padded = exchange(padded, RING)
    mine = jnp.sum(padded.astype(jnp.float32), axis=0).astype(jnp.bfloat16)
    done = spread(mine, RING, 32).reshape(96, width)[:half]
    head_grad = spread(done, "core", 2).reshape(share, width).astype(jnp.float32)

    image_grad = dot(proj_grad, full_head, 1, 1).astype(jnp.bfloat16)

    txt_dir = dot(own_weights, img_b, 0, 0)
    for block in (image_a, image_b, image_c):
        block_b = unit_rows(dot(block, full_head, 1, 0))[0].astype(jnp.bfloat16)
        weights = negatives(scale * dot(block_b, txt_b, 1, 1) + bias, scale)
        txt_dir = txt_dir + dot(weights, block_b, 0, 0)
    text_grad = off_unit(txt_dir, txt_unit, inv_txt).astype(jnp.bfloat16)
    return image_grad, text_grad, head_grad


def solution(mesh):
    fine = Mesh(mesh.devices.reshape(8, 4, 2, 4, 2), ALL)
    in_specs = (P(ALL, None), P(ALL, None), P(REP, None), P(), P(), P(ALL))
    out_specs = (P(ALL, None), P(ALL, None), P(REP, None))
    return jax.shard_map(
        per_device, mesh=fine, in_specs=in_specs, out_specs=out_specs, check_vma=False
    )
```

time: 191 us -> 192 us (level)
  the two profiles are of different devices: /device:TPU:9 before, /device:TPU:1 now
where the time goes in v2:
time: 192 us; the launch traced here: 190 us
  starting transfers between devices  72.5 us (38%)
  waiting for transfers between devices  43.3 us (23%)
  matrix products  43 us (22%)
  blocking collectives  14.5 us (8%)
  other arithmetic  9.43 us (5%)
  local copies, waits for them, and re-layouts  4.67 us (2%)
  between operations  2.96 us (2%)
    dot_general x17, matrix products, dot(): lax.dot_general(a, b, (((ca,), (cb,)), ((), ())), preferred_element_type=...  43 us
    all_to_all x4, starting transfers between devices, exchange(): return lax.all_to_all(array, axes, split_axis=0, concat_axis=0, tiled=True)  24 us
    all_to_all x4, waiting for transfers between devices, exchange(): return lax.all_to_all(array, axes, split_axis=0, concat_axis=0, tiled=True)  19.4 us
    ppermute x1, waiting for transfers between devices, per_device(): text_c = lax.ppermute(far, ALL, FAR_SECOND)  14.8 us
    all_to_all x2, blocking collectives, exchange(): return lax.all_to_all(array, axes, split_axis=0, concat_axis=0, tiled=True)  14.5 us
    ppermute x1, starting transfers between devices, per_device(): image_c = lax.ppermute(images, DP, AHEAD)  13.8 us
    ppermute x1, starting transfers between devices, per_device(): image_a = lax.ppermute(images, DP, by_chip(-1))  10.4 us
    ppermute x1, waiting for transfers between devices, per_device(): text_a = lax.ppermute(texts, DP, by_chip(1))  9.2 us
  transfers between devices with their start and end apart: 14, of which 5 were waited for; matrix products, arithmetic and copies ran while one was open for 26% of the time, Pallas kernels for 0%

profile of v2, /device:TPU:1, one launch (start us, length us, event | category | flops | bytes accessed | tf_op | source)
XLA Modules:
  0.0 190.4 jit_solution(15892910256012868452)
XLA Ops:
  1.7 7.6 %all_to_all.30 = bf16[2,72,1152]{2,1,0:T(8,128)(2,1)S(1)} all-to-all(bf16[2,72,1152]{2,1,0:T(8,128)(2,1)S(1)} %broadcast_in_dim.20), channel_id=1, replica_groups=mesh['z'=8,'yh'=4,'core'=2,'x'=4,'yl'=2] {'yl'}, dimensions={0} | all-to-all | bytes 663552 | tf_op jit(solution)/shard_map/all_to_all | solution.py:50
  10.4 4.8 %all-to-all-start.1 = ((bf16[4,2,72,1152]{3,2,1,0:T(8,128)(2,1)}), bf16[4,2,72,1152]{3,2,1,0:T(8,128)(2,1)S(1)}, u32[]{:S(2)}, u32[]{:S(2)}) async-start(bf16[4,2,72,1152]{3,2,1,0:T(8,128)(2,1)} %broadcast_in_dim.21), calls=%async_computation.1 | async-start | bytes 2654208 | tf_op jit(solution)/shard_map/all_to_all | solution.py:50
  15.2 5.3 %collective-permute-start.3 = (bf16[256,1152]{1,0:T(8,128)(2,1)S(1)}, bf16[256,1152]{1,0:T(8,128)(2,1)}, u32[]{:S(2)}, u32[]{:S(2)}) collective-permute-start(bf16[256,1152]{1,0:T(8,128)(2,1)S(1)} %copy-done.1), channel_id=1, source_target_pairs={{0,0},{1,1},{2,2},{3,3},{4,4},{5,5},{6,6},{7,7},{8,57},{9,8},{10,5... | collective-permute-start | bytes 1769480 | tf_op jit(solution)/shard_map/ppermute | solution.py:77
  20.6 1.9 %collective-permute-start.1 = (bf16[256,1152]{1,0:T(8,128)(2,1)S(1)}, bf16[256,1152]{1,0:T(8,128)(2,1)S(1)}, u32[]{:S(2)}, u32[]{:S(2)}) collective-permute-start(bf16[256,1152]{1,0:T(8,128)(2,1)S(1)} %copy-done.1), channel_id=1, source_target_pairs={{0,16},{8,24},{16,32},{24,40},{32,48},{40,56},{48,64},{56,72},{64,... | collective-permute-start | bytes 1769480 | tf_op jit(solution)/shard_map/ppermute | solution.py:78
  22.5 4.2 %collective-permute-start.8 = (bf16[256,1152]{1,0:T(8,128)(2,1)}, bf16[256,1152]{1,0:T(8,128)(2,1)}, u32[]{:S(2)}, u32[]{:S(2)}) collective-permute-start(bf16[256,1152]{1,0:T(8,128)(2,1)} %param.6), channel_id=1, source_target_pairs={{0,8},{8,0},{1,9},{9,1},{2,10},{10,2},{3,11},{11,3},{4,12},{12,4},... | collective-permute-start | bytes 1769480 | tf_op jit(solution)/shard_map/ppermute | solution.py:91
  26.7 10.4 %collective-permute-start.5 = (bf16[256,1152]{1,0:T(8,128)(2,1)}, bf16[256,1152]{1,0:T(8,128)(2,1)}, u32[]{:S(2)}, u32[]{:S(2)}) collective-permute-start(bf16[256,1152]{1,0:T(8,128)(2,1)} %param.6), channel_id=1, source_target_pairs={{0,496},{8,504},{16,0},{24,8},{32,16},{40,24},{48,32},{56,40},{64,... | collective-permute-start | bytes 1769480 | tf_op jit(solution)/shard_map/ppermute | solution.py:92
  39.2 2.4 %collective-permute-start = (bf16[4,2,72,1152]{3,2,1,0:T(8,128)(2,1)S(1)}, bf16[4,2,72,1152]{3,2,1,0:T(8,128)(2,1)}, u32[]{:S(2)}, u32[]{:S(2)}) collective-permute-start(bf16[4,2,72,1152]{3,2,1,0:T(8,128)(2,1)S(1)} %all-to-all-done.1), channel_id=1, source_target_pairs={{0,8},{8,0},{1,9},{9,1},{2,10},{10,2},{3,11},{11,3},{4,12},{12,4},... | collective-permute-start | bytes 3981320 | tf_op jit(solution)/shard_map/ppermute | solution.py:85
  43.6 9.2 %collective-permute-done.1 = bf16[256,1152]{1,0:T(8,128)(2,1)S(1)} collective-permute-done((bf16[256,1152]{1,0:T(8,128)(2,1)S(1)}, bf16[256,1152]{1,0:T(8,128)(2,1)S(1)}, u32[]{:S(2)}, u32[]{:S(2)}) %collective-permute-start.1) | collective-permute-done | bytes 589856 | tf_op jit(solution)/shard_map/ppermute | solution.py:78
  52.8 3.0 %collective-permute-start.2 = (bf16[256,1152]{1,0:T(8,128)(2,1)S(1)}, bf16[256,1152]{1,0:T(8,128)(2,1)S(1)}, u32[]{:S(2)}, u32[]{:S(2)}) collective-permute-start(bf16[256,1152]{1,0:T(8,128)(2,1)S(1)} %collective-permute-done.1), channel_id=1, source_target_pairs={{0,8},{8,0},{1,9},{9,1},{2,10},{10,2},{3,11},{11,3},{4,12},{12,4},... | collective-permute-start | bytes 1769480 | tf_op jit(solution)/shard_map/ppermute | solution.py:80
  56.0 14.8 %collective-permute-done.4 = bf16[256,1152]{1,0:T(8,128)(2,1)S(1)} collective-permute-done((bf16[256,1152]{1,0:T(8,128)(2,1)}, bf16[256,1152]{1,0:T(8,128)(2,1)S(1)}, u32[]{:S(2)}, u32[]{:S(2)}) %collective-permute-start.4) | collective-permute-done | bytes 589856 | tf_op jit(solution)/shard_map/ppermute | solution.py:79
  70.8 13.8 %collective-permute-start.7 = (bf16[256,1152]{1,0:T(8,128)(2,1)}, bf16[256,1152]{1,0:T(8,128)(2,1)}, u32[]{:S(2)}, u32[]{:S(2)}) collective-permute-start(bf16[256,1152]{1,0:T(8,128)(2,1)} %param.6), channel_id=1, source_target_pairs={{8,0},{32,8},{24,16},{48,24},{40,32},{64,40},{56,48},{80,56},{72,6... | collective-permute-start | bytes 1769480 | tf_op jit(solution)/shard_map/ppermute | solution.py:93
  85.6 2.4 %maximum_select_fusion = bf16[8,2,72,1152]{3,2,1,0:T(8,128)(2,1)S(1)} fusion(bf16[8,1,72,1152]{3,2,1,0:T(8,128)(2,1)} %bitcast.3, bf16[8,1,72,1152]{3,2,1,0:T(8,128)(2,1)S(1)} %bitcast.60, pred[]{:T(512)S(6)} %eq.36), kind=kLoop, calls=%fused_computation.9 | loop fusion | flops 3981312 | bytes 5308417 | tf_op jit(solution)/shard_map/jit(_where)/select_n | solution.py:87
  88.0 2.5 %multiply_reduce_fusion.3 = (f32[256]{0:T(256)S(1)}, f32[1152,256]{1,0:T(8,128)S(1)}) fusion(bf16[1152,1152]{1,0:T(8,128)(2,1)S(1)} %bitcast.61, bf16[256,1152]{1,0:T(8,128)(2,1)} %param.6), kind=kOutput, calls=%fused_computation.55 | convolution fusion | flops 680066816 | bytes 4424704 | tf_op jit(solution)/shard_map/dot_general | solution.py:15
  92.7 3.4 %fusion.92 = f32[256,1152]{0,1:T(8,128)} fusion(bf16[256,1152]{0,1:T(8,128)(2,1)S(1)} %bitcast_convert_fusion, bf16[256,1152]{1,0:T(8,128)(2,1)} %copy-done.5, f32[256]{0:T(256)S(1)} %add_rsqrt_fusion.3, f32[]{:T(128)} %bitcast.56, f32[]{:T(128)} %bitcast.45), kind=kOutput, calls=%fused_computation.116 | convolution fusion | flops 304218112 | bytes 2360328 | tf_op jit(solution)/shard_map/dot_general | solution.py:15
  96.0 3.3 %convolution_add_fusion.4 = f32[256,1152]{0,1:T(8,128)} fusion(f32[256,1152]{0,1:T(8,128)} %fusion.156, bf16[256,1152]{0,1:T(8,128)(2,1)S(1)} %bitcast_convert_fusion, bf16[256,1152]{1,0:T(8,128)(2,1)S(1)} %collective-permute-done.1, f32[256]{0:T(256)S(1)} %add_rsqrt_fusion.5, f32[]{:T(128)} %bitcast.58, f32[]{:T(128)} %bitcast.49), kind=kOutput, calls=%fused_computation.7 | convolution fusion | flops 304513024 | bytes 3539976 | tf_op jit(solution)/shard_map/dot_general | solution.py:15
  99.3 4.1 %fusion.31 = (f32[256]{0:T(256)S(1)}, f32[256,1152]{0,1:T(8,128)}) fusion(f32[1152,256]{1,0:T(8,128)S(1)} %get-tuple-element.4, f32[256]{0:T(256)S(1)} %add_rsqrt_fusion.7, f32[256,1152]{0,1:T(8,128)} %fusion.92, f32[256,1152]{0,1:T(8,128)} %convolution_add_fusion.4, bf16[256,1152]{1,0:T(8,128)(2,1)} %copy-done.2, f32[256]{0:T(256)S(1)} %add_rsqrt_fusion.4, ...), kind=kOutput, calls=%fused_computation.45 | convolution fusion | flops 305692416 | bytes 5901320 | tf_op jit(solution)/shard_map/dot_general | solution.py:15
  105.0 3.7 %collective-permute-start.9 = (bf16[256,1152]{0,1:T(8,128)(2,1)S(1)}, bf16[256,1152]{0,1:T(8,128)(2,1)S(1)}, u32[]{:S(2)}, u32[]{:S(2)}) collective-permute-start(bf16[256,1152]{0,1:T(8,128)(2,1)S(1)} %fusion.34), channel_id=1, source_target_pairs={{0,8},{8,0},{1,9},{9,1},{2,10},{10,2},{3,11},{11,3},{4,12},{12,4},... | collective-permute-start | bytes 1769480 | tf_op jit(solution)/shard_map/ppermute | solution.py:119
  114.1 2.0 %convolution_convert_fusion = bf16[576,1152]{1,0:T(8,128)(2,1)} fusion(bf16[256,1152]{0,1:T(8,128)(2,1)S(1)} %collective-permute-done.9, bf16[256,1152]{0,1:T(8,128)(2,1)S(1)} %fusion.34, bf16[256,576]{0,1:T(8,128)(2,1)S(1)} %fusion.35, bf16[256,576]{0,1:T(8,128)(2,1)S(1)} %fusion.38), kind=kOutput, calls=%fused_computation | convolution fusion | flops 683679744 | bytes 3096576 | tf_op jit(solution)/shard_map/dot_general | solution.py:15
  116.2 7.7 %all-to-all-start.2 = ((bf16[8,72,1152]{2,1,0:T(8,128)(2,1)}), bf16[8,72,1152]{2,1,0:T(8,128)(2,1)}, u32[]{:S(2)}, u32[]{:S(2)}) async-start(bf16[8,72,1152]{2,1,0:T(8,128)(2,1)} %bitcast.9), calls=%async_computation.2 | async-start | bytes 2654208 | tf_op jit(solution)/shard_map/all_to_all | solution.py:50
  123.9 3.0 %multiply_reduce_fusion.2 = (f32[256]{0:T(256)S(1)}, f32[1152,256]{1,0:T(8,128)S(1)}) fusion(bf16[1152,1152]{1,0:T(8,128)(2,1)} %bitcast.62, bf16[256,1152]{1,0:T(8,128)(2,1)} %collective-permute-done.5), kind=kOutput, calls=%fused_computation.54 | convolution fusion | flops 680066816 | bytes 4424704 | tf_op jit(solution)/shard_map/dot_general | solution.py:15
  126.9 2.0 %multiply_reduce_fusion.1 = (f32[256]{0:T(256)S(1)}, f32[1152,256]{1,0:T(8,128)}) fusion(bf16[1152,1152]{1,0:T(8,128)(2,1)S(1)} %bitcast.64, bf16[256,1152]{1,0:T(8,128)(2,1)S(1)} %collective-permute-done.6), kind=kOutput, calls=%fused_computation.52 | convolution fusion | flops 680066816 | bytes 4424704 | tf_op jit(solution)/shard_map/dot_general | solution.py:15
  130.4 2.1 %multiply_reduce_fusion = (f32[256]{0:T(256)S(1)}, f32[1152,256]{1,0:T(8,128)S(1)}) fusion(bf16[1152,1152]{1,0:T(8,128)(2,1)S(1)} %bitcast.65, bf16[256,1152]{1,0:T(8,128)(2,1)} %collective-permute-done.7), kind=kOutput, calls=%fused_computation.50 | convolution fusion | flops 680066816 | bytes 4424704 | tf_op jit(solution)/shard_map/dot_general | solution.py:15
  132.4 3.4 %convolution_add_fusion.2 = f32[256,1152]{1,0:T(8,128)} fusion(f32[256,1152]{1,0:T(8,128)} %fusion.163, f32[1152,256]{1,0:T(8,128)S(1)} %get-tuple-element.8, f32[256]{0:T(256)S(1)} %add_rsqrt_fusion.2, f32[]{:T(128)} %bitcast.55, f32[]{:T(128)} %bitcast.48, bf16[256,1152]{1,0:T(8,128)(2,1)S(1)} %copy-done.1, f32[256]{0:T(256)S(1)} %add_rsqrt_fusion.6), kind=kOutput, calls=%fused_computation.5 | convolution fusion | flops 304807936 | bytes 4130824 | tf_op jit(solution)/shard_map/dot_general | solution.py:15
  135.8 4.2 %convolution_add_fusion.1 = f32[256,1152]{1,0:T(8,128)} fusion(f32[256,1152]{1,0:T(8,128)} %convolution_add_fusion.2, f32[1152,256]{1,0:T(8,128)} %get-tuple-element.10, f32[256]{0:T(256)S(1)} %add_rsqrt_fusion.1, f32[]{:T(128)} %bitcast.54, f32[]{:T(128)} %bitcast.50, bf16[256,1152]{1,0:T(8,128)(2,1)S(1)} %copy-done.1, f32[256]{0:T(256)S(1)} %add_rsqrt_fusion.6), kind=kOutput, calls=%fused_computation.4 | convolution fusion | flops 304807936 | bytes 4130824 | tf_op jit(solution)/shard_map/dot_general | solution.py:15
  140.0 2.0 %all-to-all-done.2 = bf16[8,72,1152]{2,1,0:T(8,128)(2,1)} async-done(((bf16[8,72,1152]{2,1,0:T(8,128)(2,1)}), bf16[8,72,1152]{2,1,0:T(8,128)(2,1)}, u32[]{:S(2)}, u32[]{:S(2)}) %all-to-all-start.2) | async-done | bytes 1327136 | tf_op jit(solution)/shard_map/all_to_all | solution.py:50
  144.4 4.6 %all-to-all-start.3 = ((bf16[32,3,1152]{2,1,0:T(4,128)(2,1)}), bf16[32,3,1152]{2,1,0:T(4,128)(2,1)}, u32[]{:S(2)}, u32[]{:S(2)}) async-start(bf16[32,3,1152]{2,1,0:T(4,128)(2,1)} %reshape.113), calls=%async_computation.3 | async-start | bytes 589824 | tf_op jit(solution)/shard_map/all_to_all | solution.py:50
  149.0 2.5 %fusion.17 = (f32[256]{0:T(256)S(1)}, f32[256,1152]{1,0:T(8,128)S(1)}) fusion(bf16[256,1152]{1,0:T(8,128)(2,1)S(1)} %copy-done.1, f32[256]{0:T(256)S(1)} %add_rsqrt_fusion.6, f32[256,1152]{1,0:T(8,128)} %convolution_add_fusion.1, f32[1152,256]{1,0:T(8,128)S(1)} %get-tuple-element.12, f32[256]{0:T(256)S(1)} %add_rsqrt_fusion, f32[]{:T(128)} %bitcast.53, ...), kind=kOutput, calls=%fused_computation.28 | convolution fusion | flops 305987328 | bytes 4131848 | tf_op jit(solution)/shard_map/dot_general | solution.py:15
  151.5 9.7 %all-to-all-done.3 = bf16[32,3,1152]{2,1,0:T(4,128)(2,1)} async-done(((bf16[32,3,1152]{2,1,0:T(4,128)(2,1)}), bf16[32,3,1152]{2,1,0:T(4,128)(2,1)}, u32[]{:S(2)}, u32[]{:S(2)}) %all-to-all-start.3) | async-done | bytes 221216 | tf_op jit(solution)/shard_map/all_to_all | solution.py:50
  163.1 6.9 %all-to-all-start.4 = ((bf16[32,3,1152]{2,1,0:T(4,128)(2,1)}), bf16[32,3,1152]{2,1,0:T(4,128)(2,1)S(1)}, u32[]{:S(2)}, u32[]{:S(2)}) async-start(bf16[32,3,1152]{2,1,0:T(4,128)(2,1)} %broadcast_in_dim.22), calls=%async_computation.4 | async-start | bytes 589824 | tf_op jit(solution)/shard_map/all_to_all | solution.py:50
  171.1 3.6 %convolution_convert_fusion.1 = bf16[256,1152]{1,0:T(8,128)(2,1)} fusion(bf16[256,1152]{0,1:T(8,128)(2,1)S(1)} %copy-done.7, bf16[1152,1152]{1,0:T(8,128)(2,1)} %bitcast.63), kind=kOutput, calls=%fused_computation.10 | convolution fusion | flops 679772160 | bytes 3833856 | tf_op jit(solution)/shard_map/dot_general | solution.py:15
  174.7 7.6 %all-to-all-done.4 = bf16[32,3,1152]{2,1,0:T(4,128)(2,1)S(1)} async-done(((bf16[32,3,1152]{2,1,0:T(4,128)(2,1)}), bf16[32,3,1152]{2,1,0:T(4,128)(2,1)S(1)}, u32[]{:S(2)}, u32[]{:S(2)}) %all-to-all-start.4) | async-done | bytes 221216 | tf_op jit(solution)/shard_map/all_to_all | solution.py:50
  182.6 6.9 %all_to_all.31 = bf16[2,72,1152]{2,1,0:T(8,128)(2,1)S(1)} all-to-all(bf16[2,72,1152]{2,1,0:T(8,128)(2,1)S(1)} %broadcast_in_dim.24), channel_id=1, replica_groups=mesh['z'=8,'yh'=4,'core'=2,'x'=4,'yl'=2] {'core'}, dimensions={0} | all-to-all | bytes 663552 | tf_op jit(solution)/shard_map/all_to_all | solution.py:50
  (61 shorter events, 22.5 us)
Async XLA Ops:
  0.6 1.0 copy-start
  10.4 4.8 %copy-start.1 = (bf16[256,1152]{1,0:T(8,128)(2,1)S(1)}, bf16[256,1152]{1,0:T(8,128)(2,1)}, u32[]{:S(2)}) copy-start(bf16[256,1152]{1,0:T(8,128)(2,1)} %param.7) | copy-start | bytes 1769476
  10.4 28.8 %all-to-all-start.1 = ((bf16[4,2,72,1152]{3,2,1,0:T(8,128)(2,1)}), bf16[4,2,72,1152]{3,2,1,0:T(8,128)(2,1)S(1)}, u32[]{:S(2)}, u32[]{:S(2)}) async-start(bf16[4,2,72,1152]{3,2,1,0:T(8,128)(2,1)} %broadcast_in_dim.21), calls=%async_computation.1 | async-start | bytes 2654208 | tf_op jit(solution)/shard_map/all_to_all | solution.py:50
  15.2 22.0 %collective-permute-start.3 = (bf16[256,1152]{1,0:T(8,128)(2,1)S(1)}, bf16[256,1152]{1,0:T(8,128)(2,1)}, u32[]{:S(2)}, u32[]{:S(2)}) collective-permute-start(bf16[256,1152]{1,0:T(8,128)(2,1)S(1)} %copy-done.1), channel_id=1, source_target_pairs={{0,0},{1,1},{2,2},{3,3},{4,4},{5,5},{6,6},{7,7},{8,57},{9,8},{10,5... | collective-permute-start | bytes 1769480 | tf_op jit(solution)/shard_map/ppermute | solution.py:77
  20.6 32.2 %collective-permute-start.1 = (bf16[256,1152]{1,0:T(8,128)(2,1)S(1)}, bf16[256,1152]{1,0:T(8,128)(2,1)S(1)}, u32[]{:S(2)}, u32[]{:S(2)}) collective-permute-start(bf16[256,1152]{1,0:T(8,128)(2,1)S(1)} %copy-done.1), channel_id=1, source_target_pairs={{0,16},{8,24},{16,32},{24,40},{32,48},{40,56},{48,64},{56,72},{64,... | collective-permute-start | bytes 1769480 | tf_op jit(solution)/shard_map/ppermute | solution.py:78
  22.5 89.9 %collective-permute-start.8 = (bf16[256,1152]{1,0:T(8,128)(2,1)}, bf16[256,1152]{1,0:T(8,128)(2,1)}, u32[]{:S(2)}, u32[]{:S(2)}) collective-permute-start(bf16[256,1152]{1,0:T(8,128)(2,1)} %param.6), channel_id=1, source_target_pairs={{0,8},{8,0},{1,9},{9,1},{2,10},{10,2},{3,11},{11,3},{4,12},{12,4},... | collective-permute-start | bytes 1769480 | tf_op jit(solution)/shard_map/ppermute | solution.py:91
  26.7 83.7 %collective-permute-start.5 = (bf16[256,1152]{1,0:T(8,128)(2,1)}, bf16[256,1152]{1,0:T(8,128)(2,1)}, u32[]{:S(2)}, u32[]{:S(2)}) collective-permute-start(bf16[256,1152]{1,0:T(8,128)(2,1)} %param.6), channel_id=1, source_target_pairs={{0,496},{8,504},{16,0},{24,8},{32,16},{40,24},{48,32},{56,40},{64,... | collective-permute-start | bytes 1769480 | tf_op jit(solution)/shard_map/ppermute | solution.py:92
  37.3 33.5 %collective-permute-start.4 = (bf16[256,1152]{1,0:T(8,128)(2,1)}, bf16[256,1152]{1,0:T(8,128)(2,1)S(1)}, u32[]{:S(2)}, u32[]{:S(2)}) collective-permute-start(bf16[256,1152]{1,0:T(8,128)(2,1)} %collective-permute-done.3), channel_id=1, source_target_pairs={{0,8},{1,9},{2,10},{3,11},{4,12},{5,13},{6,14},{7,15},{8,33},{9,48... | collective-permute-start | bytes 1769480 | tf_op jit(solution)/shard_map/ppermute | solution.py:79
  39.2 45.8 %collective-permute-start = (bf16[4,2,72,1152]{3,2,1,0:T(8,128)(2,1)S(1)}, bf16[4,2,72,1152]{3,2,1,0:T(8,128)(2,1)}, u32[]{:S(2)}, u32[]{:S(2)}) collective-permute-start(bf16[4,2,72,1152]{3,2,1,0:T(8,128)(2,1)S(1)} %all-to-all-done.1), channel_id=1, source_target_pairs={{0,8},{8,0},{1,9},{9,1},{2,10},{10,2},{3,11},{11,3},{4,12},{12,4},... | collective-permute-start | bytes 3981320 | tf_op jit(solution)/shard_map/ppermute | solution.py:85
  52.8 32.0 %collective-permute-start.2 = (bf16[256,1152]{1,0:T(8,128)(2,1)S(1)}, bf16[256,1152]{1,0:T(8,128)(2,1)S(1)}, u32[]{:S(2)}, u32[]{:S(2)}) collective-permute-start(bf16[256,1152]{1,0:T(8,128)(2,1)S(1)} %collective-permute-done.1), channel_id=1, source_target_pairs={{0,8},{8,0},{1,9},{9,1},{2,10},{10,2},{3,11},{11,3},{4,12},{12,4},... | collective-permute-start | bytes 1769480 | tf_op jit(solution)/shard_map/ppermute | solution.py:80
  70.8 17.2 %copy-start.5 = (bf16[256,1152]{1,0:T(8,128)(2,1)}, bf16[256,1152]{1,0:T(8,128)(2,1)S(1)}, u32[]{:S(2)}) copy-start(bf16[256,1152]{1,0:T(8,128)(2,1)S(1)} %collective-permute-done.4) | copy-start | bytes 1769476
  70.8 59.6 %collective-permute-start.7 = (bf16[256,1152]{1,0:T(8,128)(2,1)}, bf16[256,1152]{1,0:T(8,128)(2,1)}, u32[]{:S(2)}, u32[]{:S(2)}) collective-permute-start(bf16[256,1152]{1,0:T(8,128)(2,1)} %param.6), channel_id=1, source_target_pairs={{8,0},{32,8},{24,16},{48,24},{40,32},{64,40},{56,48},{80,56},{72,6... | collective-permute-start | bytes 1769480 | tf_op jit(solution)/shard_map/ppermute | solution.py:93
  84.8 0.8 copy-start.2
  88.0 2.5 %copy-start.3 = (bf16[8,2,72,1152]{3,2,1,0:T(8,128)(2,1)}, bf16[8,2,72,1152]{3,2,1,0:T(8,128)(2,1)S(1)}, u32[]{:S(2)}) copy-start(bf16[8,2,72,1152]{3,2,1,0:T(8,128)(2,1)S(1)} %maximum_select_fusion) | copy-start | bytes 7962628
  104.9 9.2 %copy-start.6 = (bf16[256,1152]{0,1:T(8,128)(2,1)}, bf16[256,1152]{0,1:T(8,128)(2,1)S(1)}, u32[]{:S(2)}) copy-start(bf16[256,1152]{0,1:T(8,128)(2,1)S(1)} %fusion.34) | copy-start | bytes 1769476
  105.0 9.1 %collective-permute-start.9 = (bf16[256,1152]{0,1:T(8,128)(2,1)S(1)}, bf16[256,1152]{0,1:T(8,128)(2,1)S(1)}, u32[]{:S(2)}, u32[]{:S(2)}) collective-permute-start(bf16[256,1152]{0,1:T(8,128)(2,1)S(1)} %fusion.34), channel_id=1, source_target_pairs={{0,8},{8,0},{1,9},{9,1},{2,10},{10,2},{3,11},{11,3},{4,12},{12,4},... | collective-permute-start | bytes 1769480 | tf_op jit(solution)/shard_map/ppermute | solution.py:119
  110.4 16.4 %collective-permute-start.6 = (bf16[256,1152]{1,0:T(8,128)(2,1)}, bf16[256,1152]{1,0:T(8,128)(2,1)S(1)}, u32[]{:S(2)}, u32[]{:S(2)}) collective-permute-start(bf16[256,1152]{1,0:T(8,128)(2,1)} %collective-permute-done.5), channel_id=1, source_target_pairs={{0,8},{8,0},{1,9},{9,1},{2,10},{10,2},{3,11},{11,3},{4,12},{12,4},... | collective-permute-start | bytes 1769480 | tf_op jit(solution)/shard_map/ppermute | solution.py:94
  116.2 25.9 %all-to-all-start.2 = ((bf16[8,72,1152]{2,1,0:T(8,128)(2,1)}), bf16[8,72,1152]{2,1,0:T(8,128)(2,1)}, u32[]{:S(2)}, u32[]{:S(2)}) async-start(bf16[8,72,1152]{2,1,0:T(8,128)(2,1)} %bitcast.9), calls=%async_computation.2 | async-start | bytes 2654208 | tf_op jit(solution)/shard_map/all_to_all | solution.py:50
  123.9 3.0 %copy-start.4 = (bf16[8,2,72,1152]{3,2,1,0:T(8,128)(2,1)S(1)}, bf16[8,2,72,1152]{3,2,1,0:T(8,128)(2,1)}, u32[]{:S(2)}) copy-start(bf16[8,2,72,1152]{3,2,1,0:T(8,128)(2,1)} %copy-done.3) | copy-start | bytes 7962628
  144.4 16.8 %all-to-all-start.3 = ((bf16[32,3,1152]{2,1,0:T(4,128)(2,1)}), bf16[32,3,1152]{2,1,0:T(4,128)(2,1)}, u32[]{:S(2)}, u32[]{:S(2)}) async-start(bf16[32,3,1152]{2,1,0:T(4,128)(2,1)} %reshape.113), calls=%async_computation.3 | async-start | bytes 589824 | tf_op jit(solution)/shard_map/all_to_all | solution.py:50
  163.1 19.3 %all-to-all-start.4 = ((bf16[32,3,1152]{2,1,0:T(4,128)(2,1)}), bf16[32,3,1152]{2,1,0:T(4,128)(2,1)S(1)}, u32[]{:S(2)}, u32[]{:S(2)}) async-start(bf16[32,3,1152]{2,1,0:T(4,128)(2,1)} %broadcast_in_dim.22), calls=%async_computation.4 | async-start | bytes 589824 | tf_op jit(solution)/shard_map/all_to_all | solution.py:50
  170.0 1.1 copy-start.7

commit v3 on v2

--- a/solution.py
+++ b/solution.py
@@ -80,7 +80,10 @@
     text_b = lax.ppermute(text_a, "core", SWAP)
 
     own_half = lax.dynamic_slice_in_dim(head, core * half, half, 0)
-    pair = spread(own_half, "yl", 2)
+    across = lax.ppermute(own_half, "yl", SWAP)
+    pair = jnp.where(
+        lax.axis_index("yl") == 0, jnp.stack([own_half, across]), jnp.stack([across, own_half])
+    )
     halves = spread(pair, "x", 4)
     other = lax.ppermute(halves, "core", SWAP)
     halves, other = halves.reshape(8, half, width), other.reshape(8, half, width)
@@ -89,8 +92,9 @@
     ).reshape(width, width)
 
     image_p = lax.ppermute(images, "core", SWAP)
-    image_a = lax.ppermute(images, DP, by_chip(-1))
-    image_c = lax.ppermute(images, DP, AHEAD)
+    later = images + text_a[0, 0] * 0
+    image_a = lax.ppermute(later, DP, by_chip(-1))
+    image_c = lax.ppermute(later, DP, AHEAD)
     image_b = lax.ppermute(image_a, "core", SWAP)
 
     place_of = jnp.arange(width // 2, dtype=jnp.int32)

time: 192 us -> 212 us (1.10)
  waiting for transfers between devices: 43.3 us -> 64.4 us
  blocking collectives: 14.5 us -> 6.73 us
  starting transfers between devices: 72.5 us -> 77.6 us
    ppermute x2 -> x3, starting transfers between devices: 24.1 us -> 11 us  [the longest x1 4.49 us: per_device(): image_a = lax.ppermute(later, DP, by_chip(-1))]
    ppermute x1, waiting for transfers between devices: 9.2 us -> 20.8 us  [per_device(): text_a = lax.ppermute(texts, DP, by_chip(1))]
    all_to_all x4, starting transfers between devices: 24 us -> 34.8 us  [exchange(): return lax.all_to_all(array, axes, split_axis=0, concat_axis=0, tiled=True)]
    all_to_all x2 -> x1, blocking collectives: 14.5 us -> 6.73 us  [exchange(): return lax.all_to_all(array, axes, split_axis=0, concat_axis=0, tiled=True)]
    ppermute x1, starting transfers between devices: 1.92 us -> 9.43 us  [per_device(): image_b = lax.ppermute(image_a, 'core', SWAP)]
    ppermute x1, waiting for transfers between devices: 14.8 us -> 20.7 us  [per_device(): text_c = lax.ppermute(far, ALL, FAR_SECOND)]
    ppermute x2 -> x3, waiting for transfers between devices: 0.01 us -> 2.68 us  [the longest x1 2.68 us: per_device(): across = lax.ppermute(own_half, 'yl', SWAP)]
    ppermute x1, starting transfers between devices: 1.92 us -> 4.21 us  [per_device(): text_a = lax.ppermute(texts, DP, by_chip(1))]
  transfers between devices with their start and end apart: 14 -> 15, of which waited for: 5 -> 6; matrix products, arithmetic and copies ran while one was open for 26% -> 24% of each run, Pallas kernels for 0% -> 0%
where the time goes in v3:
time: 212 us; the launch traced here: 211 us
  starting transfers between devices  77.6 us (37%)
  waiting for transfers between devices  64.4 us (30%)
  matrix products  43.2 us (20%)
  other arithmetic  11 us (5%)
  blocking collectives  6.73 us (3%)
  local copies, waits for them, and re-layouts  4.59 us (2%)
  between operations  3.62 us (2%)
    dot_general x17, matrix products, dot(): lax.dot_general(a, b, (((ca,), (cb,)), ((), ())), preferred_element_type=...  43.2 us
    all_to_all x4, starting transfers between devices, exchange(): return lax.all_to_all(array, axes, split_axis=0, concat_axis=0, tiled=True)  34.8 us
    ppermute x1, waiting for transfers between devices, per_device(): text_a = lax.ppermute(texts, DP, by_chip(1))  20.8 us
    ppermute x1, waiting for transfers between devices, per_device(): text_c = lax.ppermute(far, ALL, FAR_SECOND)  20.7 us
    all_to_all x4, waiting for transfers between devices, exchange(): return lax.all_to_all(array, axes, split_axis=0, concat_axis=0, tiled=True)  20.2 us
    ppermute x1, starting transfers between devices, per_device(): image_b = lax.ppermute(image_a, 'core', SWAP)  9.43 us
    all_to_all x1, blocking collectives, exchange(): return lax.all_to_all(array, axes, split_axis=0, concat_axis=0, tiled=True)  6.73 us
    ppermute x1, starting transfers between devices, per_device(): far = lax.ppermute(texts, ALL, FAR_FIRST)  5.1 us
  transfers between devices with their start and end apart: 15, of which 6 were waited for; matrix products, arithmetic and copies ran while one was open for 24% of the time, Pallas kernels for 0%

profile of v3, /device:TPU:1, one launch (start us, length us, event | category | flops | bytes accessed | tf_op | source)
XLA Modules:
  0.0 211.1 jit_solution(17637962944636382197)
XLA Ops:
  1.6 4.0 %collective-permute-start = (bf16[72,1152]{1,0:T(8,128)(2,1)S(1)}, bf16[72,1152]{1,0:T(8,128)(2,1)S(1)}, u32[]{:S(2)}, u32[]{:S(2)}) collective-permute-start(bf16[72,1152]{1,0:T(8,128)(2,1)S(1)} %constant_dynamic-slice_fusion), channel_id=1, source_target_pairs={{0,1},{1,0},{2,3},{3,2},{4,5},{5,4},{6,7},{7,6},{8,9},{9,8},{10,11... | collective-permute-start | bytes 497672 | tf_op jit(solution)/shard_map/ppermute | solution.py:83
  5.7 2.7 %collective-permute-done = bf16[72,1152]{1,0:T(8,128)(2,1)S(1)} collective-permute-done((bf16[72,1152]{1,0:T(8,128)(2,1)S(1)}, bf16[72,1152]{1,0:T(8,128)(2,1)S(1)}, u32[]{:S(2)}, u32[]{:S(2)}) %collective-permute-start) | collective-permute-done | bytes 165920 | tf_op jit(solution)/shard_map/ppermute | solution.py:83
  9.7 5.2 %all-to-all-start = ((bf16[4,2,72,1152]{3,2,1,0:T(8,128)(2,1)}), bf16[4,2,72,1152]{3,2,1,0:T(8,128)(2,1)S(1)}, u32[]{:S(2)}, u32[]{:S(2)}) async-start(bf16[4,2,72,1152]{3,2,1,0:T(8,128)(2,1)} %broadcast_in_dim.18), calls=%async_computation | async-start | bytes 2654208 | tf_op jit(solution)/shard_map/all_to_all | solution.py:50
  14.9 4.2 %collective-permute-start.2 = (bf16[256,1152]{1,0:T(8,128)(2,1)S(1)}, bf16[256,1152]{1,0:T(8,128)(2,1)S(1)}, u32[]{:S(2)}, u32[]{:S(2)}) collective-permute-start(bf16[256,1152]{1,0:T(8,128)(2,1)S(1)} %copy-done.1), channel_id=1, source_target_pairs={{0,16},{8,24},{16,32},{24,40},{32,48},{40,56},{48,64},{56,72},{64,... | collective-permute-start | bytes 1769480 | tf_op jit(solution)/shard_map/ppermute | solution.py:78
  19.1 5.1 %collective-permute-start.4 = (bf16[256,1152]{1,0:T(8,128)(2,1)S(1)}, bf16[256,1152]{1,0:T(8,128)(2,1)}, u32[]{:S(2)}, u32[]{:S(2)}) collective-permute-start(bf16[256,1152]{1,0:T(8,128)(2,1)S(1)} %copy-done.1), channel_id=1, source_target_pairs={{0,0},{1,1},{2,2},{3,3},{4,4},{5,5},{6,6},{7,7},{8,57},{9,8},{10,5... | collective-permute-start | bytes 1769480 | tf_op jit(solution)/shard_map/ppermute | solution.py:77
  28.3 20.8 %collective-permute-done.2 = bf16[256,1152]{1,0:T(8,128)(2,1)S(1)} collective-permute-done((bf16[256,1152]{1,0:T(8,128)(2,1)S(1)}, bf16[256,1152]{1,0:T(8,128)(2,1)S(1)}, u32[]{:S(2)}, u32[]{:S(2)}) %collective-permute-start.2) | collective-permute-done | bytes 589856 | tf_op jit(solution)/shard_map/ppermute | solution.py:78
  50.3 5.0 %collective-permute-start.3 = (bf16[256,1152]{1,0:T(8,128)(2,1)S(1)}, bf16[256,1152]{1,0:T(8,128)(2,1)}, u32[]{:S(2)}, u32[]{:S(2)}) collective-permute-start(bf16[256,1152]{1,0:T(8,128)(2,1)S(1)} %collective-permute-done.2), channel_id=1, source_target_pairs={{0,8},{8,0},{1,9},{9,1},{2,10},{10,2},{3,11},{11,3},{4,12},{12,4},... | collective-permute-start | bytes 1769480 | tf_op jit(solution)/shard_map/ppermute | solution.py:80
  57.2 2.4 %collective-permute-start.1 = (bf16[4,2,72,1152]{3,2,1,0:T(8,128)(2,1)S(1)}, bf16[4,2,72,1152]{3,2,1,0:T(8,128)(2,1)S(1)}, u32[]{:S(2)}, u32[]{:S(2)}) collective-permute-start(bf16[4,2,72,1152]{3,2,1,0:T(8,128)(2,1)S(1)} %all-to-all-done), channel_id=1, source_target_pairs={{0,8},{8,0},{1,9},{9,1},{2,10},{10,2},{3,11},{11,3},{4,12},{12,4},... | collective-permute-start | bytes 3981320 | tf_op jit(solution)/shard_map/ppermute | solution.py:88
  59.6 1.9 broadcast_add_fusion
  61.5 4.5 %collective-permute-start.6 = (bf16[256,1152]{1,0:T(8,128)(2,1)}, bf16[256,1152]{1,0:T(8,128)(2,1)}, u32[]{:S(2)}, u32[]{:S(2)}) collective-permute-start(bf16[256,1152]{1,0:T(8,128)(2,1)} %broadcast_add_fusion), channel_id=1, source_target_pairs={{0,496},{8,504},{16,0},{24,8},{32,16},{40,24},{48,32},{56,40},{64,... | collective-permute-start | bytes 1769480 | tf_op jit(solution)/shard_map/ppermute | solution.py:96
  66.2 20.7 %collective-permute-done.5 = bf16[256,1152]{1,0:T(8,128)(2,1)S(1)} collective-permute-done((bf16[256,1152]{1,0:T(8,128)(2,1)}, bf16[256,1152]{1,0:T(8,128)(2,1)S(1)}, u32[]{:S(2)}, u32[]{:S(2)}) %collective-permute-start.5) | collective-permute-done | bytes 589856 | tf_op jit(solution)/shard_map/ppermute | solution.py:79
  89.2 2.5 %multiply_reduce_fusion.3 = (f32[256]{0:T(256)S(1)}, f32[1152,256]{1,0:T(8,128)S(1)}) fusion(bf16[1152,1152]{1,0:T(8,128)(2,1)S(1)} %bitcast.65, bf16[256,1152]{1,0:T(8,128)(2,1)} %param.6), kind=kOutput, calls=%fused_computation.55 | convolution fusion | flops 680066816 | bytes 4424704 | tf_op jit(solution)/shard_map/dot_general | solution.py:15
  93.9 3.4 %fusion.92 = f32[256,1152]{0,1:T(8,128)} fusion(bf16[256,1152]{0,1:T(8,128)(2,1)S(1)} %bitcast_convert_fusion, bf16[256,1152]{1,0:T(8,128)(2,1)} %copy-done.4, f32[256]{0:T(256)S(1)} %add_rsqrt_fusion.3, f32[]{:T(128)} %bitcast.60, f32[]{:T(128)} %bitcast.49), kind=kOutput, calls=%fused_computation.116 | convolution fusion | flops 304218112 | bytes 2360328 | tf_op jit(solution)/shard_map/dot_general | solution.py:15
  97.3 3.3 %convolution_add_fusion.4 = f32[256,1152]{0,1:T(8,128)} fusion(f32[256,1152]{0,1:T(8,128)} %fusion.156, bf16[256,1152]{0,1:T(8,128)(2,1)S(1)} %bitcast_convert_fusion, bf16[256,1152]{1,0:T(8,128)(2,1)S(1)} %collective-permute-done.2, f32[256]{0:T(256)S(1)} %add_rsqrt_fusion.5, f32[]{:T(128)} %bitcast.62, f32[]{:T(128)} %bitcast.53), kind=kOutput, calls=%fused_computation.7 | convolution fusion | flops 304513024 | bytes 3539976 | tf_op jit(solution)/shard_map/dot_general | solution.py:15
  100.6 4.1 %fusion.31 = (f32[256]{0:T(256)S(1)}, f32[256,1152]{0,1:T(8,128)}) fusion(f32[1152,256]{1,0:T(8,128)S(1)} %get-tuple-element.4, f32[256]{0:T(256)S(1)} %add_rsqrt_fusion.7, f32[256,1152]{0,1:T(8,128)} %fusion.92, f32[256,1152]{0,1:T(8,128)} %convolution_add_fusion.4, bf16[256,1152]{1,0:T(8,128)(2,1)} %collective-permute-done.3, ...), kind=kOutput, calls=%fused_computation.45 | convolution fusion | flops 305692416 | bytes 5901320 | tf_op jit(solution)/shard_map/dot_general | solution.py:15
  109.9 2.4 %collective-permute-start.8 = (bf16[256,1152]{1,0:T(8,128)(2,1)}, bf16[256,1152]{1,0:T(8,128)(2,1)}, u32[]{:S(2)}, u32[]{:S(2)}) collective-permute-start(bf16[256,1152]{1,0:T(8,128)(2,1)} %broadcast_add_fusion), channel_id=1, source_target_pairs={{8,0},{32,8},{24,16},{48,24},{40,32},{64,40},{56,48},{80,56},{72,6... | collective-permute-start | bytes 1769480 | tf_op jit(solution)/shard_map/ppermute | solution.py:97
  112.3 9.4 %collective-permute-start.7 = (bf16[256,1152]{1,0:T(8,128)(2,1)}, bf16[256,1152]{1,0:T(8,128)(2,1)S(1)}, u32[]{:S(2)}, u32[]{:S(2)}) collective-permute-start(bf16[256,1152]{1,0:T(8,128)(2,1)} %collective-permute-done.6), channel_id=1, source_target_pairs={{0,8},{8,0},{1,9},{9,1},{2,10},{10,2},{3,11},{11,3},{4,12},{12,4},... | collective-permute-start | bytes 1769480 | tf_op jit(solution)/shard_map/ppermute | solution.py:98
  123.5 2.0 convolution_convert_fusion
  125.5 7.1 %all-to-all-start.1 = ((bf16[8,72,1152]{2,1,0:T(8,128)(2,1)}), bf16[8,72,1152]{2,1,0:T(8,128)(2,1)}, u32[]{:S(2)}, u32[]{:S(2)}) async-start(bf16[8,72,1152]{2,1,0:T(8,128)(2,1)} %bitcast.12), calls=%async_computation.1 | async-start | bytes 2654208 | tf_op jit(solution)/shard_map/all_to_all | solution.py:50
  132.7 3.2 %multiply_reduce_fusion.2 = (f32[256]{0:T(256)S(1)}, f32[256,1152]{1,0:T(8,128)S(1)}) fusion(bf16[256,1152]{1,0:T(8,128)(2,1)} %collective-permute-done.6, bf16[1152,1152]{1,0:T(8,128)(2,1)} %bitcast.66), kind=kOutput, calls=%fused_computation.54 | convolution fusion | flops 680066816 | bytes 4424704 | tf_op jit(solution)/shard_map/dot_general | solution.py:15
  135.8 2.0 multiply_reduce_fusion.1
  139.3 2.1 %multiply_reduce_fusion = (f32[256]{0:T(256)S(1)}, f32[256,1152]{1,0:T(8,128)S(1)}) fusion(bf16[256,1152]{1,0:T(8,128)(2,1)} %collective-permute-done.8, bf16[1152,1152]{1,0:T(8,128)(2,1)S(1)} %bitcast.69), kind=kOutput, calls=%fused_computation.50 | convolution fusion | flops 680066816 | bytes 4424704 | tf_op jit(solution)/shard_map/dot_general | solution.py:15
  141.5 3.4 %convolution_add_fusion.2 = f32[256,1152]{1,0:T(8,128)} fusion(f32[256,1152]{1,0:T(8,128)} %fusion.163, f32[256,1152]{1,0:T(8,128)S(1)} %get-tuple-element.8, f32[256]{0:T(256)S(1)} %add_rsqrt_fusion.2, f32[]{:T(128)} %bitcast.59, f32[]{:T(128)} %bitcast.52, bf16[256,1152]{1,0:T(8,128)(2,1)S(1)} %copy-done.1, f32[256]{0:T(256)S(1)} %add_rsqrt_fusion.6), kind=kOutput, calls=%fused_computation.5 | convolution fusion | flops 304807936 | bytes 4130824 | tf_op jit(solution)/shard_map/dot_general | solution.py:15
  144.9 4.2 %convolution_add_fusion.1 = f32[256,1152]{1,0:T(8,128)} fusion(f32[256,1152]{1,0:T(8,128)} %convolution_add_fusion.2, f32[256,1152]{1,0:T(8,128)} %get-tuple-element.10, f32[256]{0:T(256)S(1)} %add_rsqrt_fusion.1, f32[]{:T(128)} %bitcast.58, f32[]{:T(128)} %bitcast.54, bf16[256,1152]{1,0:T(8,128)(2,1)S(1)} %copy-done.1, f32[256]{0:T(256)S(1)} %add_rsqrt_fusion.6), kind=kOutput, calls=%fused_computation.4 | convolution fusion | flops 304807936 | bytes 4130824 | tf_op jit(solution)/shard_map/dot_general | solution.py:15
  149.1 2.3 %all-to-all-done.1 = bf16[8,72,1152]{2,1,0:T(8,128)(2,1)} async-done(((bf16[8,72,1152]{2,1,0:T(8,128)(2,1)}), bf16[8,72,1152]{2,1,0:T(8,128)(2,1)}, u32[]{:S(2)}, u32[]{:S(2)}) %all-to-all-start.1) | async-done | bytes 1327136 | tf_op jit(solution)/shard_map/all_to_all | solution.py:50
  153.7 16.6 %all-to-all-start.2 = ((bf16[32,3,1152]{2,1,0:T(4,128)(2,1)}), bf16[32,3,1152]{2,1,0:T(4,128)(2,1)}, u32[]{:S(2)}, u32[]{:S(2)}) async-start(bf16[32,3,1152]{2,1,0:T(4,128)(2,1)} %reshape.146), calls=%async_computation.2 | async-start | bytes 589824 | tf_op jit(solution)/shard_map/all_to_all | solution.py:50
  170.3 2.5 %fusion.17 = (f32[256]{0:T(256)S(1)}, f32[256,1152]{1,0:T(8,128)S(1)}) fusion(bf16[256,1152]{1,0:T(8,128)(2,1)S(1)} %copy-done.1, f32[256]{0:T(256)S(1)} %add_rsqrt_fusion.6, f32[256,1152]{1,0:T(8,128)} %convolution_add_fusion.1, f32[256,1152]{1,0:T(8,128)S(1)} %get-tuple-element.12, f32[256]{0:T(256)S(1)} %add_rsqrt_fusion, f32[]{:T(128)} %bitcast.57, ...), kind=kOutput, calls=%fused_computation.28 | convolution fusion | flops 305987328 | bytes 4131848 | tf_op jit(solution)/shard_map/dot_general | solution.py:15
  172.8 9.9 %all-to-all-done.2 = bf16[32,3,1152]{2,1,0:T(4,128)(2,1)} async-done(((bf16[32,3,1152]{2,1,0:T(4,128)(2,1)}), bf16[32,3,1152]{2,1,0:T(4,128)(2,1)}, u32[]{:S(2)}, u32[]{:S(2)}) %all-to-all-start.2) | async-done | bytes 221216 | tf_op jit(solution)/shard_map/all_to_all | solution.py:50
  184.5 5.9 %all-to-all-start.3 = ((bf16[32,3,1152]{2,1,0:T(4,128)(2,1)}), bf16[32,3,1152]{2,1,0:T(4,128)(2,1)S(1)}, u32[]{:S(2)}, u32[]{:S(2)}) async-start(bf16[32,3,1152]{2,1,0:T(4,128)(2,1)} %broadcast_in_dim.19), calls=%async_computation.3 | async-start | bytes 589824 | tf_op jit(solution)/shard_map/all_to_all | solution.py:50
  191.5 3.6 %convolution_convert_fusion.1 = bf16[256,1152]{1,0:T(8,128)(2,1)} fusion(bf16[256,1152]{0,1:T(8,128)(2,1)S(1)} %copy-done.6, bf16[1152,1152]{1,0:T(8,128)(2,1)} %bitcast.67), kind=kOutput, calls=%fused_computation.10 | convolution fusion | flops 679772160 | bytes 3833856 | tf_op jit(solution)/shard_map/dot_general | solution.py:15
  195.2 8.1 %all-to-all-done.3 = bf16[32,3,1152]{2,1,0:T(4,128)(2,1)S(1)} async-done(((bf16[32,3,1152]{2,1,0:T(4,128)(2,1)}), bf16[32,3,1152]{2,1,0:T(4,128)(2,1)S(1)}, u32[]{:S(2)}, u32[]{:S(2)}) %all-to-all-start.3) | async-done | bytes 221216 | tf_op jit(solution)/shard_map/all_to_all | solution.py:50
  203.5 6.7 %all_to_all.25 = bf16[2,72,1152]{2,1,0:T(8,128)(2,1)S(1)} all-to-all(bf16[2,72,1152]{2,1,0:T(8,128)(2,1)S(1)} %broadcast_in_dim.21), channel_id=1, replica_groups=mesh['z'=8,'yh'=4,'core'=2,'x'=4,'yl'=2] {'core'}, dimensions={0} | all-to-all | bytes 663552 | tf_op jit(solution)/shard_map/all_to_all | solution.py:50
  (63 shorter events, 26.3 us)
Async XLA Ops:
  0.6 1.0 copy-start
  1.6 6.8 %collective-permute-start = (bf16[72,1152]{1,0:T(8,128)(2,1)S(1)}, bf16[72,1152]{1,0:T(8,128)(2,1)S(1)}, u32[]{:S(2)}, u32[]{:S(2)}) collective-permute-start(bf16[72,1152]{1,0:T(8,128)(2,1)S(1)} %constant_dynamic-slice_fusion), channel_id=1, source_target_pairs={{0,1},{1,0},{2,3},{3,2},{4,5},{5,4},{6,7},{7,6},{8,9},{9,8},{10,11... | collective-permute-start | bytes 497672 | tf_op jit(solution)/shard_map/ppermute | solution.py:83
  9.7 5.2 %copy-start.1 = (bf16[256,1152]{1,0:T(8,128)(2,1)S(1)}, bf16[256,1152]{1,0:T(8,128)(2,1)}, u32[]{:S(2)}) copy-start(bf16[256,1152]{1,0:T(8,128)(2,1)} %param.7) | copy-start | bytes 1769476
  9.7 47.5 %all-to-all-start = ((bf16[4,2,72,1152]{3,2,1,0:T(8,128)(2,1)}), bf16[4,2,72,1152]{3,2,1,0:T(8,128)(2,1)S(1)}, u32[]{:S(2)}, u32[]{:S(2)}) async-start(bf16[4,2,72,1152]{3,2,1,0:T(8,128)(2,1)} %broadcast_in_dim.18), calls=%async_computation | async-start | bytes 2654208 | tf_op jit(solution)/shard_map/all_to_all | solution.py:50
  14.9 34.2 %collective-permute-start.2 = (bf16[256,1152]{1,0:T(8,128)(2,1)S(1)}, bf16[256,1152]{1,0:T(8,128)(2,1)S(1)}, u32[]{:S(2)}, u32[]{:S(2)}) collective-permute-start(bf16[256,1152]{1,0:T(8,128)(2,1)S(1)} %copy-done.1), channel_id=1, source_target_pairs={{0,16},{8,24},{16,32},{24,40},{32,48},{40,56},{48,64},{56,72},{64,... | collective-permute-start | bytes 1769480 | tf_op jit(solution)/shard_map/ppermute | solution.py:78
  19.1 36.1 %collective-permute-start.4 = (bf16[256,1152]{1,0:T(8,128)(2,1)S(1)}, bf16[256,1152]{1,0:T(8,128)(2,1)}, u32[]{:S(2)}, u32[]{:S(2)}) collective-permute-start(bf16[256,1152]{1,0:T(8,128)(2,1)S(1)} %copy-done.1), channel_id=1, source_target_pairs={{0,0},{1,1},{2,2},{3,3},{4,4},{5,5},{6,6},{7,7},{8,57},{9,8},{10,5... | collective-permute-start | bytes 1769480 | tf_op jit(solution)/shard_map/ppermute | solution.py:77
  24.2 97.5 %collective-permute-start.9 = (bf16[256,1152]{1,0:T(8,128)(2,1)}, bf16[256,1152]{1,0:T(8,128)(2,1)}, u32[]{:S(2)}, u32[]{:S(2)}) collective-permute-start(bf16[256,1152]{1,0:T(8,128)(2,1)} %param.6), channel_id=1, source_target_pairs={{0,8},{8,0},{1,9},{9,1},{2,10},{10,2},{3,11},{11,3},{4,12},{12,4},... | collective-permute-start | bytes 1769480 | tf_op jit(solution)/shard_map/ppermute | solution.py:94
  50.3 36.8 %collective-permute-start.3 = (bf16[256,1152]{1,0:T(8,128)(2,1)S(1)}, bf16[256,1152]{1,0:T(8,128)(2,1)}, u32[]{:S(2)}, u32[]{:S(2)}) collective-permute-start(bf16[256,1152]{1,0:T(8,128)(2,1)S(1)} %collective-permute-done.2), channel_id=1, source_target_pairs={{0,8},{8,0},{1,9},{9,1},{2,10},{10,2},{3,11},{11,3},{4,12},{12,4},... | collective-permute-start | bytes 1769480 | tf_op jit(solution)/shard_map/ppermute | solution.py:80
  55.2 31.7 %collective-permute-start.5 = (bf16[256,1152]{1,0:T(8,128)(2,1)}, bf16[256,1152]{1,0:T(8,128)(2,1)S(1)}, u32[]{:S(2)}, u32[]{:S(2)}) collective-permute-start(bf16[256,1152]{1,0:T(8,128)(2,1)} %collective-permute-done.4), channel_id=1, source_target_pairs={{0,8},{1,9},{2,10},{3,11},{4,12},{5,13},{6,14},{7,15},{8,33},{9,48... | collective-permute-start | bytes 1769480 | tf_op jit(solution)/shard_map/ppermute | solution.py:79
  57.2 31.2 %collective-permute-start.1 = (bf16[4,2,72,1152]{3,2,1,0:T(8,128)(2,1)S(1)}, bf16[4,2,72,1152]{3,2,1,0:T(8,128)(2,1)S(1)}, u32[]{:S(2)}, u32[]{:S(2)}) collective-permute-start(bf16[4,2,72,1152]{3,2,1,0:T(8,128)(2,1)S(1)} %all-to-all-done), channel_id=1, source_target_pairs={{0,8},{8,0},{1,9},{9,1},{2,10},{10,2},{3,11},{11,3},{4,12},{12,4},... | collective-permute-start | bytes 3981320 | tf_op jit(solution)/shard_map/ppermute | solution.py:88
  61.5 50.8 %collective-permute-start.6 = (bf16[256,1152]{1,0:T(8,128)(2,1)}, bf16[256,1152]{1,0:T(8,128)(2,1)}, u32[]{:S(2)}, u32[]{:S(2)}) collective-permute-start(bf16[256,1152]{1,0:T(8,128)(2,1)} %broadcast_add_fusion), channel_id=1, source_target_pairs={{0,496},{8,504},{16,0},{24,8},{32,16},{40,24},{48,32},{56,40},{64,... | collective-permute-start | bytes 1769480 | tf_op jit(solution)/shard_map/ppermute | solution.py:96
  86.9 2.3 %copy-start.4 = (bf16[256,1152]{1,0:T(8,128)(2,1)}, bf16[256,1152]{1,0:T(8,128)(2,1)S(1)}, u32[]{:S(2)}) copy-start(bf16[256,1152]{1,0:T(8,128)(2,1)S(1)} %collective-permute-done.5) | copy-start | bytes 1769476
  89.2 2.5 %copy-start.2 = (bf16[8,2,72,1152]{3,2,1,0:T(8,128)(2,1)}, bf16[8,2,72,1152]{3,2,1,0:T(8,128)(2,1)S(1)}, u32[]{:S(2)}) copy-start(bf16[8,2,72,1152]{3,2,1,0:T(8,128)(2,1)S(1)} %maximum_select_fusion) | copy-start | bytes 7962628
  106.2 17.3 %copy-start.5 = (bf16[256,1152]{0,1:T(8,128)(2,1)}, bf16[256,1152]{0,1:T(8,128)(2,1)S(1)}, u32[]{:S(2)}) copy-start(bf16[256,1152]{0,1:T(8,128)(2,1)S(1)} %fusion.34) | copy-start | bytes 1769476
  106.2 17.3 %collective-permute-start.10 = (bf16[256,1152]{0,1:T(8,128)(2,1)S(1)}, bf16[256,1152]{0,1:T(8,128)(2,1)S(1)}, u32[]{:S(2)}, u32[]{:S(2)}) collective-permute-start(bf16[256,1152]{0,1:T(8,128)(2,1)S(1)} %fusion.34), channel_id=1, source_target_pairs={{0,8},{8,0},{1,9},{9,1},{2,10},{10,2},{3,11},{11,3},{4,12},{12,4},... | collective-permute-start | bytes 1769480 | tf_op jit(solution)/shard_map/ppermute | solution.py:123
  109.9 29.5 %collective-permute-start.8 = (bf16[256,1152]{1,0:T(8,128)(2,1)}, bf16[256,1152]{1,0:T(8,128)(2,1)}, u32[]{:S(2)}, u32[]{:S(2)}) collective-permute-start(bf16[256,1152]{1,0:T(8,128)(2,1)} %broadcast_add_fusion), channel_id=1, source_target_pairs={{8,0},{32,8},{24,16},{48,24},{40,32},{64,40},{56,48},{80,56},{72,6... | collective-permute-start | bytes 1769480 | tf_op jit(solution)/shard_map/ppermute | solution.py:97
  112.3 23.5 %collective-permute-start.7 = (bf16[256,1152]{1,0:T(8,128)(2,1)}, bf16[256,1152]{1,0:T(8,128)(2,1)S(1)}, u32[]{:S(2)}, u32[]{:S(2)}) collective-permute-start(bf16[256,1152]{1,0:T(8,128)(2,1)} %collective-permute-done.6), channel_id=1, source_target_pairs={{0,8},{8,0},{1,9},{9,1},{2,10},{10,2},{3,11},{11,3},{4,12},{12,4},... | collective-permute-start | bytes 1769480 | tf_op jit(solution)/shard_map/ppermute | solution.py:98
  125.5 25.8 %all-to-all-start.1 = ((bf16[8,72,1152]{2,1,0:T(8,128)(2,1)}), bf16[8,72,1152]{2,1,0:T(8,128)(2,1)}, u32[]{:S(2)}, u32[]{:S(2)}) async-start(bf16[8,72,1152]{2,1,0:T(8,128)(2,1)} %bitcast.12), calls=%async_computation.1 | async-start | bytes 2654208 | tf_op jit(solution)/shard_map/all_to_all | solution.py:50
  132.7 3.2 %copy-start.3 = (bf16[8,2,72,1152]{3,2,1,0:T(8,128)(2,1)S(1)}, bf16[8,2,72,1152]{3,2,1,0:T(8,128)(2,1)}, u32[]{:S(2)}) copy-start(bf16[8,2,72,1152]{3,2,1,0:T(8,128)(2,1)} %copy-done.2) | copy-start | bytes 7962628
  153.7 28.9 %all-to-all-start.2 = ((bf16[32,3,1152]{2,1,0:T(4,128)(2,1)}), bf16[32,3,1152]{2,1,0:T(4,128)(2,1)}, u32[]{:S(2)}, u32[]{:S(2)}) async-start(bf16[32,3,1152]{2,1,0:T(4,128)(2,1)} %reshape.146), calls=%async_computation.2 | async-start | bytes 589824 | tf_op jit(solution)/shard_map/all_to_all | solution.py:50
  184.5 18.7 %all-to-all-start.3 = ((bf16[32,3,1152]{2,1,0:T(4,128)(2,1)}), bf16[32,3,1152]{2,1,0:T(4,128)(2,1)S(1)}, u32[]{:S(2)}, u32[]{:S(2)}) async-start(bf16[32,3,1152]{2,1,0:T(4,128)(2,1)} %broadcast_in_dim.19), calls=%async_computation.3 | async-start | bytes 589824 | tf_op jit(solution)/shard_map/all_to_all | solution.py:50
  190.4 1.1 copy-start.6

commit v4 on v1

v4 whole, which is shorter than its diff:
```python
import jax
import jax.numpy as jnp
from jax import lax
from jax.experimental import pallas as pl
from jax.experimental.pallas import tpu as pltpu
from jax.sharding import Mesh
from jax.sharding import PartitionSpec as P

EPS = 1e-06
CHAIN = 20_000_000_000
DP = ("z", "yh", "core")
RING = ("z", "yh")
REP = ("x", "yl")
ALL = DP + REP


def dot(a, b, ca, cb):
    return lax.dot_general(a, b, (((ca,), (cb,)), ((), ())), preferred_element_type=jnp.float32)


def by_chip(shift):
    return [(p, (p + 2 * shift) % 64) for p in range(64)]


SWAP = [(0, 1), (1, 0)]
ON = [(p, (p + 1) % 64) for p in range(64)]
BACK = [(b, a) for a, b in ON]


def exchange(array, axes):
    return lax.all_to_all(array, axes, split_axis=0, concat_axis=0, tiled=True)


def spread(array, axes, count):
    return exchange(jnp.broadcast_to(array[None], (count,) + array.shape), axes)


def unit_rows(values):
    inverse = lax.rsqrt(jnp.sum(values * values, axis=-1, keepdims=True) + EPS)
    return values * inverse, inverse


def off_unit(direction, unit, inverse):
    return (direction - unit * jnp.sum(unit * direction, axis=-1, keepdims=True)) * inverse


def narrow(values):
    return values.astype(jnp.bfloat16)


def rounded_unit(block):
    return narrow(unit_rows(block.astype(jnp.float32))[0])


def negatives(a, b, numbers):
    logits = numbers[0] * dot(a, b, 1, 1) + numbers[1]
    return narrow(numbers[0] * jax.nn.sigmoid(logits))


def own_pairs(a, b, numbers, positive):
    logits = numbers[0] * dot(a, b, 1, 1) + numbers[1]
    sign = jnp.where(positive, jnp.float32(1.0), jnp.float32(-1.0))
    return narrow(numbers[0] * (-sign * jax.nn.sigmoid(-sign * logits)))


def positives(offset, rows, image_dim):
    image = lax.broadcasted_iota(jnp.int32, (rows, rows), image_dim)
    text = lax.broadcasted_iota(jnp.int32, (rows, rows), 1 - image_dim)
    target = image + offset
    return text == jnp.where(target >= rows, target - rows, target)


def image_kernel(numbers, offset, images, head, texts, text_a, text_b, here, unit, inverse, img_b, partial):
    proj = dot(images[...], head[...], 1, 0)
    unit_value, inverse_value = unit_rows(proj)
    unit[...] = unit_value
    inverse[...] = jnp.broadcast_to(inverse_value, inverse.shape)
    rounded = narrow(unit_value)
    img_b[...] = rounded
    block = rounded_unit(texts[...])
    weights = own_pairs(rounded, block, numbers, positives(offset[0], block.shape[0], 0))
    total = dot(weights, block, 1, 0)
    for other in (text_a, text_b):
        block = rounded_unit(other[...])
        total = total + dot(negatives(rounded, block, numbers), block, 1, 0)
    partial[...] = total


def last_kernel(numbers, text_c, unit, inverse, img_b, partial, here, picked, proj_grad):
    block = rounded_unit(text_c[...])
    total = partial[...] + dot(negatives(img_b[...], block, numbers), block, 1, 0)
    proj_grad[...] = narrow(off_unit(total, unit[...], inverse[:, :1]))


def text_kernel(numbers, offset, texts, img_b, head, image_a, image_b, image_c, text_grad):
    unit, inverse = unit_rows(texts[...].astype(jnp.float32))
    txt_b = narrow(unit)
    own = img_b[...]
    weights = own_pairs(txt_b, own, numbers, positives(offset[0], own.shape[0], 1))
    total = dot(weights, own, 1, 0)
    for other in (image_a, image_b, image_c):
        block = narrow(unit_rows(dot(other[...], head[...], 1, 0))[0])
        total = total + dot(negatives(txt_b, block, numbers), block, 1, 0)
    text_grad[...] = narrow(off_unit(total, unit, inverse))


def choose_kernel(which, first, second, out):
    out[...] = jnp.where(which[0] == 0, first[...], second[...])


def pick_kernel(core, images, image_p, picked):
    half, width = picked.shape[0] // 8, images.shape[1]
    row = lax.broadcasted_iota(jnp.int32, (picked.shape[0], width), 0)
    column = lax.broadcasted_iota(jnp.int32, (picked.shape[0], width), 1)
    wanted = row + (row // half + core[0]) * half
    pick = jnp.where(column == wanted, jnp.float32(1.0), jnp.float32(0.0)).astype(jnp.bfloat16)
    count = images.shape[0]
    picked[:, :count] = narrow(dot(pick, images[...], 1, 1))
    picked[:, count:] = narrow(dot(pick, image_p[...], 1, 1))


def term_kernel(picked, grad, grad_p, out):
    count, half = grad.shape[0], out.shape[1]
    term = dot(picked[:, :count], grad[...], 1, 0) + dot(picked[:, count:], grad_p[...], 1, 0)
    for index in range(out.shape[0]):
        out[index] = narrow(term[index * half : (index + 1) * half])


def group_kernel(term, here, out):
    total = term[0].astype(jnp.float32)
    for index in range(1, term.shape[0]):
        total = total + term[index].astype(jnp.float32)
    rows, third = out.shape[1:]
    groups = total.shape[0] // rows
    for group in range(groups):
        for part in range(3):
            piece = total[group * rows : (group + 1) * rows, part * third : (part + 1) * third]
            out[group * 3 + part] = narrow(piece)
    for index in range(groups * 3, out.shape[0]):
        out[index] = jnp.zeros((rows, third), out.dtype)


def copies_kernel(pieces, here, out):
    total = pieces[0].astype(jnp.float32)
    for index in range(1, pieces.shape[0]):
        total = total + pieces[index].astype(jnp.float32)
    for index in range(out.shape[0]):
        out[index] = narrow(total)


def join_kernel(pieces, out):
    rows, third = pieces.shape[1:]
    groups = out.shape[1] // rows
    total = jnp.concatenate(
        [
            jnp.concatenate([pieces[g * 3 + p].astype(jnp.float32) for p in range(3)], 1)
            for g in range(groups)
        ],
        0,
    )
    for index in range(out.shape[0]):
        out[index] = narrow(total)


def call(kernel, scalars, arrays, outs, flops, after=()):
    smem, vmem = pl.BlockSpec(memory_space=pltpu.SMEM), pl.BlockSpec(memory_space=pltpu.VMEM)
    moved = sum(a.size * a.dtype.itemsize for a in list(arrays) + list(outs))
    return pl.pallas_call(
        kernel,
        out_shape=outs if len(outs) > 1 else outs[0],
        in_specs=[smem] * len(scalars) + [vmem] * len(arrays) + [pl.BlockSpec(memory_space=pl.ANY)] * len(after),
        out_specs=[vmem] * len(outs) if len(outs) > 1 else vmem,
        compiler_params=pltpu.CompilerParams(vmem_limit_bytes=40 * 1024 * 1024),
        cost_estimate=pl.CostEstimate(flops=flops, bytes_accessed=moved, transcendentals=0),
    )(*scalars, *arrays, *after)


def per_device(images, texts, head, scale, bias, offsets):
    rows, width = images.shape
    share = head.shape[0]
    half = share // 2
    core = lax.axis_index("core")
    numbers = jnp.concatenate([scale, bias])
    pair_flops = 4 * rows * rows * width
    full_flops = 2 * rows * width * width
    wide = jax.ShapeDtypeStruct((rows, width), jnp.float32)
    slim = jax.ShapeDtypeStruct((rows, width), jnp.bfloat16)

    text_a = lax.ppermute(texts, DP, by_chip(1))
    image_a = lax.ppermute(images, DP, by_chip(-1))
    text_b = lax.ppermute(text_a, "core", SWAP)
    image_b = lax.ppermute(image_a, "core", SWAP)
    mine = lax.convert_element_type(core, jnp.int32).reshape(1)
    text_on = call(choose_kernel, (mine,), (texts, text_a), (slim,), CHAIN)
    image_on = call(choose_kernel, (1 - mine,), (images, image_a), (slim,), CHAIN)
    text_c = lax.ppermute(text_on, DP, ON)
    image_c = lax.ppermute(image_on, DP, BACK)

    own_half = lax.dynamic_slice_in_dim(head, core * half, half, 0)
    across = lax.ppermute(own_half, "yl", SWAP)
    pair = jnp.where(
        lax.axis_index("yl") == 0, jnp.stack([own_half, across]), jnp.stack([across, own_half])
    )
    halves = spread(pair, "x", 4)
    other = lax.ppermute(halves, "core", SWAP)
    halves, other = halves.reshape(8, half, width), other.reshape(8, half, width)
    full_head = jnp.where(
        core == 0, jnp.stack([halves, other], 1), jnp.stack([other, halves], 1)
    ).reshape(width, width)

    image_p = lax.ppermute(images, "core", SWAP)
    picked = call(
        pick_kernel,
        (mine,),
        (images, image_p),
        (jax.ShapeDtypeStruct((width // 2, 2 * rows), jnp.bfloat16),),
        2 * full_flops,
    )
    unit, inverse, img_b, partial = call(
        image_kernel,
        (numbers, offsets),
        (images, full_head, texts, text_a, text_b),
        (wide, jax.ShapeDtypeStruct((rows, 128), jnp.float32), slim, wide),
        full_flops + 3 * pair_flops,
        (image_a,),
    )
    proj_grad = call(
        last_kernel, (numbers,), (text_c, unit, inverse, img_b, partial), (slim,), pair_flops, (image_c, picked)
    )

    grad_p = lax.ppermute(proj_grad, "core", SWAP)
    pieces = jax.ShapeDtypeStruct((32, 8, width // 3), jnp.bfloat16)
    term = call(
        term_kernel,
        (),
        (picked, proj_grad, grad_p),
        (jax.ShapeDtypeStruct((8, half, width), jnp.bfloat16),),
        full_flops,
    )
    term = exchange(term, REP)
    text_grad = call(
        text_kernel,
        (numbers, offsets),
        (texts, img_b, full_head, image_a, image_b, image_c),
        (slim,),
        3 * full_flops + 4 * pair_flops,
    )
    term = call(group_kernel, (), (term,), (pieces,), term.size, (text_grad,))
    term = exchange(term, RING)
    image_grad = dot(proj_grad, full_head, 1, 1).astype(jnp.bfloat16)
    copies = call(copies_kernel, (), (term,), (pieces,), term.size, (image_grad,))
    done = exchange(copies, RING)
    done = call(
        join_kernel, (), (done,), (jax.ShapeDtypeStruct((2, half, width), jnp.bfloat16),), done.size
    )
    head_grad = exchange(done, "core").reshape(share, width).astype(jnp.float32)
    return image_grad, text_grad, head_grad


def solution(mesh):
    fine = Mesh(mesh.devices.reshape(8, 4, 2, 4, 2), ALL)
    in_specs = (P(ALL, None), P(ALL, None), P(REP, None), P(), P(), P(ALL))
    out_specs = (P(ALL, None), P(ALL, None), P(REP, None))
    return jax.shard_map(
        per_device, mesh=fine, in_specs=in_specs, out_specs=out_specs, check_vma=False
    )
```

time: 191 us -> 163 us (0.85)
  the two profiles are of different devices: /device:TPU:9 before, /device:TPU:1 now
where the time goes in v4:
time: 163 us; the launch traced here: 162 us
  starting transfers between devices  58.7 us (36%)
  waiting for transfers between devices  44.9 us (28%)
  blocking collectives  23.1 us (14%)
  Pallas kernels  20.1 us (12%)
  local copies, waits for them, and re-layouts  6.18 us (4%)
  other arithmetic  3.49 us (2%)
  between operations  2.91 us (2%)
  matrix products  2.79 us (2%)
    all_to_all x3, waiting for transfers between devices, exchange(): return lax.all_to_all(array, axes, split_axis=0, concat_axis=0, tiled=True)  23.6 us
    all_to_all x2, blocking collectives, exchange(): return lax.all_to_all(array, axes, split_axis=0, concat_axis=0, tiled=True)  23.1 us
    pallas_call x10, Pallas kernels, call(): pl.pallas_call(kernel, out_shape=outs if len(outs) > 1 else outs[0], in_s...  20.1 us
    ppermute x1, waiting for transfers between devices, per_device(): across = lax.ppermute(own_half, 'yl', SWAP)  18 us
    ppermute x1, starting transfers between devices, per_device(): image_a = lax.ppermute(images, DP, by_chip(-1))  15.3 us
    all_to_all x3, starting transfers between devices, exchange(): return lax.all_to_all(array, axes, split_axis=0, concat_axis=0, tiled=True)  11.7 us
    ppermute x1, starting transfers between devices, per_device(): grad_p = lax.ppermute(proj_grad, 'core', SWAP)  10.1 us
    unnamed x20, local copies, waits for them, and re-layouts  4.98 us
  transfers between devices with their start and end apart: 13, of which 6 were waited for; matrix products, arithmetic and copies ran while one was open for 4% of the time, Pallas kernels for 9%

profile of v4, /device:TPU:1, one launch (start us, length us, event | category | flops | bytes accessed | tf_op | source)
XLA Modules:
  0.0 162.1 jit_solution(12752739662606188066)
XLA Ops:
  0.6 15.3 %collective-permute-start.5 = (bf16[256,1152]{1,0:T(8,128)(2,1)}, bf16[256,1152]{1,0:T(8,128)(2,1)S(1)}, u32[]{:S(2)}, u32[]{:S(2)}) collective-permute-start(bf16[256,1152]{1,0:T(8,128)(2,1)} %images.3), channel_id=1, source_target_pairs={{0,496},{8,504},{16,0},{24,8},{32,16},{40,24},{48,32},{56,40},{64,... | collective-permute-start | bytes 1769480 | tf_op jit(solution)/shard_map/ppermute | solution.py:190
  16.0 2.9 %collective-permute-start.7 = (bf16[256,1152]{1,0:T(8,128)(2,1)}, bf16[256,1152]{1,0:T(8,128)(2,1)S(1)}, u32[]{:S(2)}, u32[]{:S(2)}) collective-permute-start(bf16[256,1152]{1,0:T(8,128)(2,1)} %images.3), channel_id=1, source_target_pairs={{0,8},{8,0},{1,9},{9,1},{2,10},{10,2},{3,11},{11,3},{4,12},{12,4},... | collective-permute-start | bytes 1769480 | tf_op jit(solution)/shard_map/ppermute | solution.py:211
  18.9 2.4 %collective-permute-start.2 = (bf16[72,1152]{1,0:T(8,128)(2,1)S(1)}, bf16[72,1152]{1,0:T(8,128)(2,1)S(1)}, u32[]{:S(2)}, u32[]{:S(2)}) collective-permute-start(bf16[72,1152]{1,0:T(8,128)(2,1)S(1)} %constant_dynamic-slice_fusion), channel_id=1, source_target_pairs={{0,1},{1,0},{2,3},{3,2},{4,5},{5,4},{6,7},{7,6},{8,9},{9,8},{10,11... | collective-permute-start | bytes 497672 | tf_op jit(solution)/shard_map/ppermute | solution.py:200
  21.4 1.9 %collective-permute-start = (bf16[256,1152]{1,0:T(8,128)(2,1)}, bf16[256,1152]{1,0:T(8,128)(2,1)}, u32[]{:S(2)}, u32[]{:S(2)}) collective-permute-start(bf16[256,1152]{1,0:T(8,128)(2,1)} %texts.3), channel_id=1, source_target_pairs={{0,16},{8,24},{16,32},{24,40},{32,48},{40,56},{48,64},{56,72},{64,... | collective-permute-start | bytes 1769480 | tf_op jit(solution)/shard_map/ppermute | solution.py:189
  25.3 18.0 %collective-permute-done.2 = bf16[72,1152]{1,0:T(8,128)(2,1)S(1)} collective-permute-done((bf16[72,1152]{1,0:T(8,128)(2,1)S(1)}, bf16[72,1152]{1,0:T(8,128)(2,1)S(1)}, u32[]{:S(2)}, u32[]{:S(2)}) %collective-permute-start.2) | collective-permute-done | bytes 165920 | tf_op jit(solution)/shard_map/ppermute | solution.py:200
  43.4 1.2 broadcast_in_dim.2
  44.6 4.3 %all-to-all-start = ((bf16[4,2,72,1152]{3,2,1,0:T(8,128)(2,1)}), bf16[4,2,72,1152]{3,2,1,0:T(8,128)(2,1)}, u32[]{:S(2)}, u32[]{:S(2)}) async-start(bf16[4,2,72,1152]{3,2,1,0:T(8,128)(2,1)} %broadcast_in_dim.2), calls=%async_computation | async-start | bytes 2654208 | tf_op jit(solution)/shard_map/all_to_all | solution.py:31
  49.9 3.3 %collective-permute-start.6 = (bf16[256,1152]{1,0:T(8,128)(2,1)}, bf16[256,1152]{1,0:T(8,128)(2,1)S(1)}, u32[]{:S(2)}, u32[]{:S(2)}) collective-permute-start(bf16[256,1152]{1,0:T(8,128)(2,1)} %shard_map.87), channel_id=1, source_target_pairs={{8,0},{16,8},{24,16},{32,24},{40,32},{48,40},{56,48},{64,56},{72,6... | collective-permute-start | bytes 1769480 | tf_op jit(solution)/shard_map/ppermute | solution.py:197
  53.2 12.5 %all-to-all-done = bf16[4,2,72,1152]{3,2,1,0:T(8,128)(2,1)} async-done(((bf16[4,2,72,1152]{3,2,1,0:T(8,128)(2,1)}), bf16[4,2,72,1152]{3,2,1,0:T(8,128)(2,1)}, u32[]{:S(2)}, u32[]{:S(2)}) %all-to-all-start) | async-done | bytes 1327136 | tf_op jit(solution)/shard_map/all_to_all | solution.py:31
  65.6 4.3 %collective-permute-start.3 = (bf16[4,2,72,1152]{3,2,1,0:T(8,128)(2,1)}, bf16[4,2,72,1152]{3,2,1,0:T(8,128)(2,1)S(1)}, u32[]{:S(2)}, u32[]{:S(2)}) collective-permute-start(bf16[4,2,72,1152]{3,2,1,0:T(8,128)(2,1)} %all-to-all-done), channel_id=1, source_target_pairs={{0,8},{8,0},{1,9},{9,1},{2,10},{10,2},{3,11},{11,3},{4,12},{12,4},... | collective-permute-start | bytes 3981320 | tf_op jit(solution)/shard_map/ppermute | solution.py:205
  69.9 1.1 shard_map.85
  71.1 1.9 %collective-permute-start.1 = (bf16[256,1152]{1,0:T(8,128)(2,1)S(1)}, bf16[256,1152]{1,0:T(8,128)(2,1)S(1)}, u32[]{:S(2)}, u32[]{:S(2)}) collective-permute-start(bf16[256,1152]{1,0:T(8,128)(2,1)S(1)} %shard_map.85), channel_id=1, source_target_pairs={{0,8},{8,16},{16,24},{24,32},{32,40},{40,48},{48,56},{56,64},{64,7... | collective-permute-start | bytes 1769480 | tf_op jit(solution)/shard_map/ppermute | solution.py:196
  73.0 2.4 %collective-permute-start.4 = (bf16[256,1152]{1,0:T(8,128)(2,1)}, bf16[256,1152]{1,0:T(8,128)(2,1)S(1)}, u32[]{:S(2)}, u32[]{:S(2)}) collective-permute-start(bf16[256,1152]{1,0:T(8,128)(2,1)} %collective-permute-done.second.text_a), channel_id=1, source_target_pairs={{0,8},{8,0},{1,9},{9,1},{2,10},{10,2},{3,11},{11,3},{4,12},{12,4},... | collective-permute-start | bytes 1769480 | tf_op jit(solution)/shard_map/ppermute | solution.py:191
  76.4 2.4 %maximum_select_fusion = bf16[8,2,72,1152]{3,2,1,0:T(8,128)(2,1)S(1)} fusion(bf16[8,1,72,1152]{3,2,1,0:T(8,128)(2,1)S(1)} %bitcast.15, bf16[8,1,72,1152]{3,2,1,0:T(8,128)(2,1)} %bitcast.3, pred[]{:T(512)S(6)} %eq.6), kind=kLoop, calls=%fused_computation | loop fusion | flops 3981312 | bytes 5308417 | tf_op jit(solution)/shard_map/jit(_where)/select_n | solution.py:207
  78.9 4.4 %shard_map.86 = (f32[256,1152]{1,0:T(8,128)S(1)}, f32[256,128]{1,0:T(8,128)S(1)}, bf16[256,1152]{1,0:T(8,128)(2,1)S(1)}, f32[256,1152]{1,0:T(8,128)S(1)}) custom-call(f32[2]{0:T(128)S(1)} %pad_maximum_fusion.numbers, s32[1]{0:T(128)S(6)} %copy.11.offset, bf16[256,1152]{1,0:T(8,128)(2,1)S(1)} %copy-done.5, bf16[1152,1152]{1,0:T(8,128)(2,1)S(1)} %bitcast.12, ...), custom_call_target="tpu_custom_call" | custom-call | flops 1585446912 | bytes 8093696 | tf_op jit(solution)/shard_map/pallas_call | solution.py:168
  83.3 1.9 %shard_map.89.grad = bf16[256,1152]{1,0:T(8,128)(2,1)S(1)} custom-call(f32[2]{0:T(128)S(1)} %pad_maximum_fusion.numbers, bf16[256,1152]{1,0:T(8,128)(2,1)S(1)} %collective-permute-done.1.text_c, f32[256,1152]{1,0:T(8,128)S(1)} %get-tuple-element.7.unit, f32[256,128]{1,0:T(8,128)S(1)} %get-tuple-element.8.inverse, ...), custom_call_target="tpu_custom_call" | custom-call | flops 301989888 | bytes 4259840 | tf_op jit(solution)/shard_map/pallas_call | solution.py:168
  85.2 10.1 %collective-permute-start.9 = (bf16[256,1152]{1,0:T(8,128)(2,1)S(1)}, bf16[256,1152]{1,0:T(8,128)(2,1)S(1)}, u32[]{:S(2)}, u32[]{:S(2)}) collective-permute-start(bf16[256,1152]{1,0:T(8,128)(2,1)S(1)} %shard_map.89.grad), channel_id=1, source_target_pairs={{0,8},{8,0},{1,9},{9,1},{2,10},{10,2},{3,11},{11,3},{4,12},{12,4},... | collective-permute-start | bytes 1769480 | tf_op jit(solution)/shard_map/ppermute | solution.py:231
  95.2 1.6 collective-permute-done.9.grad_p
  96.8 2.0 %shard_map.91 = bf16[8,72,1152]{2,1,0:T(8,128)(2,1)} custom-call(bf16[576,512]{1,0:T(8,128)(2,1)S(1)} %shard_map.88.picked, bf16[256,1152]{1,0:T(8,128)(2,1)S(1)} %shard_map.89.grad, bf16[256,1152]{1,0:T(8,128)(2,1)S(1)} %collective-permute-done.9.grad_p), custom_call_target="tpu_custom_call" | custom-call | flops 679477248 | bytes 3096576 | tf_op jit(solution)/shard_map/pallas_call | solution.py:168
  98.9 3.6 %all-to-all-start.1 = ((bf16[8,72,1152]{2,1,0:T(8,128)(2,1)}), bf16[8,72,1152]{2,1,0:T(8,128)(2,1)S(1)}, u32[]{:S(2)}, u32[]{:S(2)}) async-start(bf16[8,72,1152]{2,1,0:T(8,128)(2,1)} %shard_map.91), calls=%async_computation.1 | async-start | bytes 2654208 | tf_op jit(solution)/shard_map/all_to_all | solution.py:31
  102.4 2.5 %collective-permute-start.8 = (bf16[256,1152]{1,0:T(8,128)(2,1)}, bf16[256,1152]{1,0:T(8,128)(2,1)S(1)}, u32[]{:S(2)}, u32[]{:S(2)}) collective-permute-start(bf16[256,1152]{1,0:T(8,128)(2,1)} %copy-done.8), channel_id=1, source_target_pairs={{0,8},{8,0},{1,9},{9,1},{2,10},{10,2},{3,11},{11,3},{4,12},{12,4},... | collective-permute-start | bytes 1769480 | tf_op jit(solution)/shard_map/ppermute | solution.py:192
  104.9 1.6 %collective-permute-done.8.image_b = bf16[256,1152]{1,0:T(8,128)(2,1)S(1)} collective-permute-done((bf16[256,1152]{1,0:T(8,128)(2,1)}, bf16[256,1152]{1,0:T(8,128)(2,1)S(1)}, u32[]{:S(2)}, u32[]{:S(2)}) %collective-permute-start.8) | collective-permute-done | bytes 589856 | tf_op jit(solution)/shard_map/ppermute | solution.py:192
  106.5 1.7 %copy-done.2 = bf16[8,2,72,1152]{3,2,1,0:T(8,128)(2,1)S(1)} copy-done((bf16[8,2,72,1152]{3,2,1,0:T(8,128)(2,1)S(1)}, bf16[8,2,72,1152]{3,2,1,0:T(8,128)(2,1)}, u32[]{:S(2)}) %copy-start.2) | copy-done | bytes 2654232
  109.4 1.1 copy-done.9
  110.4 7.9 %shard_map.90.here = bf16[256,1152]{1,0:T(8,128)(2,1)} custom-call(f32[2]{0:T(128)S(1)} %pad_maximum_fusion.numbers, s32[1]{0:T(128)S(6)} %copy.11.offset, bf16[256,1152]{1,0:T(8,128)(2,1)S(1)} %copy-done.7, bf16[256,1152]{1,0:T(8,128)(2,1)S(1)} %get-tuple-element.9.img_b, bf16[1152,1152]{1,0:T(8,128)(2,1)S(1)} %bitcast.14, bf16[256,1152]{1,0:T(8,128)(2,1)S(1)} %copy-done.9, ...), custom_call_target="tpu_custom_call" | custom-call | flops 3246391296 | bytes 6193152 | tf_op jit(solution)/shard_map/pallas_call | solution.py:168
  118.3 2.5 %all-to-all-done.1.term = bf16[8,72,1152]{2,1,0:T(8,128)(2,1)S(1)} async-done(((bf16[8,72,1152]{2,1,0:T(8,128)(2,1)}), bf16[8,72,1152]{2,1,0:T(8,128)(2,1)S(1)}, u32[]{:S(2)}, u32[]{:S(2)}) %all-to-all-start.1) | async-done | bytes 1327136 | tf_op jit(solution)/shard_map/all_to_all | solution.py:31
  120.8 1.1 copy-done.4
  122.8 3.9 %all-to-all-start.2 = ((bf16[32,8,384]{2,1,0:T(8,128)(2,1)}), bf16[32,8,384]{2,1,0:T(8,128)(2,1)S(1)}, u32[]{:S(2)}, u32[]{:S(2)}) async-start(bf16[32,8,384]{2,1,0:T(8,128)(2,1)} %shard_map.92), calls=%async_computation.2 | async-start | bytes 393216 | tf_op jit(solution)/shard_map/all_to_all | solution.py:31
  126.6 2.8 %convolution_convert_fusion.here = bf16[256,1152]{1,0:T(8,128)(2,1)S(1)} fusion(bf16[256,1152]{1,0:T(8,128)(2,1)S(1)} %shard_map.89.grad, bf16[1152,1152]{1,0:T(8,128)(2,1)} %bitcast.13), kind=kOutput, calls=%fused_computation.1 | convolution fusion | flops 679772160 | bytes 3833856 | tf_op jit(solution)/shard_map/dot_general | solution.py:18
  129.4 8.6 %all-to-all-done.2.pieces = bf16[32,8,384]{2,1,0:T(8,128)(2,1)S(1)} async-done(((bf16[32,8,384]{2,1,0:T(8,128)(2,1)}), bf16[32,8,384]{2,1,0:T(8,128)(2,1)S(1)}, u32[]{:S(2)}, u32[]{:S(2)}) %all-to-all-start.2) | async-done | bytes 196640 | tf_op jit(solution)/shard_map/all_to_all | solution.py:31
  138.1 16.8 %all_to_all.25.pieces = bf16[32,8,384]{2,1,0:T(8,128)(2,1)S(1)} all-to-all(bf16[32,8,384]{2,1,0:T(8,128)(2,1)S(1)} %shard_map.93), channel_id=1, replica_groups=mesh['z'=8,'yh'=4,'core'=2,'x'=4,'yl'=2] {'z','yh'}, dimensions={0} | all-to-all | bytes 393216 | tf_op jit(solution)/shard_map/all_to_all | solution.py:31
  155.0 6.2 %all_to_all.26 = bf16[2,72,1152]{2,1,0:T(8,128)(2,1)S(1)} all-to-all(bf16[2,72,1152]{2,1,0:T(8,128)(2,1)S(1)} %shard_map.94), channel_id=1, replica_groups=mesh['z'=8,'yh'=4,'core'=2,'x'=4,'yl'=2] {'core'}, dimensions={0} | all-to-all | bytes 663552 | tf_op jit(solution)/shard_map/all_to_all | solution.py:31
  (34 shorter events, 5.0 us)
Async XLA Ops:
  0.6 18.2 %copy-start = (bf16[144,1152]{1,0:T(8,128)(2,1)S(1)}, bf16[144,1152]{1,0:T(8,128)(2,1)}, u32[]{:S(2)}) copy-start(bf16[144,1152]{1,0:T(8,128)(2,1)} %param.8) | copy-start | bytes 995332
  0.6 48.3 %collective-permute-start.5 = (bf16[256,1152]{1,0:T(8,128)(2,1)}, bf16[256,1152]{1,0:T(8,128)(2,1)S(1)}, u32[]{:S(2)}, u32[]{:S(2)}) collective-permute-start(bf16[256,1152]{1,0:T(8,128)(2,1)} %images.3), channel_id=1, source_target_pairs={{0,496},{8,504},{16,0},{24,8},{32,16},{40,24},{48,32},{56,40},{64,... | collective-permute-start | bytes 1769480 | tf_op jit(solution)/shard_map/ppermute | solution.py:190
  16.0 59.5 %collective-permute-start.7 = (bf16[256,1152]{1,0:T(8,128)(2,1)}, bf16[256,1152]{1,0:T(8,128)(2,1)S(1)}, u32[]{:S(2)}, u32[]{:S(2)}) collective-permute-start(bf16[256,1152]{1,0:T(8,128)(2,1)} %images.3), channel_id=1, source_target_pairs={{0,8},{8,0},{1,9},{9,1},{2,10},{10,2},{3,11},{11,3},{4,12},{12,4},... | collective-permute-start | bytes 1769480 | tf_op jit(solution)/shard_map/ppermute | solution.py:211
  18.9 30.1 %copy-start.5 = (bf16[256,1152]{1,0:T(8,128)(2,1)S(1)}, bf16[256,1152]{1,0:T(8,128)(2,1)}, u32[]{:S(2)}) copy-start(bf16[256,1152]{1,0:T(8,128)(2,1)} %images.3) | copy-start | bytes 1769476
  18.9 24.4 %collective-permute-start.2 = (bf16[72,1152]{1,0:T(8,128)(2,1)S(1)}, bf16[72,1152]{1,0:T(8,128)(2,1)S(1)}, u32[]{:S(2)}, u32[]{:S(2)}) collective-permute-start(bf16[72,1152]{1,0:T(8,128)(2,1)S(1)} %constant_dynamic-slice_fusion), channel_id=1, source_target_pairs={{0,1},{1,0},{2,3},{3,2},{4,5},{5,4},{6,7},{7,6},{8,9},{9,8},{10,11... | collective-permute-start | bytes 497672 | tf_op jit(solution)/shard_map/ppermute | solution.py:200
  21.4 48.6 %collective-permute-start = (bf16[256,1152]{1,0:T(8,128)(2,1)}, bf16[256,1152]{1,0:T(8,128)(2,1)}, u32[]{:S(2)}, u32[]{:S(2)}) collective-permute-start(bf16[256,1152]{1,0:T(8,128)(2,1)} %texts.3), channel_id=1, source_target_pairs={{0,16},{8,24},{16,32},{24,40},{32,48},{40,56},{48,64},{56,72},{64,... | collective-permute-start | bytes 1769480 | tf_op jit(solution)/shard_map/ppermute | solution.py:189
  44.6 21.0 %all-to-all-start = ((bf16[4,2,72,1152]{3,2,1,0:T(8,128)(2,1)}), bf16[4,2,72,1152]{3,2,1,0:T(8,128)(2,1)}, u32[]{:S(2)}, u32[]{:S(2)}) async-start(bf16[4,2,72,1152]{3,2,1,0:T(8,128)(2,1)} %broadcast_in_dim.2), calls=%async_computation | async-start | bytes 2654208 | tf_op jit(solution)/shard_map/all_to_all | solution.py:31
  48.9 21.0 %copy-start.6 = (bf16[256,1152]{1,0:T(8,128)(2,1)S(1)}, bf16[256,1152]{1,0:T(8,128)(2,1)}, u32[]{:S(2)}) copy-start(bf16[256,1152]{1,0:T(8,128)(2,1)} %texts.3) | copy-start | bytes 1769476
  49.0 29.9 %copy-start.8 = (bf16[256,1152]{1,0:T(8,128)(2,1)}, bf16[256,1152]{1,0:T(8,128)(2,1)S(1)}, u32[]{:S(2)}) copy-start(bf16[256,1152]{1,0:T(8,128)(2,1)S(1)} %collective-permute-done.5.here.second.image_a) | copy-start | bytes 1769476
  49.9 33.4 %collective-permute-start.6 = (bf16[256,1152]{1,0:T(8,128)(2,1)}, bf16[256,1152]{1,0:T(8,128)(2,1)S(1)}, u32[]{:S(2)}, u32[]{:S(2)}) collective-permute-start(bf16[256,1152]{1,0:T(8,128)(2,1)} %shard_map.87), channel_id=1, source_target_pairs={{8,0},{16,8},{24,16},{32,24},{40,32},{48,40},{56,48},{64,56},{72,6... | collective-permute-start | bytes 1769480 | tf_op jit(solution)/shard_map/ppermute | solution.py:197
  65.6 10.8 %collective-permute-start.3 = (bf16[4,2,72,1152]{3,2,1,0:T(8,128)(2,1)}, bf16[4,2,72,1152]{3,2,1,0:T(8,128)(2,1)S(1)}, u32[]{:S(2)}, u32[]{:S(2)}) collective-permute-start(bf16[4,2,72,1152]{3,2,1,0:T(8,128)(2,1)} %all-to-all-done), channel_id=1, source_target_pairs={{0,8},{8,0},{1,9},{9,1},{2,10},{10,2},{3,11},{11,3},{4,12},{12,4},... | collective-permute-start | bytes 3981320 | tf_op jit(solution)/shard_map/ppermute | solution.py:205
  71.1 12.2 %collective-permute-start.1 = (bf16[256,1152]{1,0:T(8,128)(2,1)S(1)}, bf16[256,1152]{1,0:T(8,128)(2,1)S(1)}, u32[]{:S(2)}, u32[]{:S(2)}) collective-permute-start(bf16[256,1152]{1,0:T(8,128)(2,1)S(1)} %shard_map.85), channel_id=1, source_target_pairs={{0,8},{8,16},{16,24},{24,32},{32,40},{40,48},{48,56},{56,64},{64,7... | collective-permute-start | bytes 1769480 | tf_op jit(solution)/shard_map/ppermute | solution.py:196
  73.0 5.8 %collective-permute-start.4 = (bf16[256,1152]{1,0:T(8,128)(2,1)}, bf16[256,1152]{1,0:T(8,128)(2,1)S(1)}, u32[]{:S(2)}, u32[]{:S(2)}) collective-permute-start(bf16[256,1152]{1,0:T(8,128)(2,1)} %collective-permute-done.second.text_a), channel_id=1, source_target_pairs={{0,8},{8,0},{1,9},{9,1},{2,10},{10,2},{3,11},{11,3},{4,12},{12,4},... | collective-permute-start | bytes 1769480 | tf_op jit(solution)/shard_map/ppermute | solution.py:191
  78.8 4.4 %copy-start.1 = (bf16[8,2,72,1152]{3,2,1,0:T(8,128)(2,1)}, bf16[8,2,72,1152]{3,2,1,0:T(8,128)(2,1)S(1)}, u32[]{:S(2)}) copy-start(bf16[8,2,72,1152]{3,2,1,0:T(8,128)(2,1)S(1)} %maximum_select_fusion) | copy-start | bytes 7962628
  85.2 11.7 %collective-permute-start.9 = (bf16[256,1152]{1,0:T(8,128)(2,1)S(1)}, bf16[256,1152]{1,0:T(8,128)(2,1)S(1)}, u32[]{:S(2)}, u32[]{:S(2)}) collective-permute-start(bf16[256,1152]{1,0:T(8,128)(2,1)S(1)} %shard_map.89.grad), channel_id=1, source_target_pairs={{0,8},{8,0},{1,9},{9,1},{2,10},{10,2},{3,11},{11,3},{4,12},{12,4},... | collective-permute-start | bytes 1769480 | tf_op jit(solution)/shard_map/ppermute | solution.py:231
  98.9 22.0 %all-to-all-start.1 = ((bf16[8,72,1152]{2,1,0:T(8,128)(2,1)}), bf16[8,72,1152]{2,1,0:T(8,128)(2,1)S(1)}, u32[]{:S(2)}, u32[]{:S(2)}) async-start(bf16[8,72,1152]{2,1,0:T(8,128)(2,1)} %shard_map.91), calls=%async_computation.1 | async-start | bytes 2654208 | tf_op jit(solution)/shard_map/all_to_all | solution.py:31
  102.4 4.1 %collective-permute-start.8 = (bf16[256,1152]{1,0:T(8,128)(2,1)}, bf16[256,1152]{1,0:T(8,128)(2,1)S(1)}, u32[]{:S(2)}, u32[]{:S(2)}) collective-permute-start(bf16[256,1152]{1,0:T(8,128)(2,1)} %copy-done.8), channel_id=1, source_target_pairs={{0,8},{8,0},{1,9},{9,1},{2,10},{10,2},{3,11},{11,3},{4,12},{12,4},... | collective-permute-start | bytes 1769480 | tf_op jit(solution)/shard_map/ppermute | solution.py:192
  106.5 1.7 %copy-start.2 = (bf16[8,2,72,1152]{3,2,1,0:T(8,128)(2,1)S(1)}, bf16[8,2,72,1152]{3,2,1,0:T(8,128)(2,1)}, u32[]{:S(2)}) copy-start(bf16[8,2,72,1152]{3,2,1,0:T(8,128)(2,1)} %copy-done.1) | copy-start | bytes 7962628
  108.3 1.1 copy-start.7
  109.4 1.1 copy-start.9
  120.8 1.1 copy-start.4
  122.8 15.3 %all-to-all-start.2 = ((bf16[32,8,384]{2,1,0:T(8,128)(2,1)}), bf16[32,8,384]{2,1,0:T(8,128)(2,1)S(1)}, u32[]{:S(2)}, u32[]{:S(2)}) async-start(bf16[32,8,384]{2,1,0:T(8,128)(2,1)} %shard_map.92), calls=%async_computation.2 | async-start | bytes 393216 | tf_op jit(solution)/shard_map/all_to_all | solution.py:31
  129.4 32.7 %copy-start.3 = (bf16[256,1152]{1,0:T(8,128)(2,1)}, bf16[256,1152]{1,0:T(8,128)(2,1)S(1)}, u32[]{:S(2)}) copy-start(bf16[256,1152]{1,0:T(8,128)(2,1)S(1)} %convolution_convert_fusion.here) | copy-start | bytes 1769476

commit v5 on v4

v5 whole, which is shorter than its diff:
```python
import jax
import jax.numpy as jnp
from jax import lax
from jax.experimental import pallas as pl
from jax.experimental.pallas import tpu as pltpu
from jax.sharding import Mesh
from jax.sharding import PartitionSpec as P

EPS = 1e-06
CHAIN = 20_000_000_000
DP = ("z", "yh", "core")
RING = ("z", "yh")
REP = ("x", "yl")
ALL = DP + REP


def dot(a, b, ca, cb):
    return lax.dot_general(a, b, (((ca,), (cb,)), ((), ())), preferred_element_type=jnp.float32)


def by_chip(shift):
    return [(p, (p + 2 * shift) % 64) for p in range(64)]


SWAP = [(0, 1), (1, 0)]
CROSS = [(0, 1), (3, 2)]
FAR = [(p, (p + (1 if p % 2 else 63)) % 64) for p in range(64)]


def exchange(array, axes):
    return lax.all_to_all(array, axes, split_axis=0, concat_axis=0, tiled=True)


def unit_rows(values):
    inverse = lax.rsqrt(jnp.sum(values * values, axis=-1, keepdims=True) + EPS)
    return values * inverse, inverse


def off_unit(direction, unit, inverse):
    return (direction - unit * jnp.sum(unit * direction, axis=-1, keepdims=True)) * inverse


def narrow(values):
    return values.astype(jnp.bfloat16)


def rounded_unit(block):
    return narrow(unit_rows(block.astype(jnp.float32))[0])


def negatives(a, b, numbers):
    logits = numbers[0] * dot(a, b, 1, 1) + numbers[1]
    return narrow(numbers[0] * jax.nn.sigmoid(logits))


def own_pairs(a, b, numbers, positive):
    logits = numbers[0] * dot(a, b, 1, 1) + numbers[1]
    sign = jnp.where(positive, jnp.float32(1.0), jnp.float32(-1.0))
    return narrow(numbers[0] * (-sign * jax.nn.sigmoid(-sign * logits)))


def positives(offset, rows, image_dim):
    image = lax.broadcasted_iota(jnp.int32, (rows, rows), image_dim)
    text = lax.broadcasted_iota(jnp.int32, (rows, rows), 1 - image_dim)
    target = image + offset
    return text == jnp.where(target >= rows, target - rows, target)


def head_kernel(crossed, head, across, copies):
    shard = jnp.where(crossed[0] == 1, across[...], head[...])
    for index in range(copies.shape[0]):
        copies[index] = shard


def turn_kernel(core, texts, text_a, image_a, units, onward):
    rows = texts.shape[0]
    units[:rows] = rounded_unit(text_a[...])
    units[rows:] = rounded_unit(texts[...])
    onward[...] = jnp.where(core[0] == 0, image_a[...], text_a[...])


def stack_kernel(first, second, out):
    rows = first.shape[0]
    out[:rows] = first[...]
    out[rows:] = second[...]


def first_kernel(
    numbers, offset, core, pair, halves, other, units,
    head, unit, inverse, img_b, far_unit, far_inverse, far_b, partial,
):
    count, share = halves.shape[:2]
    for index in range(count):
        for source, place in ((halves, core[0]), (other, 1 - core[0])):
            start = pl.multiple_of((2 * index + place) * share, 16)
            head[pl.ds(start, share), :] = source[index]

    rows = img_b.shape[0]
    unit_value, inverse_value = unit_rows(dot(pair[rows:], head[...], 1, 0))
    unit[...] = unit_value
    inverse[...] = jnp.broadcast_to(inverse_value, inverse.shape)
    rounded = narrow(unit_value)
    img_b[...] = rounded

    @pl.when(core[0] == 0)
    def _():
        unit_value, inverse_value = unit_rows(dot(pair[:rows], head[...], 1, 0))
        far_unit[...] = unit_value
        far_inverse[...] = jnp.broadcast_to(inverse_value, far_inverse.shape)
        far_b[...] = narrow(unit_value)

    @pl.when(core[0] != 0)
    def _():
        far_unit[...] = unit[...]
        far_inverse[...] = inverse[...]
        far_b[...] = img_b[...]

    block = units[rows:]
    weights = own_pairs(rounded, block, numbers, positives(offset[0], rows, 0))
    total = dot(weights, block, 1, 0)
    block = units[:rows]
    partial[...] = total + dot(negatives(rounded, block, numbers), block, 1, 0)


def grad_kernel(
    numbers, core, units_p, unit, inverse, img_b, far_unit, far_inverse, far_b, partial, here,
    grads,
):
    rows = img_b.shape[0]
    block = units_p[:rows]
    total = partial[...] + dot(negatives(img_b[...], block, numbers), block, 1, 0)
    grad = off_unit(total, unit[...], inverse[:, :1])
    far = jnp.where(core[0] == 0, block, units_p[rows:])
    total = dot(negatives(far_b[...], far, numbers), far, 1, 0)
    far_grad = off_unit(total, far_unit[...], far_inverse[:, :1])

    @pl.when(core[0] == 0)
    def _():
        grads[:rows] = narrow(grad)
        grads[rows:] = narrow(far_grad)

    @pl.when(core[0] != 0)
    def _():
        grads[:rows] = narrow(grad + far_grad)
        grads[rows:] = jnp.zeros_like(far_grad, grads.dtype)


def text_kernel(numbers, offset, core, texts, img_b, head, image_a, pair_p, far, text_grad):
    unit, inverse = unit_rows(texts[...].astype(jnp.float32))
    txt_b = narrow(unit)
    own = img_b[...]
    weights = own_pairs(txt_b, own, numbers, positives(offset[0], own.shape[0], 1))
    total = dot(weights, own, 1, 0)
    rows = own.shape[0]
    last = jnp.where(core[0] == 0, pair_p[rows:], far[...])
    for other in (image_a[...], pair_p[:rows], last):
        block = narrow(unit_rows(dot(other, head[...], 1, 0))[0])
        total = total + dot(negatives(txt_b, block, numbers), block, 1, 0)
    text_grad[...] = narrow(off_unit(total, unit, inverse))


def image_grad_kernel(numbers, core, grads, far, unit, inverse, img_b, head, image_grad):
    block = rounded_unit(far[...])
    total = dot(negatives(img_b[...], block, numbers), block, 1, 0)
    extra = jnp.where(core[0] == 0, off_unit(total, unit[...], inverse[:, :1]), jnp.float32(0.0))
    grad = narrow(grads[: block.shape[0]].astype(jnp.float32) + extra)
    image_grad[...] = narrow(dot(grad, head[...], 1, 1))


def pick_kernel(core, pair, pair_p, picked):
    half, width = picked.shape[0] // 8, pair.shape[1]
    row = lax.broadcasted_iota(jnp.int32, (picked.shape[0], width), 0)
    column = lax.broadcasted_iota(jnp.int32, (picked.shape[0], width), 1)
    wanted = row + (row // half + core[0]) * half
    pick = jnp.where(column == wanted, jnp.float32(1.0), jnp.float32(0.0)).astype(jnp.bfloat16)
    count = pair.shape[0] // 2
    far = jnp.where(core[0] == 0, pair[:count], pair_p[:count])
    for index, block in enumerate((pair[count:], pair_p[count:], far)):
        picked[:, index * count : (index + 1) * count] = narrow(dot(pick, block, 1, 1))


def near_term_kernel(core, picked, grads, here, total):
    count = grads.shape[0] // 2
    total[...] = dot(picked[:, :count], grads[:count], 1, 0)


def term_kernel(core, picked, grads, grads_p, total, out):
    count, half = grads.shape[0] // 2, out.shape[1]
    far = jnp.where(core[0] == 0, grads[count:], grads_p[count:])
    term = total[...] + dot(picked[:, count : 2 * count], grads_p[:count], 1, 0)
    term = term + dot(picked[:, 2 * count :], far, 1, 0)
    for index in range(out.shape[0]):
        out[index] = narrow(term[index * half : (index + 1) * half])


def group_kernel(term, here, out):
    total = term[0].astype(jnp.float32)
    for index in range(1, term.shape[0]):
        total = total + term[index].astype(jnp.float32)
    rows, third = out.shape[1:]
    groups = total.shape[0] // rows
    for group in range(groups):
        for part in range(3):
            piece = total[group * rows : (group + 1) * rows, part * third : (part + 1) * third]
            out[group * 3 + part] = narrow(piece)
    for index in range(groups * 3, out.shape[0]):
        out[index] = jnp.zeros((rows, third), out.dtype)


def copies_kernel(pieces, here, out):
    total = pieces[0].astype(jnp.float32)
    for index in range(1, pieces.shape[0]):
        total = total + pieces[index].astype(jnp.float32)
    for index in range(out.shape[0]):
        out[index] = narrow(total)


def join_kernel(pieces, out):
    rows, third = pieces.shape[1:]
    groups = out.shape[1] // rows
    total = jnp.concatenate(
        [
            jnp.concatenate([pieces[g * 3 + p].astype(jnp.float32) for p in range(3)], 1)
            for g in range(groups)
        ],
        0,
    )
    for index in range(out.shape[0]):
        out[index] = narrow(total)


def call(kernel, scalars, arrays, outs, flops, after=()):
    smem, vmem = pl.BlockSpec(memory_space=pltpu.SMEM), pl.BlockSpec(memory_space=pltpu.VMEM)
    moved = sum(a.size * a.dtype.itemsize for a in list(arrays) + list(outs))
    return pl.pallas_call(
        kernel,
        out_shape=outs if len(outs) > 1 else outs[0],
        in_specs=[smem] * len(scalars) + [vmem] * len(arrays) + [pl.BlockSpec(memory_space=pl.ANY)] * len(after),
        out_specs=[vmem] * len(outs) if len(outs) > 1 else vmem,
        compiler_params=pltpu.CompilerParams(vmem_limit_bytes=24 * 1024 * 1024),
        cost_estimate=pl.CostEstimate(flops=flops, bytes_accessed=moved, transcendentals=0),
    )(*scalars, *arrays, *after)


def per_device(images, texts, head, scale, bias, offsets):
    rows, width = images.shape
    share = head.shape[0]
    half = share // 2
    core = lax.axis_index("core")
    numbers = jnp.concatenate([scale, bias])
    pair_flops = 4 * rows * rows * width
    full_flops = 2 * rows * width * width
    wide = jax.ShapeDtypeStruct((rows, width), jnp.float32)
    slim = jax.ShapeDtypeStruct((rows, width), jnp.bfloat16)

    mine = lax.convert_element_type(core, jnp.int32).reshape(1)
    text_a = lax.ppermute(texts, DP, by_chip(1))
    image_a = lax.ppermute(images, DP, by_chip(-1))
    twice = jax.ShapeDtypeStruct((2 * rows, width), jnp.bfloat16)
    image_pair = call(stack_kernel, (), (image_a, images), (twice,), rows)
    image_pair_p = lax.ppermute(image_pair, "core", SWAP)
    units, onward = call(turn_kernel, (mine,), (texts, text_a, image_a), (twice, slim), CHAIN)
    units_p = lax.ppermute(units, "core", SWAP)
    far = lax.ppermute(onward, DP, FAR)

    y_lo = lax.axis_index("yl")
    across = lax.ppermute(head, ("core", "yl"), CROSS)
    crossed = lax.convert_element_type(core != y_lo, jnp.int32).reshape(1)
    copies = call(
        head_kernel,
        (crossed,),
        (head, across),
        (jax.ShapeDtypeStruct((4, share, width), jnp.bfloat16),),
        2 * CHAIN,
    )
    halves = exchange(copies, "x")
    other = lax.ppermute(halves, "core", SWAP)

    picked = call(
        pick_kernel,
        (mine,),
        (image_pair, image_pair_p),
        (jax.ShapeDtypeStruct((width // 2, 3 * rows), jnp.bfloat16),),
        CHAIN,
    )
    slight = jax.ShapeDtypeStruct((rows, 128), jnp.float32)
    full_head, unit, inverse, img_b, far_unit, far_inverse, far_b, partial = call(
        first_kernel,
        (numbers, offsets, mine),
        (image_pair, halves, other, units),
        (jax.ShapeDtypeStruct((width, width), jnp.bfloat16), wide, slight, slim, wide, slight, slim, wide),
        CHAIN,
    )
    grads = call(
        grad_kernel,
        (numbers, mine),
        (units_p, unit, inverse, img_b, far_unit, far_inverse, far_b, partial),
        (jax.ShapeDtypeStruct((2 * rows, width), jnp.bfloat16),),
        rows,
        (picked,),
    )

    grads_p = lax.ppermute(grads, "core", SWAP)
    pieces = jax.ShapeDtypeStruct((32, 8, width // 3), jnp.bfloat16)
    near = call(
        near_term_kernel,
        (mine,),
        (picked, grads),
        (jax.ShapeDtypeStruct((width // 2, width), jnp.float32),),
        CHAIN // 2,
        (far,),
    )
    term = call(
        term_kernel,
        (mine,),
        (picked, grads, grads_p, near),
        (jax.ShapeDtypeStruct((8, half, width), jnp.bfloat16),),
        full_flops,
    )
    term = exchange(term, REP)
    text_grad = call(
        text_kernel,
        (numbers, offsets, mine),
        (texts, img_b, full_head, image_a, image_pair_p, far),
        (slim,),
        3 * full_flops + 4 * pair_flops,
    )
    term = call(group_kernel, (), (term,), (pieces,), term.size, (text_grad,))
    term = exchange(term, RING)
    image_grad = call(
        image_grad_kernel,
        (numbers, mine),
        (grads, far, unit, inverse, img_b, full_head),
        (slim,),
        full_flops + pair_flops,
    )
    copies = call(copies_kernel, (), (term,), (pieces,), term.size, (image_grad,))
    done = exchange(copies, RING)
    done = call(
        join_kernel, (), (done,), (jax.ShapeDtypeStruct((2, half, width), jnp.bfloat16),), done.size
    )
    head_grad = exchange(done, "core").reshape(share, width).astype(jnp.float32)
    return image_grad, text_grad, head_grad


def solution(mesh):
    fine = Mesh(mesh.devices.reshape(8, 4, 2, 4, 2), ALL)
    in_specs = (P(ALL, None), P(ALL, None), P(REP, None), P(), P(), P(ALL))
    out_specs = (P(ALL, None), P(ALL, None), P(REP, None))
    return jax.shard_map(
        per_device, mesh=fine, in_specs=in_specs, out_specs=out_specs, check_vma=False
    )
```

time: 163 us -> 150 us (0.920)
  waiting for transfers between devices: 44.9 us -> 26 us
  Pallas kernels: 20.1 us -> 30.6 us
  starting transfers between devices: 58.7 us -> 51.8 us
  local copies, waits for them, and re-layouts: 6.18 us -> 11.5 us
  matrix products: 2.79 us -> 0 us
  blocking collectives: 23.1 us -> 25.8 us
  other arithmetic: 3.49 us -> 0.98 us
    ppermute x7 -> x5, waiting for transfers between devices: 21.3 us -> 1.9 us  [the longest x1 1.89 us: per_device(): grads_p = lax.ppermute(grads, 'core', SWAP)]
    ppermute x1, waiting for transfers between devices: 0.01 us -> 14.4 us  [per_device(): image_a = lax.ppermute(images, DP, by_chip(-1))]
    all_to_all x3, waiting for transfers between devices: 23.6 us -> 9.68 us  [exchange(): return lax.all_to_all(array, axes, split_axis=0, concat_axis=0, tiled=True)]
    pallas_call x10 -> x13, Pallas kernels: 20.1 us -> 30.6 us  [call(): pl.pallas_call(kernel, out_shape=outs if len(outs) > 1 else outs[0], in_s...]
    ppermute x7 -> x5, starting transfers between devices: 25.4 us -> 16.8 us  [the longest x1 6.98 us: per_device(): units_p = lax.ppermute(units, 'core', SWAP)]
    unnamed x20 -> x26, local copies, waits for them, and re-layouts: 4.98 us -> 11.5 us
    dot_general x1 -> x0, matrix products: 2.79 us -> none  [dot(): lax.dot_general(a, b, (((ca,), (cb,)), ((), ())), preferred_element_type=...]
    all_to_all x2, blocking collectives: 23.1 us -> 25.8 us  [exchange(): return lax.all_to_all(array, axes, split_axis=0, concat_axis=0, tiled=True)]
  transfers between devices with their start and end apart: 13 -> 11, of which waited for: 6 -> 4; matrix products, arithmetic and copies ran while one was open for 4% -> 0% of each run, Pallas kernels for 9% -> 18%
where the time goes in v5:
time: 150 us; the launch traced here: 149 us
  starting transfers between devices  51.8 us (35%)
  Pallas kernels  30.6 us (20%)
  waiting for transfers between devices  26 us (17%)
  blocking collectives  25.8 us (17%)
  local copies, waits for them, and re-layouts  11.5 us (8%)
  between operations  2.78 us (2%)
    pallas_call x13, Pallas kernels, call(): pl.pallas_call(kernel, out_shape=outs if len(outs) > 1 else outs[0], in_s...  30.6 us
    all_to_all x2, blocking collectives, exchange(): return lax.all_to_all(array, axes, split_axis=0, concat_axis=0, tiled=True)  25.8 us
    ppermute x1, starting transfers between devices, per_device(): image_a = lax.ppermute(images, DP, by_chip(-1))  15.2 us
    ppermute x1, waiting for transfers between devices, per_device(): image_a = lax.ppermute(images, DP, by_chip(-1))  14.4 us
    all_to_all x3, starting transfers between devices, exchange(): return lax.all_to_all(array, axes, split_axis=0, concat_axis=0, tiled=True)  14.3 us
    unnamed x26, local copies, waits for them, and re-layouts  11.5 us
    all_to_all x3, waiting for transfers between devices, exchange(): return lax.all_to_all(array, axes, split_axis=0, concat_axis=0, tiled=True)  9.68 us
    ppermute x1, starting transfers between devices, per_device(): units_p = lax.ppermute(units, 'core', SWAP)  6.98 us
  transfers between devices with their start and end apart: 11, of which 4 were waited for; matrix products, arithmetic and copies ran while one was open for 0% of the time, Pallas kernels for 18%

profile of v5, /device:TPU:1, one launch (start us, length us, event | category | flops | bytes accessed | tf_op | source)
XLA Modules:
  0.0 149.3 jit_solution(5436327426903843015)
XLA Ops:
  0.6 1.3 collective-permute-start.3
  1.9 15.2 %collective-permute-start.1 = (bf16[256,1152]{1,0:T(8,128)(2,1)}, bf16[256,1152]{1,0:T(8,128)(2,1)S(1)}, u32[]{:S(2)}, u32[]{:S(2)}) collective-permute-start(bf16[256,1152]{1,0:T(8,128)(2,1)} %second.1), channel_id=1, source_target_pairs={{0,496},{8,504},{16,0},{24,8},{32,16},{40,24},{48,32},{56,40},{64,... | collective-permute-start | bytes 1769480 | tf_op jit(solution)/shard_map/ppermute | solution.py:258
  17.1 1.9 %collective-permute-start = (bf16[256,1152]{1,0:T(8,128)(2,1)}, bf16[256,1152]{1,0:T(8,128)(2,1)S(1)}, u32[]{:S(2)}, u32[]{:S(2)}) collective-permute-start(bf16[256,1152]{1,0:T(8,128)(2,1)} %texts.3), channel_id=1, source_target_pairs={{0,16},{8,24},{16,32},{24,40},{32,48},{40,56},{48,64},{56,72},{64,... | collective-permute-start | bytes 1769480 | tf_op jit(solution)/shard_map/ppermute | solution.py:257
  22.1 1.2 shard_map.87
  23.3 4.1 %all-to-all-start = ((bf16[4,144,1152]{2,1,0:T(8,128)(2,1)}), bf16[4,144,1152]{2,1,0:T(8,128)(2,1)S(1)}, u32[]{:S(2)}, u32[]{:S(2)}) async-start(bf16[4,144,1152]{2,1,0:T(8,128)(2,1)} %shard_map.87), calls=%async_computation | async-start | bytes 2654208 | tf_op jit(solution)/shard_map/all_to_all | solution.py:31
  27.4 14.4 %collective-permute-done.1.image_a.first = bf16[256,1152]{1,0:T(8,128)(2,1)S(1)} collective-permute-done((bf16[256,1152]{1,0:T(8,128)(2,1)}, bf16[256,1152]{1,0:T(8,128)(2,1)S(1)}, u32[]{:S(2)}, u32[]{:S(2)}) %collective-permute-start.1) | collective-permute-done | bytes 589856 | tf_op jit(solution)/shard_map/ppermute | solution.py:258
  41.8 1.2 shard_map.86.pair
  43.0 3.7 %collective-permute-start.5 = (bf16[512,1152]{1,0:T(8,128)(2,1)}, bf16[512,1152]{1,0:T(8,128)(2,1)}, u32[]{:S(2)}, u32[]{:S(2)}) collective-permute-start(bf16[512,1152]{1,0:T(8,128)(2,1)} %shard_map.86.pair), channel_id=1, source_target_pairs={{0,8},{8,0},{1,9},{9,1},{2,10},{10,2},{3,11},{11,3},{4,12},{12,4},... | collective-permute-start | bytes 3538952 | tf_op jit(solution)/shard_map/ppermute | solution.py:261
  46.8 1.6 %shard_map.85 = (bf16[512,1152]{1,0:T(8,128)(2,1)}, bf16[256,1152]{1,0:T(8,128)(2,1)}) custom-call(s32[1]{0:T(128)} %bitcast.core, bf16[256,1152]{1,0:T(8,128)(2,1)S(1)} %copy-done.10, bf16[256,1152]{1,0:T(8,128)(2,1)S(1)} %collective-permute-done.text_a, bf16[256,1152]{1,0:T(8,128)(2,1)S(1)} %collective-permute-done.1.image_a.first), custom_call_target="tpu_custom_call" | custom-call | flops 20000000000 | bytes 3538944 | tf_op jit(solution)/shard_map/pallas_call | solution.py:235
  48.3 7.0 %collective-permute-start.2 = (bf16[512,1152]{1,0:T(8,128)(2,1)}, bf16[512,1152]{1,0:T(8,128)(2,1)S(1)}, u32[]{:S(2)}, u32[]{:S(2)}) collective-permute-start(bf16[512,1152]{1,0:T(8,128)(2,1)} %get-tuple-element.13.units), channel_id=1, source_target_pairs={{0,8},{8,0},{1,9},{9,1},{2,10},{10,2},{3,11},{11,3},{4,12},{12,4},... | collective-permute-start | bytes 3538952 | tf_op jit(solution)/shard_map/ppermute | solution.py:263
  55.3 1.9 %collective-permute-start.6 = (bf16[256,1152]{1,0:T(8,128)(2,1)}, bf16[256,1152]{1,0:T(8,128)(2,1)}, u32[]{:S(2)}, u32[]{:S(2)}) collective-permute-start(bf16[256,1152]{1,0:T(8,128)(2,1)} %get-tuple-element.21), channel_id=1, source_target_pairs={{0,504},{8,16},{16,8},{24,32},{32,24},{40,48},{48,40},{56,64},{64,... | collective-permute-start | bytes 1769480 | tf_op jit(solution)/shard_map/ppermute | solution.py:264
  57.3 3.5 %collective-permute-start.4 = (bf16[4,144,1152]{2,1,0:T(8,128)(2,1)S(1)}, bf16[4,144,1152]{2,1,0:T(8,128)(2,1)S(1)}, u32[]{:S(2)}, u32[]{:S(2)}) collective-permute-start(bf16[4,144,1152]{2,1,0:T(8,128)(2,1)S(1)} %all-to-all-done.halves), channel_id=1, source_target_pairs={{0,8},{8,0},{1,9},{9,1},{2,10},{10,2},{3,11},{11,3},{4,12},{12,4},... | collective-permute-start | bytes 3981320 | tf_op jit(solution)/shard_map/ppermute | solution.py:277
  60.8 3.0 %shard_map.89.here.picked = bf16[576,768]{1,0:T(8,128)(2,1)S(1)} custom-call(s32[1]{0:T(128)} %bitcast.core, bf16[512,1152]{1,0:T(8,128)(2,1)} %shard_map.86.pair, bf16[512,1152]{1,0:T(8,128)(2,1)} %collective-permute-done.5.pair_p), custom_call_target="tpu_custom_call" | custom-call | flops 20000000000 | bytes 3244032 | tf_op jit(solution)/shard_map/pallas_call | solution.py:235
  63.8 4.2 %shard_map.88 = (bf16[1152,1152]{1,0:T(8,128)(2,1)S(1)}, f32[256,1152]{1,0:T(8,128)S(1)}, f32[256,128]{1,0:T(8,128)S(1)}, bf16[256,1152]{1,0:T(8,128)(2,1)S(1)},...) custom-call(f32[2]{0:T(128)S(1)} %pad_maximum_fusion.numbers, ...), custom_call_target="tpu_custom_call" | custom-call | flops 20000000000 | bytes 12648448 | tf_op jit(solution)/shard_map/pallas_call | solution.py:235
  68.0 1.5 %copy-done.2 = bf16[1152,1152]{1,0:T(8,128)(2,1)} copy-done((bf16[1152,1152]{1,0:T(8,128)(2,1)}, bf16[1152,1152]{1,0:T(8,128)(2,1)S(1)}, u32[]{:S(2)}) %copy-start.2) | copy-done | bytes 2654232
  69.6 2.8 %shard_map.90.grads = bf16[512,1152]{1,0:T(8,128)(2,1)S(1)} custom-call(f32[2]{0:T(128)S(1)} %pad_maximum_fusion.numbers, s32[1]{0:T(128)} %bitcast.core, bf16[512,1152]{1,0:T(8,128)(2,1)S(1)} %collective-permute-done.2.units_p, f32[256,1152]{1,0:T(8,128)S(1)} %get-tuple-element.14.unit, f32[256,128]{1,0:T(8,128)S(1)} %get-tuple-element.15.inverse, ...), custom_call_target="tpu_custom_call" | custom-call | flops 256 | bytes 7340032 | tf_op jit(solution)/shard_map/pallas_call | solution.py:235
  72.4 2.9 %collective-permute-start.7 = (bf16[512,1152]{1,0:T(8,128)(2,1)S(1)}, bf16[512,1152]{1,0:T(8,128)(2,1)S(1)}, u32[]{:S(2)}, u32[]{:S(2)}) collective-permute-start(bf16[512,1152]{1,0:T(8,128)(2,1)S(1)} %shard_map.90.grads), channel_id=1, source_target_pairs={{0,8},{8,0},{1,9},{9,1},{2,10},{10,2},{3,11},{11,3},{4,12},{12,4},... | collective-permute-start | bytes 3538952 | tf_op jit(solution)/shard_map/ppermute | solution.py:303
  75.9 1.9 %collective-permute-done.7.grads_p = bf16[512,1152]{1,0:T(8,128)(2,1)S(1)} collective-permute-done((bf16[512,1152]{1,0:T(8,128)(2,1)S(1)}, bf16[512,1152]{1,0:T(8,128)(2,1)S(1)}, u32[]{:S(2)}, u32[]{:S(2)}) %collective-permute-start.7) | collective-permute-done | bytes 1179680 | tf_op jit(solution)/shard_map/ppermute | solution.py:303
  77.8 2.1 %shard_map.94 = bf16[8,72,1152]{2,1,0:T(8,128)(2,1)} custom-call(s32[1]{0:T(128)} %bitcast.core, bf16[576,768]{1,0:T(8,128)(2,1)S(1)} %shard_map.89.here.picked, bf16[512,1152]{1,0:T(8,128)(2,1)S(1)} %shard_map.90.grads, bf16[512,1152]{1,0:T(8,128)(2,1)S(1)} %collective-permute-done.7.grads_p, f32[576,1152]{1,0:T(8,128)S(1)} %shard_map.93.total), custom_call_target="tpu_custom_call" | custom-call | flops 679477248 | bytes 7225344 | tf_op jit(solution)/shard_map/pallas_call | solution.py:235
  79.9 4.0 %all-to-all-start.1 = ((bf16[8,72,1152]{2,1,0:T(8,128)(2,1)}), bf16[8,72,1152]{2,1,0:T(8,128)(2,1)S(1)}, u32[]{:S(2)}, u32[]{:S(2)}) async-start(bf16[8,72,1152]{2,1,0:T(8,128)(2,1)} %shard_map.94), calls=%async_computation.1 | async-start | bytes 2654208 | tf_op jit(solution)/shard_map/all_to_all | solution.py:31
  83.9 1.7 %copy-done.3 = bf16[1152,1152]{1,0:T(8,128)(2,1)S(1)} copy-done((bf16[1152,1152]{1,0:T(8,128)(2,1)S(1)}, bf16[1152,1152]{1,0:T(8,128)(2,1)}, u32[]{:S(2)}) %copy-start.3) | copy-done | bytes 2654232
  87.8 8.9 %shard_map.92.here = bf16[256,1152]{1,0:T(8,128)(2,1)} custom-call(f32[2]{0:T(128)S(1)} %pad_maximum_fusion.numbers, s32[1]{0:T(128)S(6)} %copy.11.offset, s32[1]{0:T(128)} %bitcast.core, bf16[256,1152]{1,0:T(8,128)(2,1)S(1)} %copy-done.11, bf16[256,1152]{1,0:T(8,128)(2,1)S(1)} %get-tuple-element.16.img_b, bf16[1152,1152]{1,0:T(8,128)(2,1)S(1)} %copy-done.3, ...), custom_call_target="tpu_custom_call" | custom-call | flops 3246391296 | bytes 6782976 | tf_op jit(solution)/shard_map/pallas_call | solution.py:235
  96.7 5.4 %all-to-all-done.1.term = bf16[8,72,1152]{2,1,0:T(8,128)(2,1)S(1)} async-done(((bf16[8,72,1152]{2,1,0:T(8,128)(2,1)}), bf16[8,72,1152]{2,1,0:T(8,128)(2,1)S(1)}, u32[]{:S(2)}, u32[]{:S(2)}) %all-to-all-start.1) | async-done | bytes 1327136 | tf_op jit(solution)/shard_map/all_to_all | solution.py:31
  102.1 1.1 copy-done.9
  104.0 6.1 %all-to-all-start.2 = ((bf16[32,8,384]{2,1,0:T(8,128)(2,1)}), bf16[32,8,384]{2,1,0:T(8,128)(2,1)S(1)}, u32[]{:S(2)}, u32[]{:S(2)}) async-start(bf16[32,8,384]{2,1,0:T(8,128)(2,1)} %shard_map.95), calls=%async_computation.2 | async-start | bytes 393216 | tf_op jit(solution)/shard_map/all_to_all | solution.py:31
  110.1 1.3 copy-done.1
  111.4 1.7 %copy-done.4 = bf16[1152,1152]{1,0:T(8,128)(2,1)S(1)} copy-done((bf16[1152,1152]{1,0:T(8,128)(2,1)S(1)}, bf16[1152,1152]{1,0:T(8,128)(2,1)}, u32[]{:S(2)}) %copy-start.4) | copy-done | bytes 2654232
  113.1 4.1 %shard_map.91.here = bf16[256,1152]{1,0:T(8,128)(2,1)} custom-call(f32[2]{0:T(128)S(1)} %pad_maximum_fusion.numbers, s32[1]{0:T(128)} %bitcast.core, bf16[512,1152]{1,0:T(8,128)(2,1)S(1)} %shard_map.90.grads, bf16[256,1152]{1,0:T(8,128)(2,1)} %collective-permute-done.6.far.here, f32[256,1152]{1,0:T(8,128)S(1)} %copy-done.1, ...), custom_call_target="tpu_custom_call" | custom-call | flops 981467136 | bytes 6914048 | tf_op jit(solution)/shard_map/pallas_call | solution.py:235
  117.3 4.2 %all-to-all-done.2.pieces = bf16[32,8,384]{2,1,0:T(8,128)(2,1)S(1)} async-done(((bf16[32,8,384]{2,1,0:T(8,128)(2,1)}), bf16[32,8,384]{2,1,0:T(8,128)(2,1)S(1)}, u32[]{:S(2)}, u32[]{:S(2)}) %all-to-all-start.2) | async-done | bytes 196640 | tf_op jit(solution)/shard_map/all_to_all | solution.py:31
  121.5 1.1 copy-done.5
  122.6 18.7 %all_to_all.25.pieces = bf16[32,8,384]{2,1,0:T(8,128)(2,1)S(1)} all-to-all(bf16[32,8,384]{2,1,0:T(8,128)(2,1)S(1)} %shard_map.96), channel_id=1, replica_groups=mesh['z'=8,'yh'=4,'core'=2,'x'=4,'yl'=2] {'z','yh'}, dimensions={0} | all-to-all | bytes 393216 | tf_op jit(solution)/shard_map/all_to_all | solution.py:31
  141.3 7.1 %all_to_all.26 = bf16[2,72,1152]{2,1,0:T(8,128)(2,1)S(1)} all-to-all(bf16[2,72,1152]{2,1,0:T(8,128)(2,1)S(1)} %shard_map.97), channel_id=1, replica_groups=mesh['z'=8,'yh'=4,'core'=2,'x'=4,'yl'=2] {'core'}, dimensions={0} | all-to-all | bytes 663552 | tf_op jit(solution)/shard_map/all_to_all | solution.py:31
  (33 shorter events, 5.6 us)
Async XLA Ops:
  0.6 20.5 %collective-permute-start.3 = (bf16[144,1152]{1,0:T(8,128)(2,1)}, bf16[144,1152]{1,0:T(8,128)(2,1)S(1)}, u32[]{:S(2)}, u32[]{:S(2)}) collective-permute-start(bf16[144,1152]{1,0:T(8,128)(2,1)} %head.1), channel_id=1, source_target_pairs={{0,1},{9,8},{2,3},{11,10},{4,5},{13,12},{6,7},{15,14},{16,17},{25,... | collective-permute-start | bytes 995336 | tf_op jit(solution)/shard_map/ppermute | solution.py:267
  1.9 39.9 %collective-permute-start.1 = (bf16[256,1152]{1,0:T(8,128)(2,1)}, bf16[256,1152]{1,0:T(8,128)(2,1)S(1)}, u32[]{:S(2)}, u32[]{:S(2)}) collective-permute-start(bf16[256,1152]{1,0:T(8,128)(2,1)} %second.1), channel_id=1, source_target_pairs={{0,496},{8,504},{16,0},{24,8},{32,16},{40,24},{48,32},{56,40},{64,... | collective-permute-start | bytes 1769480 | tf_op jit(solution)/shard_map/ppermute | solution.py:258
  17.1 29.6 %collective-permute-start = (bf16[256,1152]{1,0:T(8,128)(2,1)}, bf16[256,1152]{1,0:T(8,128)(2,1)S(1)}, u32[]{:S(2)}, u32[]{:S(2)}) collective-permute-start(bf16[256,1152]{1,0:T(8,128)(2,1)} %texts.3), channel_id=1, source_target_pairs={{0,16},{8,24},{16,32},{24,40},{32,48},{40,56},{48,64},{56,72},{64,... | collective-permute-start | bytes 1769480 | tf_op jit(solution)/shard_map/ppermute | solution.py:257
  21.1 1.0 copy-start.12
  23.3 18.5 %copy-start.6 = (bf16[256,1152]{1,0:T(8,128)(2,1)S(1)}, bf16[256,1152]{1,0:T(8,128)(2,1)}, u32[]{:S(2)}) copy-start(bf16[256,1152]{1,0:T(8,128)(2,1)} %second.1) | copy-start | bytes 1769476
  23.3 34.0 %all-to-all-start = ((bf16[4,144,1152]{2,1,0:T(8,128)(2,1)}), bf16[4,144,1152]{2,1,0:T(8,128)(2,1)S(1)}, u32[]{:S(2)}, u32[]{:S(2)}) async-start(bf16[4,144,1152]{2,1,0:T(8,128)(2,1)} %shard_map.87), calls=%async_computation | async-start | bytes 2654208 | tf_op jit(solution)/shard_map/all_to_all | solution.py:31
  27.4 19.3 %copy-start.10 = (bf16[256,1152]{1,0:T(8,128)(2,1)S(1)}, bf16[256,1152]{1,0:T(8,128)(2,1)}, u32[]{:S(2)}) copy-start(bf16[256,1152]{1,0:T(8,128)(2,1)} %texts.3) | copy-start | bytes 1769476
  41.8 4.9 %copy-start.7 = (bf16[256,1152]{1,0:T(8,128)(2,1)}, bf16[256,1152]{1,0:T(8,128)(2,1)S(1)}, u32[]{:S(2)}) copy-start(bf16[256,1152]{1,0:T(8,128)(2,1)S(1)} %collective-permute-done.1.image_a.first) | copy-start | bytes 1769476
  43.0 17.8 %collective-permute-start.5 = (bf16[512,1152]{1,0:T(8,128)(2,1)}, bf16[512,1152]{1,0:T(8,128)(2,1)}, u32[]{:S(2)}, u32[]{:S(2)}) collective-permute-start(bf16[512,1152]{1,0:T(8,128)(2,1)} %shard_map.86.pair), channel_id=1, source_target_pairs={{0,8},{8,0},{1,9},{9,1},{2,10},{10,2},{3,11},{11,3},{4,12},{12,4},... | collective-permute-start | bytes 3538952 | tf_op jit(solution)/shard_map/ppermute | solution.py:261
  48.3 21.2 %collective-permute-start.2 = (bf16[512,1152]{1,0:T(8,128)(2,1)}, bf16[512,1152]{1,0:T(8,128)(2,1)S(1)}, u32[]{:S(2)}, u32[]{:S(2)}) collective-permute-start(bf16[512,1152]{1,0:T(8,128)(2,1)} %get-tuple-element.13.units), channel_id=1, source_target_pairs={{0,8},{8,0},{1,9},{9,1},{2,10},{10,2},{3,11},{11,3},{4,12},{12,4},... | collective-permute-start | bytes 3538952 | tf_op jit(solution)/shard_map/ppermute | solution.py:263
  55.3 20.0 %collective-permute-start.6 = (bf16[256,1152]{1,0:T(8,128)(2,1)}, bf16[256,1152]{1,0:T(8,128)(2,1)}, u32[]{:S(2)}, u32[]{:S(2)}) collective-permute-start(bf16[256,1152]{1,0:T(8,128)(2,1)} %get-tuple-element.21), channel_id=1, source_target_pairs={{0,504},{8,16},{16,8},{24,32},{32,24},{40,48},{48,40},{56,64},{64,... | collective-permute-start | bytes 1769480 | tf_op jit(solution)/shard_map/ppermute | solution.py:264
  57.3 6.5 %collective-permute-start.4 = (bf16[4,144,1152]{2,1,0:T(8,128)(2,1)S(1)}, bf16[4,144,1152]{2,1,0:T(8,128)(2,1)S(1)}, u32[]{:S(2)}, u32[]{:S(2)}) collective-permute-start(bf16[4,144,1152]{2,1,0:T(8,128)(2,1)S(1)} %all-to-all-done.halves), channel_id=1, source_target_pairs={{0,8},{8,0},{1,9},{9,1},{2,10},{10,2},{3,11},{11,3},{4,12},{12,4},... | collective-permute-start | bytes 3981320 | tf_op jit(solution)/shard_map/ppermute | solution.py:277
  68.0 1.5 %copy-start.2 = (bf16[1152,1152]{1,0:T(8,128)(2,1)}, bf16[1152,1152]{1,0:T(8,128)(2,1)S(1)}, u32[]{:S(2)}) copy-start(bf16[1152,1152]{1,0:T(8,128)(2,1)S(1)} %get-tuple-element.22.head) | copy-start | bytes 7962628
  69.6 2.8 %copy-start = (f32[256,1152]{1,0:T(8,128)}, f32[256,1152]{1,0:T(8,128)S(1)}, u32[]{:S(2)}) copy-start(f32[256,1152]{1,0:T(8,128)S(1)} %get-tuple-element.14.unit) | copy-start | bytes 3538948
  72.4 5.4 %collective-permute-start.7 = (bf16[512,1152]{1,0:T(8,128)(2,1)S(1)}, bf16[512,1152]{1,0:T(8,128)(2,1)S(1)}, u32[]{:S(2)}, u32[]{:S(2)}) collective-permute-start(bf16[512,1152]{1,0:T(8,128)(2,1)S(1)} %shard_map.90.grads), channel_id=1, source_target_pairs={{0,8},{8,0},{1,9},{9,1},{2,10},{10,2},{3,11},{11,3},{4,12},{12,4},... | collective-permute-start | bytes 3538952 | tf_op jit(solution)/shard_map/ppermute | solution.py:303
  79.9 22.2 %all-to-all-start.1 = ((bf16[8,72,1152]{2,1,0:T(8,128)(2,1)}), bf16[8,72,1152]{2,1,0:T(8,128)(2,1)S(1)}, u32[]{:S(2)}, u32[]{:S(2)}) async-start(bf16[8,72,1152]{2,1,0:T(8,128)(2,1)} %shard_map.94), calls=%async_computation.1 | async-start | bytes 2654208 | tf_op jit(solution)/shard_map/all_to_all | solution.py:31
  83.9 1.7 %copy-start.3 = (bf16[1152,1152]{1,0:T(8,128)(2,1)S(1)}, bf16[1152,1152]{1,0:T(8,128)(2,1)}, u32[]{:S(2)}) copy-start(bf16[1152,1152]{1,0:T(8,128)(2,1)} %copy-done.2) | copy-start | bytes 7962628
  85.7 1.1 copy-start.8
  86.7 1.1 copy-start.11
  102.1 1.1 copy-start.9
  104.0 17.5 %all-to-all-start.2 = ((bf16[32,8,384]{2,1,0:T(8,128)(2,1)}), bf16[32,8,384]{2,1,0:T(8,128)(2,1)S(1)}, u32[]{:S(2)}, u32[]{:S(2)}) async-start(bf16[32,8,384]{2,1,0:T(8,128)(2,1)} %shard_map.95), calls=%async_computation.2 | async-start | bytes 393216 | tf_op jit(solution)/shard_map/all_to_all | solution.py:31
  110.1 1.3 copy-start.1
  111.4 1.7 %copy-start.4 = (bf16[1152,1152]{1,0:T(8,128)(2,1)S(1)}, bf16[1152,1152]{1,0:T(8,128)(2,1)}, u32[]{:S(2)}) copy-start(bf16[1152,1152]{1,0:T(8,128)(2,1)} %copy-done.2) | copy-start | bytes 7962628
  121.5 1.1 copy-start.5

commit v6 on v5

--- a/solution.py
+++ b/solution.py
@@ -145,7 +145,7 @@
         grads[rows:] = jnp.zeros_like(far_grad, grads.dtype)
 
 
-def text_kernel(numbers, offset, core, texts, img_b, head, image_a, pair_p, far, text_grad):
+def text_kernel(numbers, offset, core, texts, img_b, head, image_a, pair_p, far, text_grad, token):
     unit, inverse = unit_rows(texts[...].astype(jnp.float32))
     txt_b = narrow(unit)
     own = img_b[...]
@@ -157,14 +157,16 @@
         block = narrow(unit_rows(dot(other, head[...], 1, 0))[0])
         total = total + dot(negatives(txt_b, block, numbers), block, 1, 0)
     text_grad[...] = narrow(off_unit(total, unit, inverse))
-
-
-def image_grad_kernel(numbers, core, grads, far, unit, inverse, img_b, head, image_grad):
+    token[...] = inverse[: token.shape[0]] + jnp.zeros(token.shape, token.dtype)
+
+
+def image_grad_kernel(numbers, core, grads, far, unit, inverse, img_b, head, image_grad, token):
     block = rounded_unit(far[...])
     total = dot(negatives(img_b[...], block, numbers), block, 1, 0)
     extra = jnp.where(core[0] == 0, off_unit(total, unit[...], inverse[:, :1]), jnp.float32(0.0))
     grad = narrow(grads[: block.shape[0]].astype(jnp.float32) + extra)
     image_grad[...] = narrow(dot(grad, head[...], 1, 1))
+    token[...] = inverse[: token.shape[0]]
 
 
 def pick_kernel(core, pair, pair_p, picked):
@@ -217,16 +219,16 @@
 
 def join_kernel(pieces, out):
     rows, third = pieces.shape[1:]
-    groups = out.shape[1] // rows
-    total = jnp.concatenate(
-        [
-            jnp.concatenate([pieces[g * 3 + p].astype(jnp.float32) for p in range(3)], 1)
-            for g in range(groups)
-        ],
-        0,
-    )
-    for index in range(out.shape[0]):
-        out[index] = narrow(total)
+    for group in range(out.shape[0] // rows):
+        row = [pieces[group * 3 + part].astype(jnp.float32) for part in range(3)]
+        out[group * rows : (group + 1) * rows] = jnp.concatenate(row, 1)
+
+
+def last_kernel(core, rows, rows_p, out):
+    half = rows.shape[0]
+    first, second = rows[...], rows_p[...].astype(jnp.float32)
+    out[:half] = jnp.where(core[0] == 0, first, second)
+    out[half:] = jnp.where(core[0] == 0, second, first)
 
 
 def call(kernel, scalars, arrays, outs, flops, after=()):
@@ -237,7 +239,7 @@
         out_shape=outs if len(outs) > 1 else outs[0],
         in_specs=[smem] * len(scalars) + [vmem] * len(arrays) + [pl.BlockSpec(memory_space=pl.ANY)] * len(after),
         out_specs=[vmem] * len(outs) if len(outs) > 1 else vmem,
-        compiler_params=pltpu.CompilerParams(vmem_limit_bytes=24 * 1024 * 1024),
+        compiler_params=pltpu.CompilerParams(vmem_limit_bytes=16 * 1024 * 1024),
         cost_estimate=pl.CostEstimate(flops=flops, bytes_accessed=moved, transcendentals=0),
     )(*scalars, *arrays, *after)
 
@@ -318,28 +320,36 @@
         full_flops,
     )
     term = exchange(term, REP)
-    text_grad = call(
+    token = jax.ShapeDtypeStruct((8, 128), jnp.float32)
+    text_grad, text_done = call(
         text_kernel,
         (numbers, offsets, mine),
         (texts, img_b, full_head, image_a, image_pair_p, far),
-        (slim,),
+        (slim, token),
         3 * full_flops + 4 * pair_flops,
     )
-    term = call(group_kernel, (), (term,), (pieces,), term.size, (text_grad,))
+    term = call(group_kernel, (), (term,), (pieces,), term.size, (text_done,))
     term = exchange(term, RING)
-    image_grad = call(
+    image_grad, image_done = call(
         image_grad_kernel,
         (numbers, mine),
         (grads, far, unit, inverse, img_b, full_head),
-        (slim,),
+        (slim, token),
         full_flops + pair_flops,
     )
-    copies = call(copies_kernel, (), (term,), (pieces,), term.size, (image_grad,))
+    copies = call(copies_kernel, (), (term,), (pieces,), term.size, (image_done,))
     done = exchange(copies, RING)
     done = call(
-        join_kernel, (), (done,), (jax.ShapeDtypeStruct((2, half, width), jnp.bfloat16),), done.size
-    )
-    head_grad = exchange(done, "core").reshape(share, width).astype(jnp.float32)
+        join_kernel, (), (done,), (jax.ShapeDtypeStruct((half, width), jnp.float32),), done.size
+    )
+    done_p = lax.ppermute(narrow(done), "core", SWAP)
+    head_grad = call(
+        last_kernel,
+        (mine,),
+        (done, done_p),
+        (jax.ShapeDtypeStruct((share, width), jnp.float32),),
+        done.size,
+    )
     return image_grad, text_grad, head_grad
 
 

time: 150 us -> 147 us (0.980)
  blocking collectives: 25.8 us -> 18.7 us
  starting transfers between devices: 51.8 us -> 57.1 us
  local copies, waits for them, and re-layouts: 11.5 us -> 9.39 us
    all_to_all x2 -> x1, blocking collectives: 25.8 us -> 18.7 us  [exchange(): return lax.all_to_all(array, axes, split_axis=0, concat_axis=0, tiled=True)]
    ppermute x0 -> x1, starting transfers between devices: none -> 5.35 us  [per_device(): done_p = lax.ppermute(narrow(done), 'core', SWAP)]
    unnamed x26 -> x22, local copies, waits for them, and re-layouts: 11.5 us -> 9.39 us
    pallas_call x13 -> x14, Pallas kernels: 30.6 us -> 31.5 us  [call(): pl.pallas_call(kernel, out_shape=outs if len(outs) > 1 else outs[0], in_s...]
  transfers between devices with their start and end apart: 11 -> 12, of which waited for: 4 -> 5; matrix products, arithmetic and copies ran while one was open for 0% -> 0% of each run, Pallas kernels for 18% -> 19%
where the time goes in v6:
time: 147 us
  starting transfers between devices  57.1 us (39%)
  Pallas kernels  31.5 us (21%)
  waiting for transfers between devices  27 us (18%)
  blocking collectives  18.7 us (13%)
  local copies, waits for them, and re-layouts  9.39 us (6%)
  between operations  2.79 us (2%)
    pallas_call x14, Pallas kernels, call(): pl.pallas_call(kernel, out_shape=outs if len(outs) > 1 else outs[0], in_s...  31.5 us
    all_to_all x1, blocking collectives, exchange(): return lax.all_to_all(array, axes, split_axis=0, concat_axis=0, tiled=True)  18.7 us
    ppermute x1, starting transfers between devices, per_device(): image_a = lax.ppermute(images, DP, by_chip(-1))  15.2 us
    ppermute x1, waiting for transfers between devices, per_device(): image_a = lax.ppermute(images, DP, by_chip(-1))  14.4 us
    all_to_all x3, starting transfers between devices, exchange(): return lax.all_to_all(array, axes, split_axis=0, concat_axis=0, tiled=True)  14.3 us
    all_to_all x3, waiting for transfers between devices, exchange(): return lax.all_to_all(array, axes, split_axis=0, concat_axis=0, tiled=True)  9.7 us
    unnamed x22, local copies, waits for them, and re-layouts  9.39 us
    ppermute x1, starting transfers between devices, per_device(): units_p = lax.ppermute(units, 'core', SWAP)  6.98 us
  transfers between devices with their start and end apart: 12, of which 5 were waited for; matrix products, arithmetic and copies ran while one was open for 0% of the time, Pallas kernels for 19%

profile of v6, /device:TPU:1, one launch (start us, length us, event | category | flops | bytes accessed | tf_op | source)
XLA Modules:
  0.0 146.5 jit_solution(4286285549273645152)
XLA Ops:
  0.6 1.3 collective-permute-start.3
  1.9 15.2 %collective-permute-start.1 = (bf16[256,1152]{1,0:T(8,128)(2,1)}, bf16[256,1152]{1,0:T(8,128)(2,1)S(1)}, u32[]{:S(2)}, u32[]{:S(2)}) collective-permute-start(bf16[256,1152]{1,0:T(8,128)(2,1)} %second.1), channel_id=1, source_target_pairs={{0,496},{8,504},{16,0},{24,8},{32,16},{40,24},{48,32},{56,40},{64,... | collective-permute-start | bytes 1769480 | tf_op jit(solution)/shard_map/ppermute | solution.py:260
  17.1 1.9 %collective-permute-start = (bf16[256,1152]{1,0:T(8,128)(2,1)}, bf16[256,1152]{1,0:T(8,128)(2,1)S(1)}, u32[]{:S(2)}, u32[]{:S(2)}) collective-permute-start(bf16[256,1152]{1,0:T(8,128)(2,1)} %texts.3), channel_id=1, source_target_pairs={{0,16},{8,24},{16,32},{24,40},{32,48},{40,56},{48,64},{56,72},{64,... | collective-permute-start | bytes 1769480 | tf_op jit(solution)/shard_map/ppermute | solution.py:259
  22.1 1.2 shard_map.87
  23.3 4.1 %all-to-all-start = ((bf16[4,144,1152]{2,1,0:T(8,128)(2,1)}), bf16[4,144,1152]{2,1,0:T(8,128)(2,1)S(1)}, u32[]{:S(2)}, u32[]{:S(2)}) async-start(bf16[4,144,1152]{2,1,0:T(8,128)(2,1)} %shard_map.87), calls=%async_computation | async-start | bytes 2654208 | tf_op jit(solution)/shard_map/all_to_all | solution.py:31
  27.4 14.4 %collective-permute-done.1.image_a.first = bf16[256,1152]{1,0:T(8,128)(2,1)S(1)} collective-permute-done((bf16[256,1152]{1,0:T(8,128)(2,1)}, bf16[256,1152]{1,0:T(8,128)(2,1)S(1)}, u32[]{:S(2)}, u32[]{:S(2)}) %collective-permute-start.1) | collective-permute-done | bytes 589856 | tf_op jit(solution)/shard_map/ppermute | solution.py:260
  41.8 1.2 shard_map.86.pair
  43.0 3.7 %collective-permute-start.5 = (bf16[512,1152]{1,0:T(8,128)(2,1)}, bf16[512,1152]{1,0:T(8,128)(2,1)}, u32[]{:S(2)}, u32[]{:S(2)}) collective-permute-start(bf16[512,1152]{1,0:T(8,128)(2,1)} %shard_map.86.pair), channel_id=1, source_target_pairs={{0,8},{8,0},{1,9},{9,1},{2,10},{10,2},{3,11},{11,3},{4,12},{12,4},... | collective-permute-start | bytes 3538952 | tf_op jit(solution)/shard_map/ppermute | solution.py:263
  46.8 1.6 %shard_map.85 = (bf16[512,1152]{1,0:T(8,128)(2,1)}, bf16[256,1152]{1,0:T(8,128)(2,1)}) custom-call(s32[1]{0:T(128)} %bitcast.core, bf16[256,1152]{1,0:T(8,128)(2,1)S(1)} %copy-done.8, bf16[256,1152]{1,0:T(8,128)(2,1)S(1)} %collective-permute-done.text_a, bf16[256,1152]{1,0:T(8,128)(2,1)S(1)} %collective-permute-done.1.image_a.first), custom_call_target="tpu_custom_call" | custom-call | flops 20000000000 | bytes 3538944 | tf_op jit(solution)/shard_map/pallas_call | solution.py:237
  48.3 7.0 %collective-permute-start.2 = (bf16[512,1152]{1,0:T(8,128)(2,1)}, bf16[512,1152]{1,0:T(8,128)(2,1)S(1)}, u32[]{:S(2)}, u32[]{:S(2)}) collective-permute-start(bf16[512,1152]{1,0:T(8,128)(2,1)} %get-tuple-element.17.units), channel_id=1, source_target_pairs={{0,8},{8,0},{1,9},{9,1},{2,10},{10,2},{3,11},{11,3},{4,12},{12,4},... | collective-permute-start | bytes 3538952 | tf_op jit(solution)/shard_map/ppermute | solution.py:265
  55.3 1.9 %collective-permute-start.6 = (bf16[256,1152]{1,0:T(8,128)(2,1)}, bf16[256,1152]{1,0:T(8,128)(2,1)}, u32[]{:S(2)}, u32[]{:S(2)}) collective-permute-start(bf16[256,1152]{1,0:T(8,128)(2,1)} %get-tuple-element.25), channel_id=1, source_target_pairs={{0,504},{8,16},{16,8},{24,32},{32,24},{40,48},{48,40},{56,64},{64,... | collective-permute-start | bytes 1769480 | tf_op jit(solution)/shard_map/ppermute | solution.py:266
  57.3 3.5 %collective-permute-start.4 = (bf16[4,144,1152]{2,1,0:T(8,128)(2,1)S(1)}, bf16[4,144,1152]{2,1,0:T(8,128)(2,1)S(1)}, u32[]{:S(2)}, u32[]{:S(2)}) collective-permute-start(bf16[4,144,1152]{2,1,0:T(8,128)(2,1)S(1)} %all-to-all-done.halves), channel_id=1, source_target_pairs={{0,8},{8,0},{1,9},{9,1},{2,10},{10,2},{3,11},{11,3},{4,12},{12,4},... | collective-permute-start | bytes 3981320 | tf_op jit(solution)/shard_map/ppermute | solution.py:279
  60.8 3.0 %shard_map.89.here.picked = bf16[576,768]{1,0:T(8,128)(2,1)S(1)} custom-call(s32[1]{0:T(128)} %bitcast.core, bf16[512,1152]{1,0:T(8,128)(2,1)} %shard_map.86.pair, bf16[512,1152]{1,0:T(8,128)(2,1)} %collective-permute-done.5.pair_p), custom_call_target="tpu_custom_call" | custom-call | flops 20000000000 | bytes 3244032 | tf_op jit(solution)/shard_map/pallas_call | solution.py:237
  63.8 4.2 %shard_map.88 = (bf16[1152,1152]{1,0:T(8,128)(2,1)S(1)}, f32[256,1152]{1,0:T(8,128)S(1)}, f32[256,128]{1,0:T(8,128)S(1)}, bf16[256,1152]{1,0:T(8,128)(2,1)S(1)},...) custom-call(f32[2]{0:T(128)S(1)} %pad_maximum_fusion.numbers, ...), custom_call_target="tpu_custom_call" | custom-call | flops 20000000000 | bytes 12648448 | tf_op jit(solution)/shard_map/pallas_call | solution.py:237
  68.0 1.5 %copy-done.2 = bf16[1152,1152]{1,0:T(8,128)(2,1)} copy-done((bf16[1152,1152]{1,0:T(8,128)(2,1)}, bf16[1152,1152]{1,0:T(8,128)(2,1)S(1)}, u32[]{:S(2)}) %copy-start.2) | copy-done | bytes 2654232
  69.6 2.8 %shard_map.90.grads = bf16[512,1152]{1,0:T(8,128)(2,1)S(1)} custom-call(f32[2]{0:T(128)S(1)} %pad_maximum_fusion.numbers, s32[1]{0:T(128)} %bitcast.core, bf16[512,1152]{1,0:T(8,128)(2,1)S(1)} %collective-permute-done.2.units_p, f32[256,1152]{1,0:T(8,128)S(1)} %get-tuple-element.18.unit, f32[256,128]{1,0:T(8,128)S(1)} %get-tuple-element.19.inverse, ...), custom_call_target="tpu_custom_call" | custom-call | flops 256 | bytes 7340032 | tf_op jit(solution)/shard_map/pallas_call | solution.py:237
  72.3 2.9 %collective-permute-start.7 = (bf16[512,1152]{1,0:T(8,128)(2,1)S(1)}, bf16[512,1152]{1,0:T(8,128)(2,1)S(1)}, u32[]{:S(2)}, u32[]{:S(2)}) collective-permute-start(bf16[512,1152]{1,0:T(8,128)(2,1)S(1)} %shard_map.90.grads), channel_id=1, source_target_pairs={{0,8},{8,0},{1,9},{9,1},{2,10},{10,2},{3,11},{11,3},{4,12},{12,4},... | collective-permute-start | bytes 3538952 | tf_op jit(solution)/shard_map/ppermute | solution.py:305
  75.9 1.9 %collective-permute-done.7.grads_p = bf16[512,1152]{1,0:T(8,128)(2,1)S(1)} collective-permute-done((bf16[512,1152]{1,0:T(8,128)(2,1)S(1)}, bf16[512,1152]{1,0:T(8,128)(2,1)S(1)}, u32[]{:S(2)}, u32[]{:S(2)}) %collective-permute-start.7) | collective-permute-done | bytes 1179680 | tf_op jit(solution)/shard_map/ppermute | solution.py:305
  77.8 2.1 %shard_map.94 = bf16[8,72,1152]{2,1,0:T(8,128)(2,1)} custom-call(s32[1]{0:T(128)} %bitcast.core, bf16[576,768]{1,0:T(8,128)(2,1)S(1)} %shard_map.89.here.picked, bf16[512,1152]{1,0:T(8,128)(2,1)S(1)} %shard_map.90.grads, bf16[512,1152]{1,0:T(8,128)(2,1)S(1)} %collective-permute-done.7.grads_p, f32[576,1152]{1,0:T(8,128)S(1)} %shard_map.93.total), custom_call_target="tpu_custom_call" | custom-call | flops 679477248 | bytes 7225344 | tf_op jit(solution)/shard_map/pallas_call | solution.py:237
  79.9 4.0 %all-to-all-start.1 = ((bf16[8,72,1152]{2,1,0:T(8,128)(2,1)}), bf16[8,72,1152]{2,1,0:T(8,128)(2,1)S(1)}, u32[]{:S(2)}, u32[]{:S(2)}) async-start(bf16[8,72,1152]{2,1,0:T(8,128)(2,1)} %shard_map.94), calls=%async_computation.1 | async-start | bytes 2654208 | tf_op jit(solution)/shard_map/all_to_all | solution.py:31
  83.9 1.7 %copy-done.3 = bf16[1152,1152]{1,0:T(8,128)(2,1)S(1)} copy-done((bf16[1152,1152]{1,0:T(8,128)(2,1)S(1)}, bf16[1152,1152]{1,0:T(8,128)(2,1)}, u32[]{:S(2)}) %copy-start.3) | copy-done | bytes 2654232
  85.7 1.1 copy-done.7
  86.7 1.1 copy-done.9
  87.8 8.8 %shard_map.92 = (bf16[256,1152]{1,0:T(8,128)(2,1)}, f32[8,128]{1,0:T(8,128)S(1)}) custom-call(f32[2]{0:T(128)S(1)} %pad_maximum_fusion.numbers, s32[1]{0:T(128)S(6)} %copy.11.offset, s32[1]{0:T(128)} %bitcast.core, bf16[256,1152]{1,0:T(8,128)(2,1)S(1)} %copy-done.9, bf16[256,1152]{1,0:T(8,128)(2,1)S(1)} %get-tuple-element.20.img_b, ...), custom_call_target="tpu_custom_call" | custom-call | flops 3246391296 | bytes 6787072 | tf_op jit(solution)/shard_map/pallas_call | solution.py:237
  96.6 5.4 %all-to-all-done.1.term = bf16[8,72,1152]{2,1,0:T(8,128)(2,1)S(1)} async-done(((bf16[8,72,1152]{2,1,0:T(8,128)(2,1)}), bf16[8,72,1152]{2,1,0:T(8,128)(2,1)S(1)}, u32[]{:S(2)}, u32[]{:S(2)}) %all-to-all-start.1) | async-done | bytes 1327136 | tf_op jit(solution)/shard_map/all_to_all | solution.py:31
  102.9 6.1 %all-to-all-start.2 = ((bf16[32,8,384]{2,1,0:T(8,128)(2,1)}), bf16[32,8,384]{2,1,0:T(8,128)(2,1)S(1)}, u32[]{:S(2)}, u32[]{:S(2)}) async-start(bf16[32,8,384]{2,1,0:T(8,128)(2,1)} %shard_map.95), calls=%async_computation.2 | async-start | bytes 393216 | tf_op jit(solution)/shard_map/all_to_all | solution.py:31
  109.1 1.3 copy-done.1
  110.3 1.7 %copy-done.4 = bf16[1152,1152]{1,0:T(8,128)(2,1)S(1)} copy-done((bf16[1152,1152]{1,0:T(8,128)(2,1)S(1)}, bf16[1152,1152]{1,0:T(8,128)(2,1)}, u32[]{:S(2)}) %copy-start.4) | copy-done | bytes 2654232
  112.1 4.1 %shard_map.91 = (bf16[256,1152]{1,0:T(8,128)(2,1)}, f32[8,128]{1,0:T(8,128)S(1)}) custom-call(f32[2]{0:T(128)S(1)} %pad_maximum_fusion.numbers, s32[1]{0:T(128)} %bitcast.core, bf16[512,1152]{1,0:T(8,128)(2,1)S(1)} %shard_map.90.grads, bf16[256,1152]{1,0:T(8,128)(2,1)} %collective-permute-done.6.far.here, f32[256,1152]{1,0:T(8,128)S(1)} %copy-done.1, ...), custom_call_target="tpu_custom_call" | custom-call | flops 981467136 | bytes 6918144 | tf_op jit(solution)/shard_map/pallas_call | solution.py:237
  116.2 4.2 %all-to-all-done.2.pieces = bf16[32,8,384]{2,1,0:T(8,128)(2,1)S(1)} async-done(((bf16[32,8,384]{2,1,0:T(8,128)(2,1)}), bf16[32,8,384]{2,1,0:T(8,128)(2,1)S(1)}, u32[]{:S(2)}, u32[]{:S(2)}) %all-to-all-start.2) | async-done | bytes 196640 | tf_op jit(solution)/shard_map/all_to_all | solution.py:31
  120.5 18.7 %all_to_all.20.pieces = bf16[32,8,384]{2,1,0:T(8,128)(2,1)S(1)} all-to-all(bf16[32,8,384]{2,1,0:T(8,128)(2,1)S(1)} %shard_map.96), channel_id=1, replica_groups=mesh['z'=8,'yh'=4,'core'=2,'x'=4,'yl'=2] {'z','yh'}, dimensions={0} | all-to-all | bytes 393216 | tf_op jit(solution)/shard_map/all_to_all | solution.py:31
  139.2 5.3 %collective-permute-start.8 = (bf16[72,1152]{1,0:T(8,128)(2,1)S(1)}, bf16[72,1152]{1,0:T(8,128)(2,1)S(1)}, u32[]{:S(2)}, u32[]{:S(2)}) collective-permute-start(bf16[72,1152]{1,0:T(8,128)(2,1)S(1)} %convert_element_type.4), channel_id=1, source_target_pairs={{0,8},{8,0},{1,9},{9,1},{2,10},{10,2},{3,11},{11,3},{4,12},{12,4},... | collective-permute-start | bytes 497672 | tf_op jit(solution)/shard_map/ppermute | solution.py:345
  (31 shorter events, 4.5 us)
Async XLA Ops:
  0.6 20.5 %collective-permute-start.3 = (bf16[144,1152]{1,0:T(8,128)(2,1)}, bf16[144,1152]{1,0:T(8,128)(2,1)S(1)}, u32[]{:S(2)}, u32[]{:S(2)}) collective-permute-start(bf16[144,1152]{1,0:T(8,128)(2,1)} %head.1), channel_id=1, source_target_pairs={{0,1},{9,8},{2,3},{11,10},{4,5},{13,12},{6,7},{15,14},{16,17},{25,... | collective-permute-start | bytes 995336 | tf_op jit(solution)/shard_map/ppermute | solution.py:269
  1.9 39.9 %collective-permute-start.1 = (bf16[256,1152]{1,0:T(8,128)(2,1)}, bf16[256,1152]{1,0:T(8,128)(2,1)S(1)}, u32[]{:S(2)}, u32[]{:S(2)}) collective-permute-start(bf16[256,1152]{1,0:T(8,128)(2,1)} %second.1), channel_id=1, source_target_pairs={{0,496},{8,504},{16,0},{24,8},{32,16},{40,24},{48,32},{56,40},{64,... | collective-permute-start | bytes 1769480 | tf_op jit(solution)/shard_map/ppermute | solution.py:260
  17.1 29.6 %collective-permute-start = (bf16[256,1152]{1,0:T(8,128)(2,1)}, bf16[256,1152]{1,0:T(8,128)(2,1)S(1)}, u32[]{:S(2)}, u32[]{:S(2)}) collective-permute-start(bf16[256,1152]{1,0:T(8,128)(2,1)} %texts.3), channel_id=1, source_target_pairs={{0,16},{8,24},{16,32},{24,40},{32,48},{40,56},{48,64},{56,72},{64,... | collective-permute-start | bytes 1769480 | tf_op jit(solution)/shard_map/ppermute | solution.py:259
  21.1 1.0 copy-start.10
  23.3 18.5 %copy-start.5 = (bf16[256,1152]{1,0:T(8,128)(2,1)S(1)}, bf16[256,1152]{1,0:T(8,128)(2,1)}, u32[]{:S(2)}) copy-start(bf16[256,1152]{1,0:T(8,128)(2,1)} %second.1) | copy-start | bytes 1769476
  23.3 34.0 %all-to-all-start = ((bf16[4,144,1152]{2,1,0:T(8,128)(2,1)}), bf16[4,144,1152]{2,1,0:T(8,128)(2,1)S(1)}, u32[]{:S(2)}, u32[]{:S(2)}) async-start(bf16[4,144,1152]{2,1,0:T(8,128)(2,1)} %shard_map.87), calls=%async_computation | async-start | bytes 2654208 | tf_op jit(solution)/shard_map/all_to_all | solution.py:31
  27.4 19.3 %copy-start.8 = (bf16[256,1152]{1,0:T(8,128)(2,1)S(1)}, bf16[256,1152]{1,0:T(8,128)(2,1)}, u32[]{:S(2)}) copy-start(bf16[256,1152]{1,0:T(8,128)(2,1)} %texts.3) | copy-start | bytes 1769476
  41.8 4.9 %copy-start.6 = (bf16[256,1152]{1,0:T(8,128)(2,1)}, bf16[256,1152]{1,0:T(8,128)(2,1)S(1)}, u32[]{:S(2)}) copy-start(bf16[256,1152]{1,0:T(8,128)(2,1)S(1)} %collective-permute-done.1.image_a.first) | copy-start | bytes 1769476
  43.0 17.8 %collective-permute-start.5 = (bf16[512,1152]{1,0:T(8,128)(2,1)}, bf16[512,1152]{1,0:T(8,128)(2,1)}, u32[]{:S(2)}, u32[]{:S(2)}) collective-permute-start(bf16[512,1152]{1,0:T(8,128)(2,1)} %shard_map.86.pair), channel_id=1, source_target_pairs={{0,8},{8,0},{1,9},{9,1},{2,10},{10,2},{3,11},{11,3},{4,12},{12,4},... | collective-permute-start | bytes 3538952 | tf_op jit(solution)/shard_map/ppermute | solution.py:263
  48.3 21.2 %collective-permute-start.2 = (bf16[512,1152]{1,0:T(8,128)(2,1)}, bf16[512,1152]{1,0:T(8,128)(2,1)S(1)}, u32[]{:S(2)}, u32[]{:S(2)}) collective-permute-start(bf16[512,1152]{1,0:T(8,128)(2,1)} %get-tuple-element.17.units), channel_id=1, source_target_pairs={{0,8},{8,0},{1,9},{9,1},{2,10},{10,2},{3,11},{11,3},{4,12},{12,4},... | collective-permute-start | bytes 3538952 | tf_op jit(solution)/shard_map/ppermute | solution.py:265
  55.3 20.0 %collective-permute-start.6 = (bf16[256,1152]{1,0:T(8,128)(2,1)}, bf16[256,1152]{1,0:T(8,128)(2,1)}, u32[]{:S(2)}, u32[]{:S(2)}) collective-permute-start(bf16[256,1152]{1,0:T(8,128)(2,1)} %get-tuple-element.25), channel_id=1, source_target_pairs={{0,504},{8,16},{16,8},{24,32},{32,24},{40,48},{48,40},{56,64},{64,... | collective-permute-start | bytes 1769480 | tf_op jit(solution)/shard_map/ppermute | solution.py:266
  57.3 6.5 %collective-permute-start.4 = (bf16[4,144,1152]{2,1,0:T(8,128)(2,1)S(1)}, bf16[4,144,1152]{2,1,0:T(8,128)(2,1)S(1)}, u32[]{:S(2)}, u32[]{:S(2)}) collective-permute-start(bf16[4,144,1152]{2,1,0:T(8,128)(2,1)S(1)} %all-to-all-done.halves), channel_id=1, source_target_pairs={{0,8},{8,0},{1,9},{9,1},{2,10},{10,2},{3,11},{11,3},{4,12},{12,4},... | collective-permute-start | bytes 3981320 | tf_op jit(solution)/shard_map/ppermute | solution.py:279
  68.0 1.5 %copy-start.2 = (bf16[1152,1152]{1,0:T(8,128)(2,1)}, bf16[1152,1152]{1,0:T(8,128)(2,1)S(1)}, u32[]{:S(2)}) copy-start(bf16[1152,1152]{1,0:T(8,128)(2,1)S(1)} %get-tuple-element.26.head) | copy-start | bytes 7962628
  69.6 2.8 %copy-start = (f32[256,1152]{1,0:T(8,128)}, f32[256,1152]{1,0:T(8,128)S(1)}, u32[]{:S(2)}) copy-start(f32[256,1152]{1,0:T(8,128)S(1)} %get-tuple-element.18.unit) | copy-start | bytes 3538948
  72.3 5.4 %collective-permute-start.7 = (bf16[512,1152]{1,0:T(8,128)(2,1)S(1)}, bf16[512,1152]{1,0:T(8,128)(2,1)S(1)}, u32[]{:S(2)}, u32[]{:S(2)}) collective-permute-start(bf16[512,1152]{1,0:T(8,128)(2,1)S(1)} %shard_map.90.grads), channel_id=1, source_target_pairs={{0,8},{8,0},{1,9},{9,1},{2,10},{10,2},{3,11},{11,3},{4,12},{12,4},... | collective-permute-start | bytes 3538952 | tf_op jit(solution)/shard_map/ppermute | solution.py:305
  79.9 22.2 %all-to-all-start.1 = ((bf16[8,72,1152]{2,1,0:T(8,128)(2,1)}), bf16[8,72,1152]{2,1,0:T(8,128)(2,1)S(1)}, u32[]{:S(2)}, u32[]{:S(2)}) async-start(bf16[8,72,1152]{2,1,0:T(8,128)(2,1)} %shard_map.94), calls=%async_computation.1 | async-start | bytes 2654208 | tf_op jit(solution)/shard_map/all_to_all | solution.py:31
  83.9 1.7 %copy-start.3 = (bf16[1152,1152]{1,0:T(8,128)(2,1)S(1)}, bf16[1152,1152]{1,0:T(8,128)(2,1)}, u32[]{:S(2)}) copy-start(bf16[1152,1152]{1,0:T(8,128)(2,1)} %copy-done.2) | copy-start | bytes 7962628
  85.7 1.1 copy-start.7
  86.7 1.1 copy-start.9
  102.9 17.5 %all-to-all-start.2 = ((bf16[32,8,384]{2,1,0:T(8,128)(2,1)}), bf16[32,8,384]{2,1,0:T(8,128)(2,1)S(1)}, u32[]{:S(2)}, u32[]{:S(2)}) async-start(bf16[32,8,384]{2,1,0:T(8,128)(2,1)} %shard_map.95), calls=%async_computation.2 | async-start | bytes 393216 | tf_op jit(solution)/shard_map/all_to_all | solution.py:31
  109.0 1.3 copy-start.1
  110.3 1.7 %copy-start.4 = (bf16[1152,1152]{1,0:T(8,128)(2,1)S(1)}, bf16[1152,1152]{1,0:T(8,128)(2,1)}, u32[]{:S(2)}) copy-start(bf16[1152,1152]{1,0:T(8,128)(2,1)} %copy-done.2) | copy-start | bytes 7962628
  139.2 6.4 %collective-permute-start.8 = (bf16[72,1152]{1,0:T(8,128)(2,1)S(1)}, bf16[72,1152]{1,0:T(8,128)(2,1)S(1)}, u32[]{:S(2)}, u32[]{:S(2)}) collective-permute-start(bf16[72,1152]{1,0:T(8,128)(2,1)S(1)} %convert_element_type.4), channel_id=1, source_target_pairs={{0,8},{8,0},{1,9},{9,1},{2,10},{10,2},{3,11},{11,3},{4,12},{12,4},... | collective-permute-start | bytes 497672 | tf_op jit(solution)/shard_map/ppermute | solution.py:345

commit v7 on v6

--- a/solution.py
+++ b/solution.py
@@ -96,24 +96,24 @@
             head[pl.ds(start, share), :] = source[index]
 
     rows = img_b.shape[0]
-    unit_value, inverse_value = unit_rows(dot(pair[rows:], head[...], 1, 0))
-    unit[...] = unit_value
-    inverse[...] = jnp.broadcast_to(inverse_value, inverse.shape)
-    rounded = narrow(unit_value)
+    units_all, inverse_all = unit_rows(dot(pair[...], head[...], 1, 0))
+    rounded = narrow(units_all[rows:])
+    unit[...] = units_all[rows:]
+    inverse[...] = jnp.broadcast_to(inverse_all[rows:], inverse.shape)
     img_b[...] = rounded
+
+    def keep(value, inverse_value):
+        far_unit[...] = value
+        far_inverse[...] = jnp.broadcast_to(inverse_value, far_inverse.shape)
+        far_b[...] = narrow(value)
 
     @pl.when(core[0] == 0)
     def _():
-        unit_value, inverse_value = unit_rows(dot(pair[:rows], head[...], 1, 0))
-        far_unit[...] = unit_value
-        far_inverse[...] = jnp.broadcast_to(inverse_value, far_inverse.shape)
-        far_b[...] = narrow(unit_value)
+        keep(units_all[:rows], inverse_all[:rows])
 
     @pl.when(core[0] != 0)
     def _():
-        far_unit[...] = unit[...]
-        far_inverse[...] = inverse[...]
-        far_b[...] = img_b[...]
+        keep(units_all[rows:], inverse_all[rows:])
 
     block = units[rows:]
     weights = own_pairs(rounded, block, numbers, positives(offset[0], rows, 0))
@@ -189,8 +189,7 @@
 def term_kernel(core, picked, grads, grads_p, total, out):
     count, half = grads.shape[0] // 2, out.shape[1]
     far = jnp.where(core[0] == 0, grads[count:], grads_p[count:])
-    term = total[...] + dot(picked[:, count : 2 * count], grads_p[:count], 1, 0)
-    term = term + dot(picked[:, 2 * count :], far, 1, 0)
+    term = total[...] + dot(picked[:, count:], jnp.concatenate([grads_p[:count], far], 0), 1, 0)
     for index in range(out.shape[0]):
         out[index] = narrow(term[index * half : (index + 1) * half])
 

time: 147 us -> 148 us (level)
  starting transfers between devices: 57.1 us -> 55.5 us
  Pallas kernels: 31.5 us -> 33 us
    pallas_call x14, Pallas kernels: 31.5 us -> 33 us  [call(): pl.pallas_call(kernel, out_shape=outs if len(outs) > 1 else outs[0], in_s...]
  transfers between devices with their start and end apart: 12 -> 12, of which waited for: 5 -> 5; matrix products, arithmetic and copies ran while one was open for 0% -> 0% of each run, Pallas kernels for 19% -> 20%
where the time goes in v7:
time: 148 us; the launch traced here: 147 us
  starting transfers between devices  55.5 us (38%)
  Pallas kernels  33 us (22%)
  waiting for transfers between devices  27.6 us (19%)
  blocking collectives  18.7 us (13%)
  local copies, waits for them, and re-layouts  9.39 us (6%)
  between operations  2.79 us (2%)
    pallas_call x14, Pallas kernels, call(): pl.pallas_call(kernel, out_shape=outs if len(outs) > 1 else outs[0], in_s...  33 us
    all_to_all x1, blocking collectives, exchange(): return lax.all_to_all(array, axes, split_axis=0, concat_axis=0, tiled=True)  18.7 us
    ppermute x1, starting transfers between devices, per_device(): image_a = lax.ppermute(images, DP, by_chip(-1))  15.2 us
    ppermute x1, waiting for transfers between devices, per_device(): image_a = lax.ppermute(images, DP, by_chip(-1))  14.4 us
    all_to_all x3, starting transfers between devices, exchange(): return lax.all_to_all(array, axes, split_axis=0, concat_axis=0, tiled=True)  13.7 us
    all_to_all x3, waiting for transfers between devices, exchange(): return lax.all_to_all(array, axes, split_axis=0, concat_axis=0, tiled=True)  9.94 us
    unnamed x22, local copies, waits for them, and re-layouts  9.39 us
    ppermute x1, starting transfers between devices, per_device(): units_p = lax.ppermute(units, 'core', SWAP)  6.98 us
  transfers between devices with their start and end apart: 12, of which 5 were waited for; matrix products, arithmetic and copies ran while one was open for 0% of the time, Pallas kernels for 20%

profile of v7, /device:TPU:1, one launch (start us, length us, event | category | flops | bytes accessed | tf_op | source)
XLA Modules:
  0.0 147.0 jit_solution(8613150851861596225)
XLA Ops:
  0.6 1.3 collective-permute-start.3
  1.9 15.2 %collective-permute-start.1 = (bf16[256,1152]{1,0:T(8,128)(2,1)}, bf16[256,1152]{1,0:T(8,128)(2,1)S(1)}, u32[]{:S(2)}, u32[]{:S(2)}) collective-permute-start(bf16[256,1152]{1,0:T(8,128)(2,1)} %second.1), channel_id=1, source_target_pairs={{0,496},{8,504},{16,0},{24,8},{32,16},{40,24},{48,32},{56,40},{64,... | collective-permute-start | bytes 1769480 | tf_op jit(solution)/shard_map/ppermute | solution.py:259
  17.1 1.9 %collective-permute-start = (bf16[256,1152]{1,0:T(8,128)(2,1)}, bf16[256,1152]{1,0:T(8,128)(2,1)S(1)}, u32[]{:S(2)}, u32[]{:S(2)}) collective-permute-start(bf16[256,1152]{1,0:T(8,128)(2,1)} %texts.3), channel_id=1, source_target_pairs={{0,16},{8,24},{16,32},{24,40},{32,48},{40,56},{48,64},{56,72},{64,... | collective-permute-start | bytes 1769480 | tf_op jit(solution)/shard_map/ppermute | solution.py:258
  22.1 1.2 shard_map.87
  23.3 4.1 %all-to-all-start = ((bf16[4,144,1152]{2,1,0:T(8,128)(2,1)}), bf16[4,144,1152]{2,1,0:T(8,128)(2,1)S(1)}, u32[]{:S(2)}, u32[]{:S(2)}) async-start(bf16[4,144,1152]{2,1,0:T(8,128)(2,1)} %shard_map.87), calls=%async_computation | async-start | bytes 2654208 | tf_op jit(solution)/shard_map/all_to_all | solution.py:31
  27.4 14.4 %collective-permute-done.1.image_a.first = bf16[256,1152]{1,0:T(8,128)(2,1)S(1)} collective-permute-done((bf16[256,1152]{1,0:T(8,128)(2,1)}, bf16[256,1152]{1,0:T(8,128)(2,1)S(1)}, u32[]{:S(2)}, u32[]{:S(2)}) %collective-permute-start.1) | collective-permute-done | bytes 589856 | tf_op jit(solution)/shard_map/ppermute | solution.py:259
  41.8 1.2 shard_map.86.pair
  43.0 3.7 %collective-permute-start.5 = (bf16[512,1152]{1,0:T(8,128)(2,1)}, bf16[512,1152]{1,0:T(8,128)(2,1)}, u32[]{:S(2)}, u32[]{:S(2)}) collective-permute-start(bf16[512,1152]{1,0:T(8,128)(2,1)} %shard_map.86.pair), channel_id=1, source_target_pairs={{0,8},{8,0},{1,9},{9,1},{2,10},{10,2},{3,11},{11,3},{4,12},{12,4},... | collective-permute-start | bytes 3538952 | tf_op jit(solution)/shard_map/ppermute | solution.py:262
  46.8 1.6 %shard_map.85 = (bf16[512,1152]{1,0:T(8,128)(2,1)}, bf16[256,1152]{1,0:T(8,128)(2,1)}) custom-call(s32[1]{0:T(128)} %bitcast.core, bf16[256,1152]{1,0:T(8,128)(2,1)S(1)} %copy-done.8, bf16[256,1152]{1,0:T(8,128)(2,1)S(1)} %collective-permute-done.text_a, bf16[256,1152]{1,0:T(8,128)(2,1)S(1)} %collective-permute-done.1.image_a.first), custom_call_target="tpu_custom_call" | custom-call | flops 20000000000 | bytes 3538944 | tf_op jit(solution)/shard_map/pallas_call | solution.py:236
  48.3 7.0 %collective-permute-start.2 = (bf16[512,1152]{1,0:T(8,128)(2,1)}, bf16[512,1152]{1,0:T(8,128)(2,1)S(1)}, u32[]{:S(2)}, u32[]{:S(2)}) collective-permute-start(bf16[512,1152]{1,0:T(8,128)(2,1)} %get-tuple-element.17.units), channel_id=1, source_target_pairs={{0,8},{8,0},{1,9},{9,1},{2,10},{10,2},{3,11},{11,3},{4,12},{12,4},... | collective-permute-start | bytes 3538952 | tf_op jit(solution)/shard_map/ppermute | solution.py:264
  55.3 1.9 %collective-permute-start.6 = (bf16[256,1152]{1,0:T(8,128)(2,1)}, bf16[256,1152]{1,0:T(8,128)(2,1)}, u32[]{:S(2)}, u32[]{:S(2)}) collective-permute-start(bf16[256,1152]{1,0:T(8,128)(2,1)} %get-tuple-element.25), channel_id=1, source_target_pairs={{0,504},{8,16},{16,8},{24,32},{32,24},{40,48},{48,40},{56,64},{64,... | collective-permute-start | bytes 1769480 | tf_op jit(solution)/shard_map/ppermute | solution.py:265
  57.3 3.5 %collective-permute-start.4 = (bf16[4,144,1152]{2,1,0:T(8,128)(2,1)S(1)}, bf16[4,144,1152]{2,1,0:T(8,128)(2,1)S(1)}, u32[]{:S(2)}, u32[]{:S(2)}) collective-permute-start(bf16[4,144,1152]{2,1,0:T(8,128)(2,1)S(1)} %all-to-all-done.halves), channel_id=1, source_target_pairs={{0,8},{8,0},{1,9},{9,1},{2,10},{10,2},{3,11},{11,3},{4,12},{12,4},... | collective-permute-start | bytes 3981320 | tf_op jit(solution)/shard_map/ppermute | solution.py:278
  60.8 3.0 %shard_map.89.here.picked = bf16[576,768]{1,0:T(8,128)(2,1)S(1)} custom-call(s32[1]{0:T(128)} %bitcast.core, bf16[512,1152]{1,0:T(8,128)(2,1)} %shard_map.86.pair, bf16[512,1152]{1,0:T(8,128)(2,1)} %collective-permute-done.5.pair_p), custom_call_target="tpu_custom_call" | custom-call | flops 20000000000 | bytes 3244032 | tf_op jit(solution)/shard_map/pallas_call | solution.py:236
  63.8 5.8 %shard_map.88 = (bf16[1152,1152]{1,0:T(8,128)(2,1)S(1)}, f32[256,1152]{1,0:T(8,128)S(1)}, f32[256,128]{1,0:T(8,128)S(1)}, bf16[256,1152]{1,0:T(8,128)(2,1)S(1)},...) custom-call(f32[2]{0:T(128)S(1)} %pad_maximum_fusion.numbers, ...), custom_call_target="tpu_custom_call" | custom-call | flops 20000000000 | bytes 12648448 | tf_op jit(solution)/shard_map/pallas_call | solution.py:236
  69.7 1.5 %copy-done.2 = bf16[1152,1152]{1,0:T(8,128)(2,1)} copy-done((bf16[1152,1152]{1,0:T(8,128)(2,1)}, bf16[1152,1152]{1,0:T(8,128)(2,1)S(1)}, u32[]{:S(2)}) %copy-start.2) | copy-done | bytes 2654232
  71.2 2.8 %shard_map.90.grads = bf16[512,1152]{1,0:T(8,128)(2,1)S(1)} custom-call(f32[2]{0:T(128)S(1)} %pad_maximum_fusion.numbers, s32[1]{0:T(128)} %bitcast.core, bf16[512,1152]{1,0:T(8,128)(2,1)S(1)} %collective-permute-done.2.units_p, f32[256,1152]{1,0:T(8,128)S(1)} %get-tuple-element.18.unit, f32[256,128]{1,0:T(8,128)S(1)} %get-tuple-element.19.inverse, ...), custom_call_target="tpu_custom_call" | custom-call | flops 256 | bytes 7340032 | tf_op jit(solution)/shard_map/pallas_call | solution.py:236
  74.0 1.9 %collective-permute-start.7 = (bf16[512,1152]{1,0:T(8,128)(2,1)S(1)}, bf16[512,1152]{1,0:T(8,128)(2,1)S(1)}, u32[]{:S(2)}, u32[]{:S(2)}) collective-permute-start(bf16[512,1152]{1,0:T(8,128)(2,1)S(1)} %shard_map.90.grads), channel_id=1, source_target_pairs={{0,8},{8,0},{1,9},{9,1},{2,10},{10,2},{3,11},{11,3},{4,12},{12,4},... | collective-permute-start | bytes 3538952 | tf_op jit(solution)/shard_map/ppermute | solution.py:304
  76.5 2.2 %collective-permute-done.7.grads_p = bf16[512,1152]{1,0:T(8,128)(2,1)S(1)} collective-permute-done((bf16[512,1152]{1,0:T(8,128)(2,1)S(1)}, bf16[512,1152]{1,0:T(8,128)(2,1)S(1)}, u32[]{:S(2)}, u32[]{:S(2)}) %collective-permute-start.7) | collective-permute-done | bytes 1179680 | tf_op jit(solution)/shard_map/ppermute | solution.py:304
  78.7 2.1 %shard_map.94 = bf16[8,72,1152]{2,1,0:T(8,128)(2,1)} custom-call(s32[1]{0:T(128)} %bitcast.core, bf16[576,768]{1,0:T(8,128)(2,1)S(1)} %shard_map.89.here.picked, bf16[512,1152]{1,0:T(8,128)(2,1)S(1)} %shard_map.90.grads, bf16[512,1152]{1,0:T(8,128)(2,1)S(1)} %collective-permute-done.7.grads_p, f32[576,1152]{1,0:T(8,128)S(1)} %shard_map.93.total), custom_call_target="tpu_custom_call" | custom-call | flops 679477248 | bytes 7225344 | tf_op jit(solution)/shard_map/pallas_call | solution.py:236
  80.8 4.0 %all-to-all-start.1 = ((bf16[8,72,1152]{2,1,0:T(8,128)(2,1)}), bf16[8,72,1152]{2,1,0:T(8,128)(2,1)S(1)}, u32[]{:S(2)}, u32[]{:S(2)}) async-start(bf16[8,72,1152]{2,1,0:T(8,128)(2,1)} %shard_map.94), calls=%async_computation.1 | async-start | bytes 2654208 | tf_op jit(solution)/shard_map/all_to_all | solution.py:31
  84.8 1.7 %copy-done.3 = bf16[1152,1152]{1,0:T(8,128)(2,1)S(1)} copy-done((bf16[1152,1152]{1,0:T(8,128)(2,1)S(1)}, bf16[1152,1152]{1,0:T(8,128)(2,1)}, u32[]{:S(2)}) %copy-start.3) | copy-done | bytes 2654232
  86.6 1.1 copy-done.7
  87.6 1.1 copy-done.9
  88.7 8.8 %shard_map.92 = (bf16[256,1152]{1,0:T(8,128)(2,1)}, f32[8,128]{1,0:T(8,128)S(1)}) custom-call(f32[2]{0:T(128)S(1)} %pad_maximum_fusion.numbers, s32[1]{0:T(128)S(6)} %copy.11.offset, s32[1]{0:T(128)} %bitcast.core, bf16[256,1152]{1,0:T(8,128)(2,1)S(1)} %copy-done.9, bf16[256,1152]{1,0:T(8,128)(2,1)S(1)} %get-tuple-element.20.img_b, ...), custom_call_target="tpu_custom_call" | custom-call | flops 3246391296 | bytes 6787072 | tf_op jit(solution)/shard_map/pallas_call | solution.py:236
  97.5 5.7 %all-to-all-done.1.term = bf16[8,72,1152]{2,1,0:T(8,128)(2,1)S(1)} async-done(((bf16[8,72,1152]{2,1,0:T(8,128)(2,1)}), bf16[8,72,1152]{2,1,0:T(8,128)(2,1)S(1)}, u32[]{:S(2)}, u32[]{:S(2)}) %all-to-all-start.1) | async-done | bytes 1327136 | tf_op jit(solution)/shard_map/all_to_all | solution.py:31
  104.1 5.5 %all-to-all-start.2 = ((bf16[32,8,384]{2,1,0:T(8,128)(2,1)}), bf16[32,8,384]{2,1,0:T(8,128)(2,1)S(1)}, u32[]{:S(2)}, u32[]{:S(2)}) async-start(bf16[32,8,384]{2,1,0:T(8,128)(2,1)} %shard_map.95), calls=%async_computation.2 | async-start | bytes 393216 | tf_op jit(solution)/shard_map/all_to_all | solution.py:31
  109.6 1.3 copy-done.1
  110.8 1.7 %copy-done.4 = bf16[1152,1152]{1,0:T(8,128)(2,1)S(1)} copy-done((bf16[1152,1152]{1,0:T(8,128)(2,1)S(1)}, bf16[1152,1152]{1,0:T(8,128)(2,1)}, u32[]{:S(2)}) %copy-start.4) | copy-done | bytes 2654232
  112.6 4.1 %shard_map.91 = (bf16[256,1152]{1,0:T(8,128)(2,1)}, f32[8,128]{1,0:T(8,128)S(1)}) custom-call(f32[2]{0:T(128)S(1)} %pad_maximum_fusion.numbers, s32[1]{0:T(128)} %bitcast.core, bf16[512,1152]{1,0:T(8,128)(2,1)S(1)} %shard_map.90.grads, bf16[256,1152]{1,0:T(8,128)(2,1)} %collective-permute-done.6.far.here, f32[256,1152]{1,0:T(8,128)S(1)} %copy-done.1, ...), custom_call_target="tpu_custom_call" | custom-call | flops 981467136 | bytes 6918144 | tf_op jit(solution)/shard_map/pallas_call | solution.py:236
  116.7 4.2 %all-to-all-done.2.pieces = bf16[32,8,384]{2,1,0:T(8,128)(2,1)S(1)} async-done(((bf16[32,8,384]{2,1,0:T(8,128)(2,1)}), bf16[32,8,384]{2,1,0:T(8,128)(2,1)S(1)}, u32[]{:S(2)}, u32[]{:S(2)}) %all-to-all-start.2) | async-done | bytes 196640 | tf_op jit(solution)/shard_map/all_to_all | solution.py:31
  121.0 18.7 %all_to_all.20.pieces = bf16[32,8,384]{2,1,0:T(8,128)(2,1)S(1)} all-to-all(bf16[32,8,384]{2,1,0:T(8,128)(2,1)S(1)} %shard_map.96), channel_id=1, replica_groups=mesh['z'=8,'yh'=4,'core'=2,'x'=4,'yl'=2] {'z','yh'}, dimensions={0} | all-to-all | bytes 393216 | tf_op jit(solution)/shard_map/all_to_all | solution.py:31
  139.8 5.3 %collective-permute-start.8 = (bf16[72,1152]{1,0:T(8,128)(2,1)S(1)}, bf16[72,1152]{1,0:T(8,128)(2,1)S(1)}, u32[]{:S(2)}, u32[]{:S(2)}) collective-permute-start(bf16[72,1152]{1,0:T(8,128)(2,1)S(1)} %convert_element_type.4), channel_id=1, source_target_pairs={{0,8},{8,0},{1,9},{9,1},{2,10},{10,2},{3,11},{11,3},{4,12},{12,4},... | collective-permute-start | bytes 497672 | tf_op jit(solution)/shard_map/ppermute | solution.py:344
  (31 shorter events, 4.5 us)
Async XLA Ops:
  0.6 20.5 %collective-permute-start.3 = (bf16[144,1152]{1,0:T(8,128)(2,1)}, bf16[144,1152]{1,0:T(8,128)(2,1)S(1)}, u32[]{:S(2)}, u32[]{:S(2)}) collective-permute-start(bf16[144,1152]{1,0:T(8,128)(2,1)} %head.1), channel_id=1, source_target_pairs={{0,1},{9,8},{2,3},{11,10},{4,5},{13,12},{6,7},{15,14},{16,17},{25,... | collective-permute-start | bytes 995336 | tf_op jit(solution)/shard_map/ppermute | solution.py:268
  1.9 39.9 %collective-permute-start.1 = (bf16[256,1152]{1,0:T(8,128)(2,1)}, bf16[256,1152]{1,0:T(8,128)(2,1)S(1)}, u32[]{:S(2)}, u32[]{:S(2)}) collective-permute-start(bf16[256,1152]{1,0:T(8,128)(2,1)} %second.1), channel_id=1, source_target_pairs={{0,496},{8,504},{16,0},{24,8},{32,16},{40,24},{48,32},{56,40},{64,... | collective-permute-start | bytes 1769480 | tf_op jit(solution)/shard_map/ppermute | solution.py:259
  17.1 29.6 %collective-permute-start = (bf16[256,1152]{1,0:T(8,128)(2,1)}, bf16[256,1152]{1,0:T(8,128)(2,1)S(1)}, u32[]{:S(2)}, u32[]{:S(2)}) collective-permute-start(bf16[256,1152]{1,0:T(8,128)(2,1)} %texts.3), channel_id=1, source_target_pairs={{0,16},{8,24},{16,32},{24,40},{32,48},{40,56},{48,64},{56,72},{64,... | collective-permute-start | bytes 1769480 | tf_op jit(solution)/shard_map/ppermute | solution.py:258
  21.1 1.0 copy-start.10
  23.3 18.5 %copy-start.5 = (bf16[256,1152]{1,0:T(8,128)(2,1)S(1)}, bf16[256,1152]{1,0:T(8,128)(2,1)}, u32[]{:S(2)}) copy-start(bf16[256,1152]{1,0:T(8,128)(2,1)} %second.1) | copy-start | bytes 1769476
  23.3 34.0 %all-to-all-start = ((bf16[4,144,1152]{2,1,0:T(8,128)(2,1)}), bf16[4,144,1152]{2,1,0:T(8,128)(2,1)S(1)}, u32[]{:S(2)}, u32[]{:S(2)}) async-start(bf16[4,144,1152]{2,1,0:T(8,128)(2,1)} %shard_map.87), calls=%async_computation | async-start | bytes 2654208 | tf_op jit(solution)/shard_map/all_to_all | solution.py:31
  27.4 19.3 %copy-start.8 = (bf16[256,1152]{1,0:T(8,128)(2,1)S(1)}, bf16[256,1152]{1,0:T(8,128)(2,1)}, u32[]{:S(2)}) copy-start(bf16[256,1152]{1,0:T(8,128)(2,1)} %texts.3) | copy-start | bytes 1769476
  41.8 4.9 %copy-start.6 = (bf16[256,1152]{1,0:T(8,128)(2,1)}, bf16[256,1152]{1,0:T(8,128)(2,1)S(1)}, u32[]{:S(2)}) copy-start(bf16[256,1152]{1,0:T(8,128)(2,1)S(1)} %collective-permute-done.1.image_a.first) | copy-start | bytes 1769476
  43.0 17.8 %collective-permute-start.5 = (bf16[512,1152]{1,0:T(8,128)(2,1)}, bf16[512,1152]{1,0:T(8,128)(2,1)}, u32[]{:S(2)}, u32[]{:S(2)}) collective-permute-start(bf16[512,1152]{1,0:T(8,128)(2,1)} %shard_map.86.pair), channel_id=1, source_target_pairs={{0,8},{8,0},{1,9},{9,1},{2,10},{10,2},{3,11},{11,3},{4,12},{12,4},... | collective-permute-start | bytes 3538952 | tf_op jit(solution)/shard_map/ppermute | solution.py:262
  48.3 22.8 %collective-permute-start.2 = (bf16[512,1152]{1,0:T(8,128)(2,1)}, bf16[512,1152]{1,0:T(8,128)(2,1)S(1)}, u32[]{:S(2)}, u32[]{:S(2)}) collective-permute-start(bf16[512,1152]{1,0:T(8,128)(2,1)} %get-tuple-element.17.units), channel_id=1, source_target_pairs={{0,8},{8,0},{1,9},{9,1},{2,10},{10,2},{3,11},{11,3},{4,12},{12,4},... | collective-permute-start | bytes 3538952 | tf_op jit(solution)/shard_map/ppermute | solution.py:264
  55.3 20.6 %collective-permute-start.6 = (bf16[256,1152]{1,0:T(8,128)(2,1)}, bf16[256,1152]{1,0:T(8,128)(2,1)}, u32[]{:S(2)}, u32[]{:S(2)}) collective-permute-start(bf16[256,1152]{1,0:T(8,128)(2,1)} %get-tuple-element.25), channel_id=1, source_target_pairs={{0,504},{8,16},{16,8},{24,32},{32,24},{40,48},{48,40},{56,64},{64,... | collective-permute-start | bytes 1769480 | tf_op jit(solution)/shard_map/ppermute | solution.py:265
  57.3 6.5 %collective-permute-start.4 = (bf16[4,144,1152]{2,1,0:T(8,128)(2,1)S(1)}, bf16[4,144,1152]{2,1,0:T(8,128)(2,1)S(1)}, u32[]{:S(2)}, u32[]{:S(2)}) collective-permute-start(bf16[4,144,1152]{2,1,0:T(8,128)(2,1)S(1)} %all-to-all-done.halves), channel_id=1, source_target_pairs={{0,8},{8,0},{1,9},{9,1},{2,10},{10,2},{3,11},{11,3},{4,12},{12,4},... | collective-permute-start | bytes 3981320 | tf_op jit(solution)/shard_map/ppermute | solution.py:278
  69.6 1.5 %copy-start.2 = (bf16[1152,1152]{1,0:T(8,128)(2,1)}, bf16[1152,1152]{1,0:T(8,128)(2,1)S(1)}, u32[]{:S(2)}) copy-start(bf16[1152,1152]{1,0:T(8,128)(2,1)S(1)} %get-tuple-element.26.head) | copy-start | bytes 7962628
  71.2 2.8 %copy-start = (f32[256,1152]{1,0:T(8,128)}, f32[256,1152]{1,0:T(8,128)S(1)}, u32[]{:S(2)}) copy-start(f32[256,1152]{1,0:T(8,128)S(1)} %get-tuple-element.18.unit) | copy-start | bytes 3538948
  74.0 4.7 %collective-permute-start.7 = (bf16[512,1152]{1,0:T(8,128)(2,1)S(1)}, bf16[512,1152]{1,0:T(8,128)(2,1)S(1)}, u32[]{:S(2)}, u32[]{:S(2)}) collective-permute-start(bf16[512,1152]{1,0:T(8,128)(2,1)S(1)} %shard_map.90.grads), channel_id=1, source_target_pairs={{0,8},{8,0},{1,9},{9,1},{2,10},{10,2},{3,11},{11,3},{4,12},{12,4},... | collective-permute-start | bytes 3538952 | tf_op jit(solution)/shard_map/ppermute | solution.py:304
  80.8 22.4 %all-to-all-start.1 = ((bf16[8,72,1152]{2,1,0:T(8,128)(2,1)}), bf16[8,72,1152]{2,1,0:T(8,128)(2,1)S(1)}, u32[]{:S(2)}, u32[]{:S(2)}) async-start(bf16[8,72,1152]{2,1,0:T(8,128)(2,1)} %shard_map.94), calls=%async_computation.1 | async-start | bytes 2654208 | tf_op jit(solution)/shard_map/all_to_all | solution.py:31
  84.8 1.7 %copy-start.3 = (bf16[1152,1152]{1,0:T(8,128)(2,1)S(1)}, bf16[1152,1152]{1,0:T(8,128)(2,1)}, u32[]{:S(2)}) copy-start(bf16[1152,1152]{1,0:T(8,128)(2,1)} %copy-done.2) | copy-start | bytes 7962628
  86.6 1.1 copy-start.7
  87.6 1.1 copy-start.9
  104.1 16.9 %all-to-all-start.2 = ((bf16[32,8,384]{2,1,0:T(8,128)(2,1)}), bf16[32,8,384]{2,1,0:T(8,128)(2,1)S(1)}, u32[]{:S(2)}, u32[]{:S(2)}) async-start(bf16[32,8,384]{2,1,0:T(8,128)(2,1)} %shard_map.95), calls=%async_computation.2 | async-start | bytes 393216 | tf_op jit(solution)/shard_map/all_to_all | solution.py:31
  109.6 1.3 copy-start.1
  110.8 1.7 %copy-start.4 = (bf16[1152,1152]{1,0:T(8,128)(2,1)S(1)}, bf16[1152,1152]{1,0:T(8,128)(2,1)}, u32[]{:S(2)}) copy-start(bf16[1152,1152]{1,0:T(8,128)(2,1)} %copy-done.2) | copy-start | bytes 7962628
  139.8 6.4 %collective-permute-start.8 = (bf16[72,1152]{1,0:T(8,128)(2,1)S(1)}, bf16[72,1152]{1,0:T(8,128)(2,1)S(1)}, u32[]{:S(2)}, u32[]{:S(2)}) collective-permute-start(bf16[72,1152]{1,0:T(8,128)(2,1)S(1)} %convert_element_type.4), channel_id=1, source_target_pairs={{0,8},{8,0},{1,9},{9,1},{2,10},{10,2},{3,11},{11,3},{4,12},{12,4},... | collective-permute-start | bytes 497672 | tf_op jit(solution)/shard_map/ppermute | solution.py:344
